TPU v7x, 32 devices: a whole 2x2x4 slice. The times are simulated.
32 devices in a mesh: subj: 2 (over x), tr: 16 (over z, y, core).
Axes of the slice: x: 2, y: 2, z: 4, core: 2. Of those that a mesh axis runs over, the one named last changes fastest.
Arguments:
- features: bfloat16 [1024, 2048], P('tr', 'subj'), may hold values from -6 to 6
- block_orders: int32 [4, 16], replicated, may hold values from 0 to 15, each once within a row
- offsets: int32 [4, 4], replicated, may hold values from 0 to 8
- tap_gains: float32 [4, 4], replicated, may hold values from 0.2 to 1
- weights: bfloat16 [2, 2048, 256], P('subj'), may hold values from -0.125 to 0.125
- signal: bfloat16 [2, 1024, 256], P('subj', 'tr')
- block_owner: int32 [2, 64, 1], P('subj'), may hold values from 0 to 15; in each aligned block of 64 rows (0 to 63, 64 to 127, ..., all dimensions but the last counted through in order) at most 8 rows name the same one
Outputs:
- energy: float32 [2, 1024, 5], P('subj', 'tr')
- scores: float32 [2, 128, 5], P('subj', 'tr')
Inputs may be any that keep to these rules, and one draw needn't show every extreme that they name: `block_orders`: each row names every 1024 block once. `block_owner`: no owner is named by more than 8 voxel blocks of one subject.
All inputs are finite; a program needn't handle non-finite values.
Results may differ from a plain program's by a relative error of at most 0.0003.
Values may be sent and summed in bfloat16 or wider, within the bound.
No kernel may reach another device: no remote copies, remote signals or barrier semaphores. Data moves between devices by JAX's collectives and lax.ppermute only.
A program may use at most 64 MiB of HBM per device.

v0:
```python
import jax
import jax.numpy as jnp
from jax import lax
from jax.sharding import PartitionSpec as P

MAXLAG = 8
VB = 4
CAP = 8


epsilon = 1e-06


def passed_along(value, axis, steps):
    count = lax.axis_size(axis)
    leading, last = (max(0, -steps), min(count, count - steps))
    return lax.ppermute(value, axis, [(source, source + steps) for source in range(leading, last)])


def lag_table(offsets, tap_gains, first_column, width, columns_all):
    bands = offsets.shape[0]
    lag_range = jnp.arange(MAXLAG + 1, dtype=jnp.int32)
    hits = (offsets[:, :, None] == lag_range[None, None, :]).astype(jnp.float32)
    band_table = jnp.sum(tap_gains[:, :, None] * hits, axis=1)
    column_band = (first_column + jnp.arange(width, dtype=jnp.int32)) // (columns_all // bands)
    selector = (column_band[None, :] == jnp.arange(bands, dtype=jnp.int32)[:, None]).astype(
        jnp.float32
    )
    return jnp.dot(band_table.T, selector, precision=lax.Precision.HIGHEST)


def arrange(panel, block_orders, offsets, tap_gains, first_column, columns_all):
    tr_count = lax.axis_size("tr")
    tr_rows, width = panel.shape
    pieces = panel.reshape(tr_count, tr_rows // tr_count, width)
    spread = lax.all_to_all(pieces, "tr", split_axis=0, concat_axis=0, tiled=True)
    outgoing = jnp.take(spread, block_orders, axis=0)
    arrived = lax.all_to_all(outgoing, "tr", split_axis=1, concat_axis=1, tiled=True)
    moved = arrived.reshape(block_orders.shape[0], tr_rows, width)
    series = jnp.concatenate([panel[None], moved], axis=0)
    rim = passed_along(series[:, tr_rows - MAXLAG :, :], "tr", 1)
    extended = jnp.concatenate([rim, series], axis=1)
    table = lag_table(offsets, tap_gains, first_column, width, columns_all)
    total = jnp.zeros(series.shape, jnp.float32)
    for lag in range(MAXLAG + 1):
        window = extended[:, MAXLAG - lag : MAXLAG - lag + tr_rows, :].astype(jnp.float32)
        total = total + table[lag][None, None, :] * window
    return total.astype(jnp.bfloat16)


def on_device(features, block_orders, offsets, tap_gains, weights, signal, block_owner):
    weight = weights[0]
    columns_all = weight.shape[0]
    panel = lax.all_gather(features, "subj", axis=1, tiled=True)
    filtered = arrange(panel, block_orders, offsets, tap_gains, 0, columns_all)
    predicted = jnp.einsum("ctf,fv->ctv", filtered, weight, preferred_element_type=jnp.float32)
    measured = signal[0].astype(jnp.float32)
    residual = measured[None] - predicted
    squared = residual * residual
    energy = jnp.mean(squared, axis=2).T[None]
    stats = jnp.concatenate(
        [jnp.sum(squared, axis=1), jnp.sum(measured * measured, axis=0)[None]], axis=0
    )
    conditions = stats.shape[0] - 1
    owners = block_owner[0, :, 0]
    blocks = owners.shape[0]
    order = jnp.arange(blocks, dtype=jnp.int32)
    same_owner = (owners[:, None] == owners[None, :]) & (order[:, None] > order[None, :])
    rank = jnp.sum(same_owner.astype(jnp.int32), axis=1)
    slot = owners * CAP + rank
    totals = lax.psum(stats, "tr")
    fit = jnp.log((totals[:conditions] + epsilon) / (totals[conditions] + epsilon)[None, :])
    block_fit = jnp.mean(fit.reshape(conditions, blocks, VB), axis=2)
    wanted = lax.axis_index("tr") * CAP + jnp.arange(CAP, dtype=jnp.int32)
    selector = (slot[None, :] == wanted[:, None]).astype(jnp.float32)
    scores = jnp.dot(selector, block_fit.T, precision=lax.Precision.HIGHEST)
    return (energy, scores[None])


def solution(mesh):
    placed = (
        P("tr", "subj"),
        P(),
        P(),
        P(),
        P("subj", None, None),
        P("subj", "tr", None),
        P("subj", None, None),
    )
    return jax.shard_map(
        on_device,
        mesh=mesh,
        in_specs=placed,
        out_specs=(P("subj", "tr", None), P("subj", "tr", None)),
        check_vma=False,
    )
```

profile of v0, /device:TPU:0, one launch (start us, length us, event | category | flops | bytes accessed | tf_op | source)
XLA Modules:
  0.0 105.2 jit_solution(4510352992656379212)
XLA Ops:
  0.6 0.0 copy-start
  0.6 7.5 %all_gather.3 = bf16[64,2048]{1,0:T(8,128)(2,1)S(1)} all-gather(bf16[64,1024]{1,0:T(8,128)(2,1)} %param.7), channel_id=1, replica_groups=mesh['subj'=2,'tr'=16] {'subj'}, dimensions={1}, use_global_device_ids=true | all-gather | bytes 393216 | tf_op jit(solution)/shard_map/all_gather | solution.py:54
  8.1 0.8 reshape.58
  8.9 6.1 %all-to-all-start = ((bf16[16,4,2048]{2,1,0:T(4,128)(2,1)}), bf16[16,4,2048]{2,1,0:T(4,128)(2,1)S(1)}, u32[]{:S(2)}, u32[]{:S(2)}) async-start(bf16[16,4,2048]{2,1,0:T(4,128)(2,1)} %reshape.58), calls=%async_computation | async-start | bytes 524288 | tf_op jit(solution)/shard_map/all_to_all | solution.py:36
  15.1 0.7 compare_select_fusion
  15.8 0.1 reshape.64
  15.9 0.7 compare_and_fusion
  16.6 8.6 %all-to-all-done = bf16[16,4,2048]{2,1,0:T(4,128)(2,1)S(1)} async-done(((bf16[16,4,2048]{2,1,0:T(4,128)(2,1)}), bf16[16,4,2048]{2,1,0:T(4,128)(2,1)S(1)}, u32[]{:S(2)}, u32[]{:S(2)}) %all-to-all-start) | async-done | bytes 262176 | tf_op jit(solution)/shard_map/all_to_all | solution.py:36
  25.1 1.4 %gather_fusion = bf16[64,4,2048]{2,1,0:T(4,128)(2,1)S(1)} fusion(bf16[16,4,2048]{2,1,0:T(4,128)(2,1)S(1)} %all-to-all-done, s32[1024]{0:T(1024)S(1)} %pad_clamp_fusion), kind=kCustom, calls=%fused_computation | custom fusion | bytes 2097408 | tf_op jit(solution)/shard_map/jit(_take)/gather | solution.py:37
  26.6 0.6 copy.23
  27.2 0.2 broadcast_select_fusion
  27.3 0.0 copy-start.4
  27.4 0.0 copy-start.2
  27.4 0.0 copy-start.3
  27.4 0.0 copy-start.1
  27.4 1.8 %copy.24 = bf16[4,16,4,2048]{3,2,0,1:T(4,128)(2,1)} copy(bf16[4,16,4,2048]{3,1,0,2:T(8,128)(2,1)S(1)} %broadcast_select_fusion) | data formatting | bytes 2097152 | tf_op jit(solution)/shard_map/jit(_take)/select_n | solution.py:37
  29.2 3.7 %all-to-all-start.1 = ((bf16[4,16,4,2048]{3,2,0,1:T(4,128)(2,1)}), bf16[4,16,4,2048]{3,2,0,1:T(4,128)(2,1)S(1)}, u32[]{:S(2)}, u32[]{:S(2)}) async-start(bf16[4,16,4,2048]{3,2,0,1:T(4,128)(2,1)} %copy.24), calls=%async_computation.1 | async-start | bytes 2097152 | tf_op jit(solution)/shard_map/all_to_all | solution.py:38
  32.9 0.4 copy.26
  33.3 0.0 copy-done.4
  33.3 0.2 convert_reduce_fusion
  33.5 0.0 copy-done.2
  33.5 0.0 copy-done.3
  33.5 0.1 select_reduce_fusion
  33.6 0.0 copy-done.1
  33.6 0.3 fusion.11
  33.9 0.1 fusion.26
  33.9 21.8 %all-to-all-done.1 = bf16[4,16,4,2048]{3,2,0,1:T(4,128)(2,1)S(1)} async-done(((bf16[4,16,4,2048]{3,2,0,1:T(4,128)(2,1)}), bf16[4,16,4,2048]{3,2,0,1:T(4,128)(2,1)S(1)}, u32[]{:S(2)}, u32[]{:S(2)}) %all-to-all-start.1) | async-done | bytes 1048608 | tf_op jit(solution)/shard_map/all_to_all | solution.py:38
  55.7 0.9 copy.25
  56.6 0.1 fusion.9
  56.8 2.5 %collective-permute-start = (bf16[5,8,2048]{2,0,1:T(8,128)(2,1)S(1)}, bf16[5,8,2048]{2,0,1:T(8,128)(2,1)S(1)}, u32[]{:S(2)}, u32[]{:S(2)}) collective-permute-start(bf16[5,8,2048]{2,0,1:T(8,128)(2,1)S(1)} %fusion.9), channel_id=1, source_target_pairs={{0,1},{1,2},{2,3},{3,4},{4,5},{5,6},{6,7},{7,8},{8,9},{9,10},{10,1... | collective-permute-start | bytes 491528 | tf_op jit(solution)/shard_map/ppermute | solution.py:17
  59.3 1.1 %collective-permute-done = bf16[5,8,2048]{2,0,1:T(8,128)(2,1)S(1)} collective-permute-done((bf16[5,8,2048]{2,0,1:T(8,128)(2,1)S(1)}, bf16[5,8,2048]{2,0,1:T(8,128)(2,1)S(1)}, u32[]{:S(2)}, u32[]{:S(2)}) %collective-permute-start) | collective-permute-done | bytes 163872 | tf_op jit(solution)/shard_map/ppermute | solution.py:17
  60.4 1.1 %maximum_maximum_fusion = bf16[5,72,2048]{2,0,1:T(8,128)(2,1)S(1)} fusion(bf16[4,64,2048]{2,0,1:T(4,128)(2,1)S(1)} %bitcast.32, bf16[1,64,2048]{2,0,1:T(2,128)(2,1)S(1)} %copy.26, bf16[5,8,2048]{2,0,1:T(8,128)(2,1)S(1)} %collective-permute-done), kind=kLoop, calls=%fused_computation.5 | loop fusion | flops 4423680 | bytes 2949120 | tf_op jit(solution)/shard_map/concatenate | solution.py:42
  61.5 5.1 %add_convert_fusion = bf16[5,64,2048]{2,0,1:T(8,128)(2,1)S(1)} fusion(bf16[4,64,2048]{2,0,1:T(4,128)(2,1)S(1)} %bitcast.33, bf16[1,64,2048]{2,0,1:T(2,128)(2,1)S(1)} %copy.26, bf16[5,72,2048]{2,0,1:T(8,128)(2,1)S(1)} %maximum_maximum_fusion, f32[2048]{0:T(1024)S(1)} %bitcast.37, f32[2048]{0:T(1024)S(1)} %bitcast.38, f32[2048]{0:T(1024)S(1)} %bitcast.39, ...), kind=kLoop, calls=%fused_computation.1 | loop fusion | flops 19660800 | bytes 13180928 | tf_op jit(solution)/shard_map/convert_element_type | solution.py:48
  66.6 0.0 copy-done
  66.6 1.6 %fusion.25 = (f32[5,256]{1,0:T(8,128)S(1)}, f32[5,64]{1,0:T(8,128)S(1)}) fusion(bf16[1,2048,256]{2,1,0:T(8,128)(2,1)S(1)} %copy-done, bf16[5,64,2048]{2,0,1:T(8,128)(2,1)S(1)} %add_convert_fusion, f32[64,256]{1,0:T(8,128)S(1)} %convert_bitcast_fusion), kind=kOutput, calls=%fused_computation.49 | convolution fusion | flops 335870400 | bytes 2431232 | tf_op jit(solution)/shard_map/ctf,fv->ctv/dot_general | solution.py:56
  68.3 35.1 %psum.7 = f32[6,256]{1,0:T(8,128)S(1)} all-reduce(f32[6,256]{1,0:T(8,128)S(1)} %pad_maximum_fusion.1), channel_id=1, replica_groups=mesh['subj'=2,'tr'=16] {'tr'}, use_global_device_ids=true, to_apply=%region_5.6 | all-reduce | flops 1536 | bytes 12288 | tf_op jit(solution)/shard_map/psum | solution.py:71
  103.4 0.2 reshape.60
  103.6 0.1 reduce_sum.59
  103.7 0.2 convolution_bitcast_fusion
  103.9 0.7 copy.28
  104.6 0.6 broadcast_in_dim.39
  (10 shorter events, 0.1 us)
Async XLA Ops:
  0.6 66.0 %copy-start = (bf16[1,2048,256]{2,1,0:T(8,128)(2,1)S(1)}, bf16[1,2048,256]{2,1,0:T(8,128)(2,1)}, u32[]{:S(2)}) copy-start(bf16[1,2048,256]{2,1,0:T(8,128)(2,1)} %param.11) | copy-start | bytes 3145732
  8.9 16.2 %all-to-all-start = ((bf16[16,4,2048]{2,1,0:T(4,128)(2,1)}), bf16[16,4,2048]{2,1,0:T(4,128)(2,1)S(1)}, u32[]{:S(2)}, u32[]{:S(2)}) async-start(bf16[16,4,2048]{2,1,0:T(4,128)(2,1)} %reshape.58), calls=%async_computation | async-start | bytes 524288 | tf_op jit(solution)/shard_map/all_to_all | solution.py:36
  27.3 5.9 %copy-start.4 = (s32[1,64,1]{1,2,0:T(1,128)S(1)}, s32[1,64,1]{1,2,0:T(1,128)}, u32[]{:S(2)}) copy-start(s32[1,64,1]{1,2,0:T(1,128)} %param.13) | copy-start | bytes 772
  27.4 6.1 %copy-start.2 = (f32[4,4]{1,0:T(4,128)S(1)}, f32[4,4]{1,0:T(4,128)}, u32[]{:S(2)}) copy-start(f32[4,4]{1,0:T(4,128)} %param.10) | copy-start | bytes 196
  27.4 6.1 %copy-start.3 = (s32[4,4]{1,0:T(4,128)S(1)}, s32[4,4]{1,0:T(4,128)}, u32[]{:S(2)}) copy-start(s32[4,4]{1,0:T(4,128)} %param.9) | copy-start | bytes 196
  27.4 6.2 %copy-start.1 = (bf16[1,64,256]{2,1,0:T(8,128)(2,1)S(1)}, bf16[1,64,256]{2,1,0:T(8,128)(2,1)}, u32[]{:S(2)}) copy-start(bf16[1,64,256]{2,1,0:T(8,128)(2,1)} %param.12) | copy-start | bytes 98308
  29.2 26.6 %all-to-all-start.1 = ((bf16[4,16,4,2048]{3,2,0,1:T(4,128)(2,1)}), bf16[4,16,4,2048]{3,2,0,1:T(4,128)(2,1)S(1)}, u32[]{:S(2)}, u32[]{:S(2)}) async-start(bf16[4,16,4,2048]{3,2,0,1:T(4,128)(2,1)} %copy.24), calls=%async_computation.1 | async-start | bytes 2097152 | tf_op jit(solution)/shard_map/all_to_all | solution.py:38
  56.8 3.6 %collective-permute-start = (bf16[5,8,2048]{2,0,1:T(8,128)(2,1)S(1)}, bf16[5,8,2048]{2,0,1:T(8,128)(2,1)S(1)}, u32[]{:S(2)}, u32[]{:S(2)}) collective-permute-start(bf16[5,8,2048]{2,0,1:T(8,128)(2,1)S(1)} %fusion.9), channel_id=1, source_target_pairs={{0,1},{1,2},{2,3},{3,4},{4,5},{5,6},{6,7},{7,8},{8,9},{9,10},{10,1... | collective-permute-start | bytes 491528 | tf_op jit(solution)/shard_map/ppermute | solution.py:17
where the time goes:
time: 106 us; the launch traced here: 105 us
  blocking collectives  42.6 us (40%)
  waiting for transfers between devices  31.5 us (30%)
  starting transfers between devices  12.3 us (12%)
  other arithmetic  8.31 us (8%)
  local copies, waits for them, and re-layouts  7.5 us (7%)
  matrix products  2.08 us (2%)
    psum x1, blocking collectives, on_device(): totals = lax.psum(stats, 'tr')  35.1 us
    all_to_all x1, waiting for transfers between devices, arrange(): lax.all_to_all(outgoing, 'tr', split_axis=1, concat_axis=1, tiled=True)  21.8 us
    all_to_all x1, waiting for transfers between devices, arrange(): lax.all_to_all(pieces, 'tr', split_axis=0, concat_axis=0, tiled=True)  8.58 us
    all_gather x1, blocking collectives, on_device(): panel = lax.all_gather(features, 'subj', axis=1, tiled=True)  7.5 us
    all_to_all x1, starting transfers between devices, arrange(): lax.all_to_all(pieces, 'tr', split_axis=0, concat_axis=0, tiled=True)  6.15 us
    convert_element_type x1, other arithmetic, arrange(): return total.astype(jnp.bfloat16)  5.08 us
    all_to_all x1, starting transfers between devices, arrange(): lax.all_to_all(outgoing, 'tr', split_axis=1, concat_axis=1, tiled=True)  3.65 us
    ppermute x1, starting transfers between devices, passed_along(): lax.ppermute(value, axis, [(source, source + steps) for source in range(l...  2.5 us
  transfers between devices with their start and end apart: 3, of which 3 were waited for; matrix products, arithmetic and copies ran while one was open for 2% of the time, Pallas kernels for 0%

commit v1 on v0

v1 whole, which is shorter than its diff:
```python
import functools

import jax
import jax.numpy as jnp
from jax import lax
from jax.experimental import pallas as pl
from jax.experimental.pallas import tpu as pltpu
from jax.sharding import PartitionSpec as P

MAXLAG = 8
VB = 4
CAP = 8
LANES = 128
EPSILON = 1e-6

f32 = jnp.float32
bf16 = jnp.bfloat16
i32 = jnp.int32

VMEM = pl.BlockSpec(memory_space=pltpu.VMEM)
SMEM = pl.BlockSpec(memory_space=pltpu.SMEM)


def iota(shape, axis):
    return lax.broadcasted_iota(i32, shape, axis)


def dot(a, b):
    return jnp.dot(a, b, preferred_element_type=f32)


def thirds(x):
    first = x.astype(bf16)
    rest = x - first.astype(f32)
    second = rest.astype(bf16)
    return first, second, (rest - second.astype(f32)).astype(bf16)


def params(**more):
    return pltpu.CompilerParams(vmem_limit_bytes=48 * 1024 * 1024, **more)


def cost(flops, nbytes):
    return pl.CostEstimate(flops=flops, bytes_accessed=nbytes, transcendentals=0)


class Sizes:
    def __init__(self, features, block_orders, offsets, weights, block_owner):
        self.subjects = lax.axis_size("subj")
        self.n = lax.axis_size("tr")
        self.rows, self.width = features.shape
        self.columns, self.voxels = weights.shape[1:]
        self.bands, self.taps = offsets.shape
        self.band_width = self.columns // self.bands
        self.piece = min(self.width, self.band_width)
        self.conditions = block_orders.shape[0] + 1
        self.blocks = block_owner.shape[1]
        self.own_rows = self.rows // self.n
        self.own_ext = self.own_rows + 1
        self.ext = self.own_ext * self.n
        self.slots = 2 * self.own_ext + self.own_rows
        self.slots_padded = -(-self.slots // 16) * 16
        self.residual_rows = (self.conditions + 1) * self.own_rows * self.n
        self.owned = CAP * VB
        self.energy_lane = (self.conditions + 1) * self.owned
        used = self.energy_lane + self.conditions * self.own_rows
        self.lanes = -(-used // LANES) * LANES
        assert self.rows % self.n == 0 and self.n >= MAXLAG


def filtered_product(z, x_ref, w_ref, table_ref, source):
    total = jnp.zeros((z.ext, z.voxels), f32)
    for part in range(z.width // z.piece):
        first = source * z.width + part * z.piece
        first = pl.multiple_of(first, z.piece)
        x = x_ref[:, part * z.piece : (part + 1) * z.piece]
        table = table_ref[lax.div(first, z.band_width)]
        stacked = jnp.concatenate([x] * (table.shape[1] // z.rows), axis=0)
        filtered = dot(table, stacked)
        high = filtered.astype(bf16)
        low = filtered - high.astype(f32)
        tail = z.rows + MAXLAG
        edges = [filtered, low[:MAXLAG], low[z.rows : tail]]
        edges = jnp.concatenate(edges, axis=0).astype(bf16)
        product = dot(edges, w_ref[pl.ds(first, z.piece), :])
        total = total + product[: z.ext]
        head = product[z.ext : z.ext + MAXLAG]
        rim = product[z.ext + MAXLAG :]
        parts = [head, jnp.zeros((z.rows - MAXLAG, z.voxels), f32), rim]
        if z.ext > tail:
            parts.append(jnp.zeros((z.ext - tail, z.voxels), f32))
        total = total + jnp.concatenate(parts, axis=0)
    return total


def fill_table(z, offsets_ref, gains_ref, table_ref):
    lanes = table_ref.shape[2]
    column = iota((z.ext, lanes), 1)
    lag = iota((z.ext, lanes), 0) - column % z.rows
    term = column // z.rows
    for band in range(z.bands):
        value = jnp.zeros((z.ext, lanes), f32)
        for tap in range(z.taps):
            hit = lag == offsets_ref[band, tap]
            value = value + jnp.where(hit, gains_ref[band, tap], 0.0)
        first, second, third = (t.astype(f32) for t in thirds(value))
        chosen = jnp.where(term == 0, first, jnp.where(term == 1, second, third))
        chosen = jnp.where(term > 2, 0.0, chosen)
        table_ref[band] = chosen.astype(bf16)


def fill_choice(z, orders_ref, choice_ref):
    shape = (z.residual_rows, z.slots_padded * z.n)
    per = z.own_rows * z.n
    permutations = z.conditions - 1
    row = iota((z.residual_rows, 1), 0)
    condition = row // per
    own = (row % per) // z.n
    position = row % z.n
    which = iota((z.residual_rows, permutations), 1)
    wanted = (which == condition - 1).astype(f32).astype(bf16)
    orders = dot(wanted, orders_ref[...].astype(f32).astype(bf16))
    place = iota((z.residual_rows, z.n), 1)
    here = jnp.sum(jnp.where(place == position, orders, 0.0), axis=1, keepdims=True)
    ahead = jnp.where(place == position - 1, orders, 0.0)
    ahead = jnp.sum(ahead, axis=1, keepdims=True)
    observed = condition == 0
    here = jnp.where(observed, position, here.astype(i32))
    ahead = jnp.where(observed, position - 1, ahead.astype(i32))
    ahead = jnp.where((position == 0) | (own > 0), -1, ahead)
    signal_only = condition == z.conditions
    here = jnp.where(signal_only, -1, here)
    ahead = jnp.where(signal_only, -1, ahead)
    column = iota(shape, 1)
    source = column // z.slots_padded
    slot = column % z.slots_padded
    half = jnp.where(slot >= z.own_ext, slot - z.own_ext, slot)
    predicted = (source == here) & (half == own) & (slot < 2 * z.own_ext)
    rim = (source == ahead) & (half == z.own_rows) & (slot < 2 * z.own_ext)
    measured = (source == position) & (slot == 2 * z.own_ext + own)
    value = jnp.where(measured, 1.0, jnp.where(predicted | rim, -1.0, 0.0))
    choice_ref[...] = value.astype(bf16)


def fill_owners(z, owners_ref, mine_ref, place_ref):
    owners = owners_ref[...]
    other = iota((z.voxels, z.blocks), 1)
    block = iota((z.voxels, 1), 0) // VB
    owner = jnp.sum(jnp.where(other == block, owners, 0), axis=1, keepdims=True)
    before = (owners == owner) & (other < block)
    rank = jnp.sum(before.astype(i32), axis=1, keepdims=True)
    lane = rank * VB + iota((z.voxels, 1), 0) % VB
    place = iota((z.voxels, LANES), 1) == lane
    place_ref[...] = place.astype(f32).astype(bf16)
    square = (z.blocks, z.blocks)
    diagonal = iota(square, 0) == iota(square, 1)
    down = jnp.sum(jnp.where(diagonal, owners, 0), axis=1, keepdims=True)
    shape = (z.blocks, z.voxels)
    held = iota(shape, 0) == iota(shape, 1) // VB
    along = jnp.sum(jnp.where(held, down, 0), axis=0, keepdims=True)
    mine_ref[...] = (iota((z.n, z.voxels), 0) == along).astype(f32)


def first_kernel(
    z, orders_ref, offsets_ref, gains_ref, owners_ref, x_ref, w_ref,
    table_ref, choice_ref, mine_ref, place_ref, total_ref,
):
    fill_table(z, offsets_ref, gains_ref, table_ref)
    me = lax.axis_index("subj")
    total_ref[...] = filtered_product(z, x_ref, w_ref, table_ref, me)
    fill_choice(z, orders_ref, choice_ref)
    fill_owners(z, owners_ref, mine_ref, place_ref)


def second_kernel(z, table_ref, w_ref, total_ref, signal_ref, *refs):
    others, out_ref = refs[:-1], refs[-1]
    me = lax.axis_index("subj")
    total = total_ref[...]
    for step, x_ref in enumerate(others):
        source = lax.rem(me + step + 1, z.subjects)
        total = total + filtered_product(z, x_ref, w_ref, table_ref, source)
    high = total.astype(bf16)
    low = total - high.astype(f32)
    stacked = jnp.concatenate([total, low, signal_ref[0].astype(f32)], axis=0)
    stacked = stacked.astype(bf16)
    shape = (z.n * z.slots_padded, z.slots * z.n)
    row = iota(shape, 0)
    column = (row % z.slots_padded) * z.n + row // z.slots_padded
    hit = (iota(shape, 1) == column) & (row % z.slots_padded < z.slots)
    order = hit.astype(f32).astype(bf16)
    out_ref[...] = dot(order, stacked).astype(bf16)


def third_kernel(z, choice_ref, mine_ref, place_ref, received_ref, out_ref):
    residual = dot(choice_ref[...], received_ref[...])
    squared = residual * residual
    per = z.own_rows * z.n
    spread = []
    for index in range(z.conditions + 1):
        stat = jnp.sum(squared[index * per : (index + 1) * per], axis=0, keepdims=True)
        spread.append(stat * mine_ref[...])
    spread = jnp.concatenate(spread, axis=0)
    terms = jnp.concatenate(thirds(spread), axis=0)
    placed = dot(terms, place_ref[...])
    count = (z.conditions + 1) * z.n
    placed = placed[:count] + placed[count : 2 * count] + placed[2 * count :]
    energy = jnp.sum(squared[: z.conditions * per], axis=1, keepdims=True)
    energy = energy * (1.0 / z.voxels)
    tiles = [jnp.zeros((z.n, LANES), f32) for _ in range(z.lanes // LANES)]
    for index in range(z.conditions + 1):
        tile, lane = divmod(index * z.owned, LANES)
        value = placed[index * z.n : (index + 1) * z.n]
        tiles[tile] = tiles[tile] + pltpu.roll(value, lane, 1)
    lanes = iota((z.n, LANES), 1)
    for own in range(z.own_rows):
        for index in range(z.conditions):
            tile, lane = divmod(z.energy_lane + own * z.conditions + index, LANES)
            start = index * per + own * z.n
            value = energy[start : start + z.n]
            tiles[tile] = jnp.where(lanes == lane, value, tiles[tile])
    out_ref[...] = jnp.concatenate(tiles, axis=1)


def fourth_kernel(z, received_ref, energy_ref, scores_ref):
    tiles = [
        received_ref[:, start : start + LANES] for start in range(0, z.lanes, LANES)
    ]
    pieces = []
    for own in range(z.own_rows):
        tile, lane = divmod(z.energy_lane + own * z.conditions, LANES)
        assert lane + z.conditions <= LANES
        pieces.append(pltpu.roll(tiles[tile], (LANES - lane) % LANES, 1))
    turned = jnp.transpose(jnp.concatenate(pieces, axis=0))
    for index in range(z.conditions):
        energy_ref[index] = turned[index : index + 1, : z.rows]
    sums = [jnp.sum(tile, axis=0, keepdims=True) for tile in tiles]
    sums = [jnp.broadcast_to(tile, (8, LANES)) for tile in sums]
    lanes = iota((8, LANES), 1)
    tile, lane = divmod(z.conditions * z.owned, LANES)
    signal = pltpu.roll(sums[tile], (LANES - lane) % LANES, 1)
    signal = jnp.where(lanes < z.owned, signal, 0.0)
    square = (LANES, LANES)
    mean = (iota(square, 0) < z.owned) & (iota(square, 0) // VB == iota(square, 1))
    mean = jnp.where(mean, 1.0 / VB, 0.0).astype(bf16)
    rows = iota((8, LANES), 0)
    fit = jnp.zeros((8, LANES), f32)
    for index in range(z.conditions):
        tile, lane = divmod(index * z.owned, LANES)
        value = pltpu.roll(sums[tile], (LANES - lane) % LANES, 1)
        fit = jnp.where(rows == index, value, fit)
    fit = jnp.where(lanes < z.owned, fit, 0.0)
    fit = jnp.log((fit + EPSILON) / (signal + EPSILON))
    terms = jnp.concatenate([t.astype(f32) for t in thirds(fit)], axis=0).astype(bf16)
    score = dot(terms, mean)
    score = score[:8] + score[8:16] + score[16:]
    for index in range(z.conditions):
        scores_ref[index] = score[index : index + 1, :CAP]


def on_device(features, block_orders, offsets, tap_gains, weights, signal, block_owner):
    z = Sizes(features, block_orders, offsets, weights, block_owner)
    assert z.conditions <= 8
    weight = weights[0]
    owners = block_owner.reshape(1, z.blocks)
    others = [
        lax.ppermute(
            features,
            "subj",
            [((i + step) % z.subjects, i) for i in range(z.subjects)],
        )
        for step in range(1, z.subjects)
    ]
    term_lanes = -(-3 * z.rows // LANES) * LANES
    work = 2 * z.ext * z.width * z.voxels
    shapes = [
        jax.ShapeDtypeStruct((z.bands, z.ext, term_lanes), bf16),
        jax.ShapeDtypeStruct((z.residual_rows, z.slots_padded * z.n), bf16),
        jax.ShapeDtypeStruct((z.n, z.voxels), f32),
        jax.ShapeDtypeStruct((z.voxels, LANES), bf16),
        jax.ShapeDtypeStruct((z.ext, z.voxels), f32),
    ]
    table, choice, mine, place, total = pl.pallas_call(
        functools.partial(first_kernel, z),
        out_shape=shapes,
        in_specs=[VMEM, SMEM, SMEM, VMEM, VMEM, VMEM],
        out_specs=[VMEM] * 5,
        compiler_params=params(),
        cost_estimate=cost(work, 3 << 20),
        name="prepare_and_own_columns",
    )(block_orders, offsets, tap_gains, owners, features, weight)
    outgoing = pl.pallas_call(
        functools.partial(second_kernel, z),
        out_shape=jax.ShapeDtypeStruct((z.n * z.slots_padded, z.voxels), bf16),
        in_specs=[VMEM] * (4 + len(others)),
        out_specs=VMEM,
        compiler_params=params(),
        cost_estimate=cost(work, 2 << 20),
        name="other_columns",
    )(table, weight, total, signal, *others)
    received = lax.all_to_all(outgoing, "tr", 0, 0, tiled=True)
    outgoing = pl.pallas_call(
        functools.partial(third_kernel, z),
        out_shape=jax.ShapeDtypeStruct((z.n, z.lanes), f32),
        in_specs=[VMEM] * 4,
        out_specs=VMEM,
        compiler_params=params(),
        cost_estimate=cost(work, 1 << 20),
        name="residuals",
    )(choice, mine, place, received)
    received = lax.all_to_all(outgoing, "tr", 0, 0, tiled=True)
    energy, scores = pl.pallas_call(
        functools.partial(fourth_kernel, z),
        out_shape=[
            jax.ShapeDtypeStruct((z.conditions, 1, z.rows), f32),
            jax.ShapeDtypeStruct((z.conditions, 1, CAP), f32),
        ],
        in_specs=[VMEM],
        out_specs=[VMEM, VMEM],
        compiler_params=params(),
        cost_estimate=cost(1 << 20, 1 << 16),
        name="scores",
    )(received)
    return energy.transpose(1, 2, 0), scores.transpose(1, 2, 0)


def solution(mesh):
    placed = (
        P("tr", "subj"),
        P(),
        P(),
        P(),
        P("subj", None, None),
        P("subj", "tr", None),
        P("subj", None, None),
    )
    return jax.shard_map(
        on_device,
        mesh=mesh,
        in_specs=placed,
        out_specs=(P("subj", "tr", None), P("subj", "tr", None)),
        check_vma=False,
    )
```

time: 106 us -> 34.2 us (0.32)
  waiting for transfers between devices: 31.5 us -> 0.01 us
  blocking collectives: 42.6 us -> 22.7 us
  starting transfers between devices: 12.3 us -> 3 us
  other arithmetic: 8.31 us -> 0 us
  local copies, waits for them, and re-layouts: 7.5 us -> 4.17 us
  Pallas kernels: 0 us -> 3.32 us
  matrix products: 2.08 us -> 0 us
    psum x1 -> x0, blocking collectives: 35.1 us -> none  [on_device(): totals = lax.psum(stats, 'tr')]
    all_to_all x2 -> x0, waiting for transfers between devices: 30.4 us -> none  [the longest x1 21.8 us: arrange(): lax.all_to_all(outgoing, 'tr', split_axis=1, concat_axis=1, tiled=True)]
    all_to_all x0 -> x2, blocking collectives: none -> 22.7 us  [on_device(): received = lax.all_to_all(outgoing, 'tr', 0, 0, tiled=True)]
    all_to_all x2 -> x0, starting transfers between devices: 9.8 us -> none  [the longest x1 6.15 us: arrange(): lax.all_to_all(pieces, 'tr', split_axis=0, concat_axis=0, tiled=True)]
    all_gather x1 -> x0, blocking collectives: 7.5 us -> none  [on_device(): panel = lax.all_gather(features, 'subj', axis=1, tiled=True)]
    convert_element_type x1 -> x0, other arithmetic: 5.08 us -> none  [arrange(): return total.astype(jnp.bfloat16)]
    unnamed x11 -> x17, local copies, waits for them, and re-layouts: 0.7 us -> 4.16 us
    pallas_call x0 -> x4, Pallas kernels: none -> 3.32 us  [the longest x1 1.38 us: on_device(): pl.pallas_call(functools.partial(first_kernel, z), out_shape=shapes, in_s...]
  transfers between devices with their start and end apart: 3 -> 1, of which waited for: 3 -> 0; matrix products, arithmetic and copies ran while one was open for 2% -> 0% of each run, Pallas kernels for 0% -> 4%
where the time goes in v1:
time: 34.2 us; the launch traced here: 33.9 us
  blocking collectives  22.7 us (66%)
  local copies, waits for them, and re-layouts  4.17 us (12%)
  Pallas kernels  3.32 us (10%)
  starting transfers between devices  3 us (9%)
  between operations  0.7 us (2%)
    all_to_all x2, blocking collectives, on_device(): received = lax.all_to_all(outgoing, 'tr', 0, 0, tiled=True)  22.7 us
    unnamed x17, local copies, waits for them, and re-layouts  4.16 us
    ppermute x1, starting transfers between devices, on_device(): lax.ppermute(features, 'subj', [((i + step) % z.subjects, i) for i in ran...  3 us
    pallas_call x1, Pallas kernels, on_device(): pl.pallas_call(functools.partial(first_kernel, z), out_shape=shapes, in_s...  1.38 us
    pallas_call x1, Pallas kernels, on_device(): pl.pallas_call(functools.partial(fourth_kernel, z), out_shape=[jax.ShapeD...  0.8 us
  transfers between devices with their start and end apart: 1, of which 0 were waited for; matrix products, arithmetic and copies ran while one was open for 0% of the time, Pallas kernels for 4%

profile of v1, /device:TPU:0, one launch (start us, length us, event | category | flops | bytes accessed | tf_op | source)
XLA Modules:
  0.0 33.9 jit_solution(8505255121476417429)
XLA Ops:
  0.6 0.0 copy-start.4
  0.6 3.0 %collective-permute-start = (bf16[64,1024]{1,0:T(8,128)(2,1)}, bf16[64,1024]{1,0:T(8,128)(2,1)S(1)}, u32[]{:S(2)}, u32[]{:S(2)}) collective-permute-start(bf16[64,1024]{1,0:T(8,128)(2,1)} %x_ref.1), channel_id=1, source_target_pairs={{16,0},{0,16},{17,1},{1,17},{18,2},{2,18},{19,3},{3,19},{20,4},{4,... | collective-permute-start | bytes 393224 | tf_op jit(solution)/shard_map/ppermute | solution.py:266
  3.6 0.0 copy-start.7
  3.6 0.0 copy-done.4
  3.7 0.7 %copy-done.7 = s32[1,64,1]{1,2,0:T(1,128)S(1)} copy-done((s32[1,64,1]{1,2,0:T(1,128)S(1)}, s32[1,64,1]{1,2,0:T(1,128)}, u32[]{:S(2)}) %copy-start.7) | copy-done | bytes 280
  4.3 0.0 copy-start
  4.3 1.2 %copy-done = bf16[1,2048,256]{2,1,0:T(8,128)(2,1)S(1)} copy-done((bf16[1,2048,256]{2,1,0:T(8,128)(2,1)S(1)}, bf16[1,2048,256]{2,1,0:T(8,128)(2,1)}, u32[]{:S(2)}) %copy-start) | copy-done | bytes 1048600
  5.5 0.0 copy-start.2
  5.5 0.9 %copy-done.2 = bf16[64,1024]{1,0:T(8,128)(2,1)S(1)} copy-done((bf16[64,1024]{1,0:T(8,128)(2,1)S(1)}, bf16[64,1024]{1,0:T(8,128)(2,1)}, u32[]{:S(2)}) %copy-start.2) | copy-done | bytes 131096
  6.4 0.0 copy-start.5
  6.4 0.7 %copy-done.5 = s32[4,4]{1,0:T(4,128)S(1)} copy-done((s32[4,4]{1,0:T(4,128)S(1)}, s32[4,4]{1,0:T(4,128)}, u32[]{:S(2)}) %copy-start.5) | copy-done | bytes 88
  7.1 0.0 copy-start.6
  7.1 0.7 %copy-done.6 = f32[4,4]{1,0:T(4,128)S(1)} copy-done((f32[4,4]{1,0:T(4,128)S(1)}, f32[4,4]{1,0:T(4,128)}, u32[]{:S(2)}) %copy-start.6) | copy-done | bytes 88
  7.8 0.0 copy-start.1
  7.8 0.0 copy-start.3
  7.8 1.4 %prepare_and_own_columns.1 = (bf16[4,80,256]{2,1,0:T(8,128)(2,1)S(1)}, bf16[384,256]{1,0:T(8,128)(2,1)S(1)}, f32[16,256]{1,0:T(8,128)S(1)}, bf16[256,128]{1,0:T(8,128)(2,1)S(1)}, f32[80,256]{1,0:T(8,128)S(1)}) custom-call(s32[4,16]{1,0:T(4,128)S(1)} %copy-done.4, s32[4,4]{1,0:T(4,128)S(1)} %copy-done.5, f32[4,4]{1,0:T(4,128)S(1)} %copy-done.6, ...), custom_call_target="tpu_custom_call" | custom-call | flops 41943040 | bytes 3145728 | tf_op jit(solution)/shard_map/prepare_and_own_columns/pallas_call | solution.py:282
  9.2 0.0 collective-permute-done.refs_0_
  9.2 0.0 copy-done.1
  9.2 0.0 copy-done.3
  9.2 0.6 %other_columns.1 = bf16[256,256]{1,0:T(8,128)(2,1)S(1)} custom-call(bf16[4,80,256]{2,1,0:T(8,128)(2,1)S(1)} %get-tuple-element.12.table_ref, bf16[2048,256]{1,0:T(8,128)(2,1)S(1)} %bitcast.11, f32[80,256]{1,0:T(8,128)S(1)} %get-tuple-element.13.total_ref, bf16[1,64,256]{2,1,0:T(8,128)(2,1)S(1)} %copy-done.3, bf16[64,1024]{1,0:T(8,128)(2,1)S(1)} %collective-permute-done.refs_0_), custom_call_target="tpu_custom_call" | custom-call | flops 41943040 | bytes 2097152 | tf_op jit(solution)/shard_map/other_columns/pallas_call | solution.py:291
  9.8 13.7 %all_to_all.22 = bf16[16,16,256]{2,1,0:T(8,128)(2,1)S(1)} all-to-all(bf16[16,16,256]{2,1,0:T(8,128)(2,1)S(1)} %bitcast.12), channel_id=1, replica_groups=mesh['subj'=2,'tr'=16] {'tr'}, dimensions={0} | all-to-all | bytes 262144 | tf_op jit(solution)/shard_map/all_to_all | solution.py:300
  23.5 0.5 %residuals.1 = f32[16,256]{1,0:T(8,128)S(1)} custom-call(bf16[384,256]{1,0:T(8,128)(2,1)S(1)} %get-tuple-element.9.choice_ref, f32[16,256]{1,0:T(8,128)S(1)} %get-tuple-element.10.mine_ref, bf16[256,128]{1,0:T(8,128)(2,1)S(1)} %get-tuple-element.11.place_ref, bf16[256,256]{1,0:T(8,128)(2,1)S(1)} %bitcast.13), custom_call_target="tpu_custom_call" | custom-call | flops 41943040 | bytes 1048576 | tf_op jit(solution)/shard_map/residuals/pallas_call | solution.py:301
  24.1 9.1 %all_to_all.23 = f32[16,1,256]{2,1,0:T(1,128)S(1)} all-to-all(f32[16,1,256]{2,1,0:T(1,128)S(1)} %copy.9), channel_id=1, replica_groups=mesh['subj'=2,'tr'=16] {'tr'}, dimensions={0} | all-to-all | bytes 32768 | tf_op jit(solution)/shard_map/all_to_all | solution.py:310
  33.1 0.8 %scores.1 = (f32[5,1,64]{2,1,0:T(1,128)}, f32[5,1,8]{2,1,0:T(1,128)}) custom-call(f32[16,256]{1,0:T(8,128)S(1)} %bitcast.14), custom_call_target="tpu_custom_call" | custom-call | flops 1048576 | bytes 65536 | tf_op jit(solution)/shard_map/scores/pallas_call | solution.py:311
  (2 shorter events, 0.0 us)
Async XLA Ops:
  0.6 3.0 %copy-start.4 = (s32[4,16]{1,0:T(4,128)S(1)}, s32[4,16]{1,0:T(4,128)}, u32[]{:S(2)}) copy-start(s32[4,16]{1,0:T(4,128)} %orders_ref.1) | copy-start | bytes 772
  0.6 8.6 %collective-permute-start = (bf16[64,1024]{1,0:T(8,128)(2,1)}, bf16[64,1024]{1,0:T(8,128)(2,1)S(1)}, u32[]{:S(2)}, u32[]{:S(2)}) collective-permute-start(bf16[64,1024]{1,0:T(8,128)(2,1)} %x_ref.1), channel_id=1, source_target_pairs={{16,0},{0,16},{17,1},{1,17},{18,2},{2,18},{19,3},{3,19},{20,4},{4,... | collective-permute-start | bytes 393224 | tf_op jit(solution)/shard_map/ppermute | solution.py:266
  3.6 0.7 %copy-start.7 = (s32[1,64,1]{1,2,0:T(1,128)S(1)}, s32[1,64,1]{1,2,0:T(1,128)}, u32[]{:S(2)}) copy-start(s32[1,64,1]{1,2,0:T(1,128)} %param.13) | copy-start | bytes 772
  4.3 1.2 %copy-start = (bf16[1,2048,256]{2,1,0:T(8,128)(2,1)S(1)}, bf16[1,2048,256]{2,1,0:T(8,128)(2,1)}, u32[]{:S(2)}) copy-start(bf16[1,2048,256]{2,1,0:T(8,128)(2,1)} %param.11) | copy-start | bytes 3145732
  5.5 0.9 %copy-start.2 = (bf16[64,1024]{1,0:T(8,128)(2,1)S(1)}, bf16[64,1024]{1,0:T(8,128)(2,1)}, u32[]{:S(2)}) copy-start(bf16[64,1024]{1,0:T(8,128)(2,1)} %x_ref.1) | copy-start | bytes 393220
  6.4 0.7 %copy-start.5 = (s32[4,4]{1,0:T(4,128)S(1)}, s32[4,4]{1,0:T(4,128)}, u32[]{:S(2)}) copy-start(s32[4,4]{1,0:T(4,128)} %offsets_ref.1) | copy-start | bytes 196
  7.1 0.7 %copy-start.6 = (f32[4,4]{1,0:T(4,128)S(1)}, f32[4,4]{1,0:T(4,128)}, u32[]{:S(2)}) copy-start(f32[4,4]{1,0:T(4,128)} %gains_ref.1) | copy-start | bytes 196
  7.8 1.4 %copy-start.1 = (bf16[1,2048,256]{2,1,0:T(8,128)(2,1)S(1)}, bf16[1,2048,256]{2,1,0:T(8,128)(2,1)}, u32[]{:S(2)}) copy-start(bf16[1,2048,256]{2,1,0:T(8,128)(2,1)} %param.11) | copy-start | bytes 3145732
  7.8 1.4 %copy-start.3 = (bf16[1,64,256]{2,1,0:T(8,128)(2,1)S(1)}, bf16[1,64,256]{2,1,0:T(8,128)(2,1)}, u32[]{:S(2)}) copy-start(bf16[1,64,256]{2,1,0:T(8,128)(2,1)} %signal_ref.1) | copy-start | bytes 98308

commit v2 on v1

--- a/solution.py
+++ b/solution.py
@@ -18,7 +18,7 @@
 i32 = jnp.int32
 
 VMEM = pl.BlockSpec(memory_space=pltpu.VMEM)
-SMEM = pl.BlockSpec(memory_space=pltpu.SMEM)
+HBM = pl.BlockSpec(memory_space=pltpu.HBM)
 
 
 def iota(shape, axis):
@@ -71,10 +71,9 @@
 def filtered_product(z, x_ref, w_ref, table_ref, source):
     total = jnp.zeros((z.ext, z.voxels), f32)
     for part in range(z.width // z.piece):
-        first = source * z.width + part * z.piece
-        first = pl.multiple_of(first, z.piece)
-        x = x_ref[:, part * z.piece : (part + 1) * z.piece]
-        table = table_ref[lax.div(first, z.band_width)]
+        columns = slice(part * z.piece, (part + 1) * z.piece)
+        x = x_ref[:, columns]
+        table = table_ref[lax.div(source * z.width + part * z.piece, z.band_width)]
         stacked = jnp.concatenate([x] * (table.shape[1] // z.rows), axis=0)
         filtered = dot(table, stacked)
         high = filtered.astype(bf16)
@@ -82,7 +81,7 @@
         tail = z.rows + MAXLAG
         edges = [filtered, low[:MAXLAG], low[z.rows : tail]]
         edges = jnp.concatenate(edges, axis=0).astype(bf16)
-        product = dot(edges, w_ref[pl.ds(first, z.piece), :])
+        product = dot(edges, w_ref[columns, :])
         total = total + product[: z.ext]
         head = product[z.ext : z.ext + MAXLAG]
         rim = product[z.ext + MAXLAG :]
@@ -162,14 +161,47 @@
 
 
 def first_kernel(
-    z, orders_ref, offsets_ref, gains_ref, owners_ref, x_ref, w_ref,
-    table_ref, choice_ref, mine_ref, place_ref, total_ref,
+    z, orders_hbm, offsets_hbm, gains_hbm, owners_hbm, x_hbm, w_hbm, signal_hbm,
+    table_ref, choice_ref, mine_ref, place_ref, total_ref, rest_ref, signal_ref,
+    orders_ref, offsets_ref, gains_ref, owners_ref, x_ref, w_ref, sems,
 ):
+    me = lax.axis_index("subj")
+
+    def weight_rows(step):
+        source = lax.rem(me + step, z.subjects)
+        start = pl.multiple_of(source * z.width, z.width)
+        return w_hbm.at[pl.ds(start, z.width), :]
+
+    moves = [
+        (offsets_hbm, offsets_ref),
+        (gains_hbm, gains_ref),
+        (x_hbm, x_ref),
+        (weight_rows(0), w_ref),
+        (orders_hbm, orders_ref),
+        (owners_hbm, owners_ref),
+        (signal_hbm, signal_ref),
+    ]
+    for step in range(1, z.subjects):
+        rows = pl.ds((step - 1) * z.width, z.width)
+        moves.append((weight_rows(step), rest_ref.at[rows, :]))
+    copies = [
+        pltpu.make_async_copy(origin, target, sems.at[index])
+        for index, (origin, target) in enumerate(moves)
+    ]
+    for copy in copies:
+        copy.start()
+    copies[0].wait()
+    copies[1].wait()
     fill_table(z, offsets_ref, gains_ref, table_ref)
-    me = lax.axis_index("subj")
+    copies[2].wait()
+    copies[3].wait()
     total_ref[...] = filtered_product(z, x_ref, w_ref, table_ref, me)
+    copies[4].wait()
     fill_choice(z, orders_ref, choice_ref)
+    copies[5].wait()
     fill_owners(z, owners_ref, mine_ref, place_ref)
+    for copy in copies[6:]:
+        copy.wait()
 
 
 def second_kernel(z, table_ref, w_ref, total_ref, signal_ref, *refs):
@@ -178,10 +210,11 @@
     total = total_ref[...]
     for step, x_ref in enumerate(others):
         source = lax.rem(me + step + 1, z.subjects)
-        total = total + filtered_product(z, x_ref, w_ref, table_ref, source)
+        rows = w_ref.at[step * z.width : (step + 1) * z.width, :]
+        total = total + filtered_product(z, x_ref, rows, table_ref, source)
     high = total.astype(bf16)
     low = total - high.astype(f32)
-    stacked = jnp.concatenate([total, low, signal_ref[0].astype(f32)], axis=0)
+    stacked = jnp.concatenate([total, low, signal_ref[...].astype(f32)], axis=0)
     stacked = stacked.astype(bf16)
     shape = (z.n * z.slots_padded, z.slots * z.n)
     row = iota(shape, 0)
@@ -278,16 +311,28 @@
         jax.ShapeDtypeStruct((z.n, z.voxels), f32),
         jax.ShapeDtypeStruct((z.voxels, LANES), bf16),
         jax.ShapeDtypeStruct((z.ext, z.voxels), f32),
-    ]
-    table, choice, mine, place, total = pl.pallas_call(
+        jax.ShapeDtypeStruct((z.columns - z.width, z.voxels), bf16),
+        jax.ShapeDtypeStruct((z.rows, z.voxels), bf16),
+    ]
+    scratch = [
+        pltpu.VMEM(block_orders.shape, i32),
+        pltpu.SMEM(offsets.shape, i32),
+        pltpu.SMEM(tap_gains.shape, f32),
+        pltpu.VMEM(owners.shape, i32),
+        pltpu.VMEM(features.shape, bf16),
+        pltpu.VMEM((z.width, z.voxels), bf16),
+        pltpu.SemaphoreType.DMA((6 + z.subjects,)),
+    ]
+    table, choice, mine, place, total, rest, signal = pl.pallas_call(
         functools.partial(first_kernel, z),
         out_shape=shapes,
-        in_specs=[VMEM, SMEM, SMEM, VMEM, VMEM, VMEM],
-        out_specs=[VMEM] * 5,
+        in_specs=[HBM] * 7,
+        out_specs=[VMEM] * 7,
+        scratch_shapes=scratch,
         compiler_params=params(),
         cost_estimate=cost(work, 3 << 20),
         name="prepare_and_own_columns",
-    )(block_orders, offsets, tap_gains, owners, features, weight)
+    )(block_orders, offsets, tap_gains, owners, features, weight, signal[0])
     outgoing = pl.pallas_call(
         functools.partial(second_kernel, z),
         out_shape=jax.ShapeDtypeStruct((z.n * z.slots_padded, z.voxels), bf16),
@@ -296,7 +341,7 @@
         compiler_params=params(),
         cost_estimate=cost(work, 2 << 20),
         name="other_columns",
-    )(table, weight, total, signal, *others)
+    )(table, rest, total, signal, *others)
     received = lax.all_to_all(outgoing, "tr", 0, 0, tiled=True)
     outgoing = pl.pallas_call(
         functools.partial(third_kernel, z),

time: 34.2 us -> 34.9 us (1.020)
  Pallas kernels: 3.32 us -> 3.8 us
    pallas_call x1, Pallas kernels: 1.38 us -> 1.87 us  [on_device(): pl.pallas_call(functools.partial(first_kernel, z), out_shape=shapes, in_s...]
    unnamed x17 -> x15, local copies, waits for them, and re-layouts: 4.16 us -> 4.27 us
  transfers between devices with their start and end apart: 1 -> 1, of which waited for: 0 -> 0; matrix products, arithmetic and copies ran while one was open for 0% -> 0% of each run, Pallas kernels for 4% -> 5%
where the time goes in v2:
time: 34.9 us; the launch traced here: 34.5 us
  blocking collectives  22.7 us (65%)
  local copies, waits for them, and re-layouts  4.28 us (12%)
  Pallas kernels  3.8 us (11%)
  starting transfers between devices  3 us (9%)
  between operations  0.67 us (2%)
    all_to_all x2, blocking collectives, on_device(): received = lax.all_to_all(outgoing, 'tr', 0, 0, tiled=True)  22.7 us
    unnamed x15, local copies, waits for them, and re-layouts  4.27 us
    ppermute x1, starting transfers between devices, on_device(): lax.ppermute(features, 'subj', [((i + step) % z.subjects, i) for i in ran...  3 us
    pallas_call x1, Pallas kernels, on_device(): pl.pallas_call(functools.partial(first_kernel, z), out_shape=shapes, in_s...  1.87 us
    pallas_call x1, Pallas kernels, on_device(): pl.pallas_call(functools.partial(fourth_kernel, z), out_shape=[jax.ShapeD...  0.8 us
  transfers between devices with their start and end apart: 1, of which 0 were waited for; matrix products, arithmetic and copies ran while one was open for 0% of the time, Pallas kernels for 5%

profile of v2, /device:TPU:0, one launch (start us, length us, event | category | flops | bytes accessed | tf_op | source)
XLA Modules:
  0.0 34.5 jit_solution(6926332342153422232)
XLA Ops:
  0.6 3.0 %collective-permute-start = (bf16[64,1024]{1,0:T(8,128)(2,1)}, bf16[64,1024]{1,0:T(8,128)(2,1)S(1)}, u32[]{:S(2)}, u32[]{:S(2)}) collective-permute-start(bf16[64,1024]{1,0:T(8,128)(2,1)} %x_hbm.1), channel_id=1, source_target_pairs={{16,0},{0,16},{17,1},{1,17},{18,2},{2,18},{19,3},{3,19},{20,4},{4,... | collective-permute-start | bytes 393224 | tf_op jit(solution)/shard_map/ppermute | solution.py:299
  3.6 0.0 copy-start.4
  3.6 0.0 copy-start.3
  3.6 0.0 copy-start.6
  3.6 0.7 %copy-done.4 = s32[4,4]{1,0:T(4,128)S(1)} copy-done((s32[4,4]{1,0:T(4,128)S(1)}, s32[4,4]{1,0:T(4,128)}, u32[]{:S(2)}) %copy-start.4) | copy-done | bytes 88
  4.3 0.0 copy-done.3
  4.3 0.0 copy-done.6
  4.3 0.0 copy-start
  4.3 1.2 %copy-done = bf16[1,2048,256]{2,1,0:T(8,128)(2,1)S(1)} copy-done((bf16[1,2048,256]{2,1,0:T(8,128)(2,1)S(1)}, bf16[1,2048,256]{2,1,0:T(8,128)(2,1)}, u32[]{:S(2)}) %copy-start) | copy-done | bytes 1048600
  5.6 0.0 copy-start.1
  5.6 0.9 %copy-done.1 = bf16[64,1024]{1,0:T(8,128)(2,1)S(1)} copy-done((bf16[64,1024]{1,0:T(8,128)(2,1)S(1)}, bf16[64,1024]{1,0:T(8,128)(2,1)}, u32[]{:S(2)}) %copy-start.1) | copy-done | bytes 131096
  6.5 0.0 copy-start.2
  6.5 0.8 %copy-done.2 = bf16[1,64,256]{2,1,0:T(8,128)(2,1)S(1)} copy-done((bf16[1,64,256]{2,1,0:T(8,128)(2,1)S(1)}, bf16[1,64,256]{2,1,0:T(8,128)(2,1)}, u32[]{:S(2)}) %copy-start.2) | copy-done | bytes 32792
  7.2 0.0 copy-start.5
  7.2 0.7 %copy-done.5 = f32[4,4]{1,0:T(4,128)S(1)} copy-done((f32[4,4]{1,0:T(4,128)S(1)}, f32[4,4]{1,0:T(4,128)}, u32[]{:S(2)}) %copy-start.5) | copy-done | bytes 88
  7.9 1.9 %prepare_and_own_columns.1 = (bf16[4,80,256]{2,1,0:T(8,128)(2,1)S(1)}, bf16[384,256]{1,0:T(8,128)(2,1)S(1)}, f32[16,256]{1,0:T(8,128)S(1)}, bf16[256,128]{1,0:T(...) custom-call(s32[4,16]{1,0:T(4,128)S(1)} %copy-done.3, ...), custom_call_target="tpu_custom_call" | custom-call | flops 41943040 | bytes 3145728 | tf_op jit(solution)/shard_map/prepare_and_own_columns/pallas_call | solution.py:326
  9.8 0.0 collective-permute-done.refs_0_
  9.8 0.6 %other_columns.1 = bf16[256,256]{1,0:T(8,128)(2,1)S(1)} custom-call(bf16[4,80,256]{2,1,0:T(8,128)(2,1)S(1)} %get-tuple-element.14.table_ref, bf16[1024,256]{1,0:T(8,128)(2,1)S(1)} %get-tuple-element.15.w_ref, f32[80,256]{1,0:T(8,128)S(1)} %get-tuple-element.16.total_ref, bf16[64,256]{1,0:T(8,128)(2,1)S(1)} %get-tuple-element.17.signal_ref, ...), custom_call_target="tpu_custom_call" | custom-call | flops 41943040 | bytes 2097152 | tf_op jit(solution)/shard_map/other_columns/pallas_call | solution.py:336
  10.4 13.7 %all_to_all.22 = bf16[16,16,256]{2,1,0:T(8,128)(2,1)S(1)} all-to-all(bf16[16,16,256]{2,1,0:T(8,128)(2,1)S(1)} %bitcast.13), channel_id=1, replica_groups=mesh['subj'=2,'tr'=16] {'tr'}, dimensions={0} | all-to-all | bytes 262144 | tf_op jit(solution)/shard_map/all_to_all | solution.py:345
  24.1 0.5 %residuals.1 = f32[16,256]{1,0:T(8,128)S(1)} custom-call(bf16[384,256]{1,0:T(8,128)(2,1)S(1)} %get-tuple-element.11.choice_ref, f32[16,256]{1,0:T(8,128)S(1)} %get-tuple-element.12.mine_ref, bf16[256,128]{1,0:T(8,128)(2,1)S(1)} %get-tuple-element.13.place_ref, bf16[256,256]{1,0:T(8,128)(2,1)S(1)} %bitcast.12), custom_call_target="tpu_custom_call" | custom-call | flops 41943040 | bytes 1048576 | tf_op jit(solution)/shard_map/residuals/pallas_call | solution.py:346
  24.6 9.1 %all_to_all.23 = f32[16,1,256]{2,1,0:T(1,128)S(1)} all-to-all(f32[16,1,256]{2,1,0:T(1,128)S(1)} %copy.9), channel_id=1, replica_groups=mesh['subj'=2,'tr'=16] {'tr'}, dimensions={0} | all-to-all | bytes 32768 | tf_op jit(solution)/shard_map/all_to_all | solution.py:355
  33.7 0.8 %scores.1 = (f32[5,1,64]{2,1,0:T(1,128)}, f32[5,1,8]{2,1,0:T(1,128)}) custom-call(f32[16,256]{1,0:T(8,128)S(1)} %bitcast.14), custom_call_target="tpu_custom_call" | custom-call | flops 1048576 | bytes 65536 | tf_op jit(solution)/shard_map/scores/pallas_call | solution.py:356
  (2 shorter events, 0.0 us)
Async XLA Ops:
  0.6 9.2 %collective-permute-start = (bf16[64,1024]{1,0:T(8,128)(2,1)}, bf16[64,1024]{1,0:T(8,128)(2,1)S(1)}, u32[]{:S(2)}, u32[]{:S(2)}) collective-permute-start(bf16[64,1024]{1,0:T(8,128)(2,1)} %x_hbm.1), channel_id=1, source_target_pairs={{16,0},{0,16},{17,1},{1,17},{18,2},{2,18},{19,3},{3,19},{20,4},{4,... | collective-permute-start | bytes 393224 | tf_op jit(solution)/shard_map/ppermute | solution.py:299
  3.6 0.7 %copy-start.4 = (s32[4,4]{1,0:T(4,128)S(1)}, s32[4,4]{1,0:T(4,128)}, u32[]{:S(2)}) copy-start(s32[4,4]{1,0:T(4,128)} %offsets_hbm.1) | copy-start | bytes 196
  3.6 0.7 %copy-start.3 = (s32[4,16]{1,0:T(4,128)S(1)}, s32[4,16]{1,0:T(4,128)}, u32[]{:S(2)}) copy-start(s32[4,16]{1,0:T(4,128)} %orders_hbm.1) | copy-start | bytes 772
  3.6 0.7 %copy-start.6 = (s32[1,64,1]{1,2,0:T(1,128)S(1)}, s32[1,64,1]{1,2,0:T(1,128)}, u32[]{:S(2)}) copy-start(s32[1,64,1]{1,2,0:T(1,128)} %param.13) | copy-start | bytes 772
  4.3 1.2 %copy-start = (bf16[1,2048,256]{2,1,0:T(8,128)(2,1)S(1)}, bf16[1,2048,256]{2,1,0:T(8,128)(2,1)}, u32[]{:S(2)}) copy-start(bf16[1,2048,256]{2,1,0:T(8,128)(2,1)} %param.11) | copy-start | bytes 3145732
  5.6 0.9 %copy-start.1 = (bf16[64,1024]{1,0:T(8,128)(2,1)S(1)}, bf16[64,1024]{1,0:T(8,128)(2,1)}, u32[]{:S(2)}) copy-start(bf16[64,1024]{1,0:T(8,128)(2,1)} %x_hbm.1) | copy-start | bytes 393220
  6.5 0.8 %copy-start.2 = (bf16[1,64,256]{2,1,0:T(8,128)(2,1)S(1)}, bf16[1,64,256]{2,1,0:T(8,128)(2,1)}, u32[]{:S(2)}) copy-start(bf16[1,64,256]{2,1,0:T(8,128)(2,1)} %param.12) | copy-start | bytes 98308
  7.2 0.7 %copy-start.5 = (f32[4,4]{1,0:T(4,128)S(1)}, f32[4,4]{1,0:T(4,128)}, u32[]{:S(2)}) copy-start(f32[4,4]{1,0:T(4,128)} %gains_hbm.1) | copy-start | bytes 196

commit v3 on v2

--- a/solution.py
+++ b/solution.py
@@ -323,6 +323,8 @@
         pltpu.VMEM((z.width, z.voxels), bf16),
         pltpu.SemaphoreType.DMA((6 + z.subjects,)),
     ]
+    operands = (block_orders, offsets, tap_gains, owners, features, weight, signal[0])
+    operands = [pltpu.with_memory_space_constraint(x, pltpu.HBM) for x in operands]
     table, choice, mine, place, total, rest, signal = pl.pallas_call(
         functools.partial(first_kernel, z),
         out_shape=shapes,
@@ -332,7 +334,7 @@
         compiler_params=params(),
         cost_estimate=cost(work, 3 << 20),
         name="prepare_and_own_columns",
-    )(block_orders, offsets, tap_gains, owners, features, weight, signal[0])
+    )(*operands)
     outgoing = pl.pallas_call(
         functools.partial(second_kernel, z),
         out_shape=jax.ShapeDtypeStruct((z.n * z.slots_padded, z.voxels), bf16),

time: 34.9 us -> 32.5 us (0.931)
  local copies, waits for them, and re-layouts: 4.28 us -> 0.02 us
  waiting for transfers between devices: 0.01 us -> 1.53 us
    unnamed x15 -> x1, local copies, waits for them, and re-layouts: 4.27 us -> 0.01 us
    ppermute x1, waiting for transfers between devices: 0.01 us -> 1.53 us  [on_device(): lax.ppermute(features, 'subj', [((i + step) % z.subjects, i) for i in ran...]
  transfers between devices with their start and end apart: 1 -> 1, of which waited for: 0 -> 1; matrix products, arithmetic and copies ran while one was open for 0% -> 0% of each run, Pallas kernels for 5% -> 7%
where the time goes in v3:
time: 32.5 us; the launch traced here: 32.3 us
  blocking collectives  23 us (71%)
  Pallas kernels  4.1 us (13%)
  starting transfers between devices  3 us (9%)
  waiting for transfers between devices  1.53 us (5%)
  between operations  0.66 us (2%)
    all_to_all x2, blocking collectives, on_device(): received = lax.all_to_all(outgoing, 'tr', 0, 0, tiled=True)  23 us
    ppermute x1, starting transfers between devices, on_device(): lax.ppermute(features, 'subj', [((i + step) % z.subjects, i) for i in ran...  3 us
    pallas_call x1, Pallas kernels, on_device(): pl.pallas_call(functools.partial(first_kernel, z), out_shape=shapes, in_s...  2.17 us
    ppermute x1, waiting for transfers between devices, on_device(): lax.ppermute(features, 'subj', [((i + step) % z.subjects, i) for i in ran...  1.53 us
    pallas_call x1, Pallas kernels, on_device(): pl.pallas_call(functools.partial(fourth_kernel, z), out_shape=[jax.ShapeD...  0.8 us
  transfers between devices with their start and end apart: 1, of which 1 were waited for; matrix products, arithmetic and copies ran while one was open for 0% of the time, Pallas kernels for 7%

profile of v3, /device:TPU:0, one launch (start us, length us, event | category | flops | bytes accessed | tf_op | source)
XLA Modules:
  0.0 32.3 jit_solution(2009925196553162738)
XLA Ops:
  0.6 3.0 %collective-permute-start = (bf16[64,1024]{1,0:T(8,128)(2,1)}, bf16[64,1024]{1,0:T(8,128)(2,1)S(1)}, u32[]{:S(2)}, u32[]{:S(2)}) collective-permute-start(bf16[64,1024]{1,0:T(8,128)(2,1)} %x_hbm.1), channel_id=1, source_target_pairs={{16,0},{0,16},{17,1},{1,17},{18,2},{2,18},{19,3},{3,19},{20,4},{4,... | collective-permute-start | bytes 393224 | tf_op jit(solution)/shard_map/ppermute | solution.py:299
  3.6 2.2 %prepare_and_own_columns.1 = (bf16[4,80,256]{2,1,0:T(8,128)(2,1)S(1)}, bf16[384,256]{1,0:T(8,128)(2,1)S(1)}, f32[16,256]{1,0:T(8,128)S(1)}, bf16[256,128]{1,0:T(...) custom-call(s32[4,16]{1,0:T(4,128)} %orders_hbm.1, ...), custom_call_target="tpu_custom_call" | custom-call | flops 41943040 | bytes 3145728 | tf_op jit(solution)/shard_map/prepare_and_own_columns/pallas_call | solution.py:328
  5.8 1.5 %collective-permute-done.refs_0_ = bf16[64,1024]{1,0:T(8,128)(2,1)S(1)} collective-permute-done((bf16[64,1024]{1,0:T(8,128)(2,1)}, bf16[64,1024]{1,0:T(8,128)(2,1)S(1)}, u32[]{:S(2)}, u32[]{:S(2)}) %collective-permute-start) | collective-permute-done | bytes 131104 | tf_op jit(solution)/shard_map/ppermute | solution.py:299
  7.3 0.6 %other_columns.1 = bf16[256,256]{1,0:T(8,128)(2,1)S(1)} custom-call(bf16[4,80,256]{2,1,0:T(8,128)(2,1)S(1)} %get-tuple-element.14.table_ref, bf16[1024,256]{1,0:T(8,128)(2,1)S(1)} %get-tuple-element.15.w_ref, f32[80,256]{1,0:T(8,128)S(1)} %get-tuple-element.16.total_ref, bf16[64,256]{1,0:T(8,128)(2,1)S(1)} %get-tuple-element.17.signal_ref, ...), custom_call_target="tpu_custom_call" | custom-call | flops 41943040 | bytes 2097152 | tf_op jit(solution)/shard_map/other_columns/pallas_call | solution.py:338
  8.0 13.9 %all_to_all.22 = bf16[16,16,256]{2,1,0:T(8,128)(2,1)S(1)} all-to-all(bf16[16,16,256]{2,1,0:T(8,128)(2,1)S(1)} %bitcast.12), channel_id=1, replica_groups=mesh['subj'=2,'tr'=16] {'tr'}, dimensions={0} | all-to-all | bytes 262144 | tf_op jit(solution)/shard_map/all_to_all | solution.py:347
  21.9 0.5 %residuals.1 = f32[16,256]{1,0:T(8,128)S(1)} custom-call(bf16[384,256]{1,0:T(8,128)(2,1)S(1)} %get-tuple-element.11.choice_ref, f32[16,256]{1,0:T(8,128)S(1)} %get-tuple-element.12.mine_ref, bf16[256,128]{1,0:T(8,128)(2,1)S(1)} %get-tuple-element.13.place_ref, bf16[256,256]{1,0:T(8,128)(2,1)S(1)} %bitcast.11), custom_call_target="tpu_custom_call" | custom-call | flops 41943040 | bytes 1048576 | tf_op jit(solution)/shard_map/residuals/pallas_call | solution.py:348
  22.4 9.1 %all_to_all.23 = f32[16,1,256]{2,1,0:T(1,128)S(1)} all-to-all(f32[16,1,256]{2,1,0:T(1,128)S(1)} %copy.9), channel_id=1, replica_groups=mesh['subj'=2,'tr'=16] {'tr'}, dimensions={0} | all-to-all | bytes 32768 | tf_op jit(solution)/shard_map/all_to_all | solution.py:357
  31.5 0.8 %scores.1 = (f32[5,1,64]{2,1,0:T(1,128)}, f32[5,1,8]{2,1,0:T(1,128)}) custom-call(f32[16,256]{1,0:T(8,128)S(1)} %bitcast.13), custom_call_target="tpu_custom_call" | custom-call | flops 1048576 | bytes 65536 | tf_op jit(solution)/shard_map/scores/pallas_call | solution.py:358
  (2 shorter events, 0.0 us)
Async XLA Ops:
  0.6 6.7 %collective-permute-start = (bf16[64,1024]{1,0:T(8,128)(2,1)}, bf16[64,1024]{1,0:T(8,128)(2,1)S(1)}, u32[]{:S(2)}, u32[]{:S(2)}) collective-permute-start(bf16[64,1024]{1,0:T(8,128)(2,1)} %x_hbm.1), channel_id=1, source_target_pairs={{16,0},{0,16},{17,1},{1,17},{18,2},{2,18},{19,3},{3,19},{20,4},{4,... | collective-permute-start | bytes 393224 | tf_op jit(solution)/shard_map/ppermute | solution.py:299

commit v4 on v3

v4 whole, which is shorter than its diff:
```python
import functools

import jax
import jax.numpy as jnp
from jax import lax
from jax.experimental import pallas as pl
from jax.experimental.pallas import tpu as pltpu
from jax.sharding import PartitionSpec as P

MAXLAG = 8
VB = 4
CAP = 8
LANES = 128
GROUP = 4
EPSILON = 1e-6

f32 = jnp.float32
bf16 = jnp.bfloat16
i32 = jnp.int32

VMEM = pl.BlockSpec(memory_space=pltpu.VMEM)
SMEM = pl.BlockSpec(memory_space=pltpu.SMEM)
HBM = pl.BlockSpec(memory_space=pltpu.HBM)


def iota(shape, axis):
    return lax.broadcasted_iota(i32, shape, axis)


def dot(a, b):
    return jnp.dot(a, b, preferred_element_type=f32)


def thirds(x):
    first = x.astype(bf16)
    rest = x - first.astype(f32)
    second = rest.astype(bf16)
    return first, second, (rest - second.astype(f32)).astype(bf16)


def params(**more):
    return pltpu.CompilerParams(vmem_limit_bytes=48 * 1024 * 1024, **more)


def cost(flops, nbytes):
    return pl.CostEstimate(flops=flops, bytes_accessed=nbytes, transcendentals=0)


class Sizes:
    def __init__(self, features, block_orders, offsets, weights, block_owner):
        self.subjects = lax.axis_size("subj")
        self.n = lax.axis_size("tr")
        self.rows, self.width = features.shape
        self.columns, self.voxels = weights.shape[1:]
        self.bands, self.taps = offsets.shape
        self.band_width = self.columns // self.bands
        self.piece = min(self.width, self.band_width)
        self.conditions = block_orders.shape[0] + 1
        self.blocks = block_owner.shape[1]
        self.ext = self.rows + MAXLAG
        self.own = self.rows // GROUP
        self.own_tail = MAXLAG // GROUP
        self.tiles = self.voxels // LANES
        self.signal_at = self.tiles * self.own
        self.tail_at = 2 * self.signal_at
        self.scale_at = self.tail_at + self.tiles * self.own_tail
        self.signal_scale_at = self.scale_at + self.tiles
        self.message = -(-(self.signal_scale_at + self.tiles) // 8) * 8
        assert self.n % GROUP == 0 and self.own % 8 == 0 and self.conditions < 8
        assert self.own_tail <= 8 and CAP * VB <= LANES


def coded(x):
    largest = jnp.max(jnp.abs(x), axis=0, keepdims=True)
    power = jnp.floor(jnp.log2(jnp.maximum(largest, 2.0**-100))) + 1.0
    value = jnp.round(x * jnp.exp2(15.0 - power))
    return jnp.clip(value, -32767.0, 32767.0), power


def arranged(z, x, order):
    value, power = coded(x)
    upper = jnp.floor(value * (1.0 / 256.0))
    lower = value - 256.0 * upper
    powers = jnp.broadcast_to(power, (8, z.voxels))
    high, low = [], []
    for tile in range(z.tiles):
        lanes = slice(tile * LANES, (tile + 1) * LANES)
        high += [upper[:, lanes], jnp.zeros((8, LANES), f32)]
        low += [lower[:, lanes], powers[:, lanes]]
    high = jnp.concatenate(high, axis=0).astype(bf16)
    low = jnp.concatenate(low, axis=0).astype(bf16)
    return 256.0 * dot(order, high) + dot(order, low)


def filtered_product(z, x_ref, w_ref, table_ref, source):
    total = jnp.zeros((z.ext, z.voxels), f32)
    for part in range(z.width // z.piece):
        columns = slice(part * z.piece, (part + 1) * z.piece)
        x = x_ref[:, columns]
        table = table_ref[lax.div(source * z.width + part * z.piece, z.band_width)]
        stacked = jnp.concatenate([x] * (table.shape[1] // z.rows), axis=0)
        filtered = dot(table, stacked)
        high = filtered.astype(bf16)
        low = filtered - high.astype(f32)
        tail = z.rows + MAXLAG
        edges = [filtered, low[:MAXLAG], low[z.rows : tail]]
        edges = jnp.concatenate(edges, axis=0).astype(bf16)
        product = dot(edges, w_ref[columns, :])
        total = total + product[: z.ext]
        head = product[z.ext : z.ext + MAXLAG]
        rim = product[z.ext + MAXLAG :]
        parts = [head, jnp.zeros((z.rows - MAXLAG, z.voxels), f32), rim]
        if z.ext > tail:
            parts.append(jnp.zeros((z.ext - tail, z.voxels), f32))
        total = total + jnp.concatenate(parts, axis=0)
    return total


def fill_table(z, offsets_ref, gains_ref, table_ref):
    lanes = table_ref.shape[2]
    column = iota((z.ext, lanes), 1)
    lag = iota((z.ext, lanes), 0) - column % z.rows
    term = column // z.rows
    for band in range(z.bands):
        value = jnp.zeros((z.ext, lanes), f32)
        for tap in range(z.taps):
            hit = lag == offsets_ref[band, tap]
            value = value + jnp.where(hit, gains_ref[band, tap], 0.0)
        first, second, third = (t.astype(f32) for t in thirds(value))
        chosen = jnp.where(term == 0, first, jnp.where(term == 1, second, third))
        chosen = jnp.where(term > 2, 0.0, chosen)
        table_ref[band] = chosen.astype(bf16)


def fill_order(z, order_ref, rows, body_at, tail_at, scale_at):
    row = iota((GROUP * z.message, 1), 0)
    member = row // z.message
    place = row % z.message
    per = rows + 8
    body = place - body_at
    source = (body // z.own) * per + member + GROUP * (body % z.own)
    source = jnp.where((body >= 0) & (body < z.tiles * z.own), source, -1)
    if tail_at is not None:
        tail = place - tail_at
        found = (tail // z.own_tail) * per + z.rows + member
        found = found + GROUP * (tail % z.own_tail)
        source = jnp.where((tail >= 0) & (tail < z.tiles * z.own_tail), found, source)
    scale = place - scale_at
    source = jnp.where((scale >= 0) & (scale < z.tiles), scale * per + rows, source)
    column = iota((GROUP * z.message, z.tiles * per), 1)
    order_ref[...] = (column == source).astype(f32).astype(bf16)


def fill_owners(z, owners_ref, along_ref, place_ref):
    owners = owners_ref[...]
    other = iota((z.voxels, z.blocks), 1)
    block = iota((z.voxels, 1), 0) // VB
    owner = jnp.sum(jnp.where(other == block, owners, 0), axis=1, keepdims=True)
    before = (owners == owner) & (other < block)
    rank = jnp.sum(before.astype(i32), axis=1, keepdims=True)
    lane = rank * VB + iota((z.voxels, 1), 0) % VB
    place = iota((z.voxels, LANES), 1) == lane
    place_ref[...] = place.astype(f32).astype(bf16)
    square = (z.blocks, z.blocks)
    diagonal = iota(square, 0) == iota(square, 1)
    down = jnp.sum(jnp.where(diagonal, owners, 0), axis=1, keepdims=True)
    shape = (z.blocks, z.voxels)
    held = iota(shape, 0) == iota(shape, 1) // VB
    along = jnp.sum(jnp.where(held, down, 0), axis=0, keepdims=True)
    along_ref[...] = jnp.broadcast_to(along, (8, z.voxels))


def first_kernel(
    z, offsets_hbm, gains_hbm, owners_hbm, x_hbm, w_hbm, signal_hbm,
    table_ref, order_ref, base_ref, along_ref, place_ref, total_ref, rest_ref,
    offsets_ref, gains_ref, owners_ref, x_ref, w_ref, signal_ref, signal_order_ref, sems,
):
    me = lax.axis_index("subj")

    def weight_rows(step):
        source = lax.rem(me + step, z.subjects)
        start = pl.multiple_of(source * z.width, z.width)
        return w_hbm.at[pl.ds(start, z.width), :]

    moves = [
        (offsets_hbm, offsets_ref),
        (gains_hbm, gains_ref),
        (x_hbm, x_ref),
        (weight_rows(0), w_ref),
        (owners_hbm, owners_ref),
        (signal_hbm, signal_ref),
    ]
    for step in range(1, z.subjects):
        rows = pl.ds((step - 1) * z.width, z.width)
        moves.append((weight_rows(step), rest_ref.at[rows, :]))
    copies = [
        pltpu.make_async_copy(origin, target, sems.at[index])
        for index, (origin, target) in enumerate(moves)
    ]
    for copy in copies:
        copy.start()
    copies[0].wait()
    copies[1].wait()
    fill_table(z, offsets_ref, gains_ref, table_ref)
    copies[2].wait()
    copies[3].wait()
    total_ref[...] = filtered_product(z, x_ref, w_ref, table_ref, me)
    fill_order(z, order_ref, z.ext, 0, z.tail_at, z.scale_at)
    fill_order(z, signal_order_ref, z.rows, z.signal_at, None, z.signal_scale_at)
    copies[4].wait()
    fill_owners(z, owners_ref, along_ref, place_ref)
    copies[5].wait()
    base_ref[...] = arranged(z, signal_ref[...].astype(f32), signal_order_ref[...])
    for copy in copies[6:]:
        copy.wait()


def second_kernel(z, table_ref, w_ref, total_ref, order_ref, base_ref, *refs):
    others, out_ref = refs[:-1], refs[-1]
    me = lax.axis_index("subj")
    total = total_ref[...]
    for step, x_ref in enumerate(others):
        source = lax.rem(me + step + 1, z.subjects)
        rows = w_ref.at[step * z.width : (step + 1) * z.width, :]
        total = total + filtered_product(z, x_ref, rows, table_ref, source)
    messages = arranged(z, total, order_ref[...]) + base_ref[...]
    for member in range(GROUP):
        message = messages[member * z.message : (member + 1) * z.message]
        message = message.astype(i32).astype(jnp.int16)
        for index in range(member, z.n, GROUP):
            out_ref[index] = message


def third_kernel(z, orders_ref, along_ref, place_ref, received_ref, *refs):
    out_refs, (block_ref, tail_ref, signal_ref) = refs[:GROUP], refs[GROUP:]
    me = lax.axis_index("tr")
    row = iota((8, LANES), 0)

    def unpack(index, _):
        x = received_ref[index].astype(i32).astype(f32)
        scales = jnp.exp2(x[z.scale_at : z.scale_at + 2 * z.tiles] - 15.0)
        for tile in range(z.tiles):
            scale = scales[tile : tile + 1]
            own = slice(tile * z.own, (tile + 1) * z.own)
            block_ref[index, own, :] = x[own] * scale
            at = z.tail_at + tile * z.own_tail
            start = at // 8 * 8
            tail = pltpu.roll(x[start : start + 8], (8 - at % 8) % 8, 0)
            tail = jnp.where(row < z.own_tail, tail * scale, 0.0)
            tail_ref[index, tile * 8 : (tile + 1) * 8, :] = tail
            scale = scales[z.tiles + tile : z.tiles + tile + 1]
            values = x[z.signal_at + tile * z.own : z.signal_at + (tile + 1) * z.own]
            signal_ref[index, own, :] = values * scale
        return 0

    for index in range(z.n) if z.n <= 16 else ():
        unpack(index, 0)
    if z.n > 16:
        lax.fori_loop(0, z.n, unpack, 0)
    tail_ref[z.n] = jnp.zeros((z.tiles * 8, LANES), f32)

    def folded(x):
        return [
            sum(
                x[tile * z.own + start : tile * z.own + start + 8]
                for start in range(0, z.own, 8)
            )
            for tile in range(z.tiles)
        ]

    def squares(position, condition):
        signal = signal_ref[position]
        if condition == z.conditions:
            return signal * signal
        if condition == 0:
            here, ahead = position, position - 1
        else:
            here = orders_ref[condition - 1, position]
            ahead = orders_ref[condition - 1, jnp.maximum(position - 1, 0)]
        ahead = jnp.where(position == 0, z.n, ahead)
        residual = signal - block_ref[here]
        tail = tail_ref[ahead]
        parts = []
        for tile in range(z.tiles):
            start = tile * z.own
            head = residual[start : start + 8] - tail[tile * 8 : (tile + 1) * 8]
            parts += [head, residual[start + 8 : start + z.own]]
        residual = jnp.concatenate(parts, axis=0)
        return residual * residual

    def add_position(position, sums):
        added = []
        for condition in range(z.conditions + 1):
            parts = folded(squares(position, condition))
            old = sums[condition * z.tiles : (condition + 1) * z.tiles]
            added += [o + p for o, p in zip(old, parts)]
        return tuple(added)

    def add_positions(step, sums):
        for index in range(GROUP):
            sums = add_position(step * GROUP + index, sums)
        return sums

    zero = jnp.zeros((8, LANES), f32)
    sums = tuple(zero for _ in range((z.conditions + 1) * z.tiles))
    sums = lax.fori_loop(0, z.n // GROUP, add_positions, sums)
    stats = []
    for tile in range(z.tiles):
        value = zero
        for condition in range(z.conditions + 1):
            stat = jnp.sum(sums[condition * z.tiles + tile], axis=0, keepdims=True)
            value = jnp.where(row == condition, stat, value)
        stats.append(value)
    stats = jnp.concatenate(stats, axis=1)
    masked = [
        jnp.where(along_ref[...] == jnp.bitwise_xor(me, step), stats, 0.0)
        for step in range(GROUP)
    ]
    terms = jnp.concatenate(
        [t.astype(f32) for t in thirds(jnp.concatenate(masked, axis=0))], axis=0
    )
    placed = dot(terms.astype(bf16), place_ref[...])
    placed = placed[: GROUP * 8] + placed[GROUP * 8 : GROUP * 16] + placed[GROUP * 16 :]
    lanes = iota((z.own, LANES), 1)
    for step, out_ref in enumerate(out_refs):
        energy = jnp.zeros((z.own, LANES), f32)
        for condition in range(z.conditions):
            value = squares(jnp.bitwise_xor(me, step), condition)
            value = sum(
                value[tile * z.own : (tile + 1) * z.own] for tile in range(z.tiles)
            )
            value = jnp.sum(value, axis=1, keepdims=True) * (1.0 / z.voxels)
            energy = jnp.where(lanes == condition, value, energy)
        out_ref[: z.own, :] = energy
        out_ref[z.own :, :] = placed[step * 8 : (step + 1) * 8]


def fourth_kernel(z, *refs):
    parts, (energy_ref, scores_ref) = refs[:GROUP], refs[GROUP:]
    member = lax.rem(lax.axis_index("tr"), GROUP)
    turned = jnp.transpose(jnp.concatenate([p[: z.own, :] for p in parts], axis=0))
    column = iota((z.rows, LANES), 0)
    owner = jnp.bitwise_xor(column // z.own, member)
    order = iota((z.rows, LANES), 1) == owner + GROUP * (column % z.own)
    order = order.astype(f32).astype(bf16)
    terms = [t.astype(f32) for t in thirds(turned[:8, : z.rows])]
    energy = dot(jnp.concatenate(terms, axis=0).astype(bf16), order)
    energy = energy[:8] + energy[8:16] + energy[16:]
    sums = sum(p[z.own :, :] for p in parts)
    lanes = iota((8, LANES), 1)
    sums = jnp.where(lanes < CAP * VB, sums, 0.0)
    signal = sums[z.conditions : z.conditions + 1]
    square = (LANES, LANES)
    mean = iota(square, 0) // VB == iota(square, 1)
    mean = jnp.where(mean & (iota(square, 1) < CAP), 1.0 / VB, 0.0).astype(bf16)
    fit = jnp.log((sums + EPSILON) / (signal + EPSILON))
    terms = jnp.concatenate([t.astype(f32) for t in thirds(fit)], axis=0).astype(bf16)
    score = dot(terms, mean)
    score = score[:8] + score[8:16] + score[16:]
    for index in range(z.conditions):
        energy_ref[index] = energy[index : index + 1, : z.rows]
        scores_ref[index] = score[index : index + 1, :CAP]


def on_device(features, block_orders, offsets, tap_gains, weights, signal, block_owner):
    z = Sizes(features, block_orders, offsets, weights, block_owner)
    owners = block_owner.reshape(1, z.blocks)
    others = [
        lax.ppermute(
            features,
            "subj",
            [((i + step) % z.subjects, i) for i in range(z.subjects)],
        )
        for step in range(1, z.subjects)
    ]
    term_lanes = -(-3 * z.rows // LANES) * LANES
    work = 2 * z.ext * z.width * z.voxels
    messages = GROUP * z.message
    shapes = [
        jax.ShapeDtypeStruct((z.bands, z.ext, term_lanes), bf16),
        jax.ShapeDtypeStruct((messages, z.tiles * (z.ext + 8)), bf16),
        jax.ShapeDtypeStruct((messages, LANES), f32),
        jax.ShapeDtypeStruct((8, z.voxels), i32),
        jax.ShapeDtypeStruct((z.voxels, LANES), bf16),
        jax.ShapeDtypeStruct((z.ext, z.voxels), f32),
        jax.ShapeDtypeStruct((z.columns - z.width, z.voxels), bf16),
    ]
    scratch = [
        pltpu.SMEM(offsets.shape, i32),
        pltpu.SMEM(tap_gains.shape, f32),
        pltpu.VMEM(owners.shape, i32),
        pltpu.VMEM(features.shape, bf16),
        pltpu.VMEM((z.width, z.voxels), bf16),
        pltpu.VMEM((z.rows, z.voxels), bf16),
        pltpu.VMEM((messages, z.tiles * (z.rows + 8)), bf16),
        pltpu.SemaphoreType.DMA((5 + z.subjects,)),
    ]
    operands = (offsets, tap_gains, owners, features, weights[0], signal[0])
    operands = [pltpu.with_memory_space_constraint(x, pltpu.HBM) for x in operands]
    table, order, base, along, place, total, rest = pl.pallas_call(
        functools.partial(first_kernel, z),
        out_shape=shapes,
        in_specs=[HBM] * 6,
        out_specs=[VMEM] * 7,
        scratch_shapes=scratch,
        compiler_params=params(),
        cost_estimate=cost(work, 3 << 20),
        name="prepare_and_own_columns",
    )(*operands)
    outgoing = pl.pallas_call(
        functools.partial(second_kernel, z),
        out_shape=jax.ShapeDtypeStruct((z.n, z.message, LANES), jnp.int16),
        in_specs=[VMEM] * (5 + len(others)),
        out_specs=VMEM,
        compiler_params=params(),
        cost_estimate=cost(work, 2 << 20),
        name="other_columns",
    )(table, rest, total, order, base, *others)
    received = lax.all_to_all(outgoing, "tr", 0, 0, tiled=True)
    orders = pltpu.with_memory_space_constraint(block_orders, pltpu.SMEM)
    part = jax.ShapeDtypeStruct((z.own + 8, LANES), f32)
    parts = pl.pallas_call(
        functools.partial(third_kernel, z),
        out_shape=[part] * GROUP,
        in_specs=[SMEM, VMEM, VMEM, VMEM],
        out_specs=[VMEM] * GROUP,
        scratch_shapes=[
            pltpu.VMEM((z.n, z.tiles * z.own, LANES), f32),
            pltpu.VMEM((z.n + 1, z.tiles * 8, LANES), f32),
            pltpu.VMEM((z.n, z.tiles * z.own, LANES), f32),
        ],
        compiler_params=params(),
        cost_estimate=cost(work, 1 << 20),
        name="residuals",
    )(orders, along, place, received)
    parts = [parts[0]] + [
        lax.ppermute(parts[step], "tr", [(i, i ^ step) for i in range(z.n)])
        for step in range(1, GROUP)
    ]
    energy, scores = pl.pallas_call(
        functools.partial(fourth_kernel, z),
        out_shape=[
            jax.ShapeDtypeStruct((z.conditions, 1, z.rows), f32),
            jax.ShapeDtypeStruct((z.conditions, 1, CAP), f32),
        ],
        in_specs=[VMEM] * GROUP,
        out_specs=[VMEM, VMEM],
        compiler_params=params(),
        cost_estimate=cost(1 << 20, 1 << 16),
        name="scores",
    )(*parts)
    return energy.transpose(1, 2, 0), scores.transpose(1, 2, 0)


def solution(mesh):
    placed = (
        P("tr", "subj"),
        P(),
        P(),
        P(),
        P("subj", None, None),
        P("subj", "tr", None),
        P("subj", None, None),
    )
    return jax.shard_map(
        on_device,
        mesh=mesh,
        in_specs=placed,
        out_specs=(P("subj", "tr", None), P("subj", "tr", None)),
        check_vma=False,
    )
```

time: 32.5 us -> 31.3 us (0.963)
  blocking collectives: 23 us -> 16.6 us
  starting transfers between devices: 3 us -> 4.94 us
  Pallas kernels: 4.1 us -> 5.52 us
  waiting for transfers between devices: 1.53 us -> 2.76 us
  local copies, waits for them, and re-layouts: 0.02 us -> 0.68 us
    all_to_all x2 -> x1, blocking collectives: 23 us -> 16.6 us  [on_device(): received = lax.all_to_all(outgoing, 'tr', 0, 0, tiled=True)]
    ppermute x0 -> x3, waiting for transfers between devices: none -> 2.04 us  [on_device(): lax.ppermute(parts[step], 'tr', [(i, i ^ step) for i in range(z.n)])]
    ppermute x0 -> x3, starting transfers between devices: none -> 1.93 us  [on_device(): lax.ppermute(parts[step], 'tr', [(i, i ^ step) for i in range(z.n)])]
    ppermute x1, waiting for transfers between devices: 1.53 us -> 0.72 us  [on_device(): lax.ppermute(features, 'subj', [((i + step) % z.subjects, i) for i in ran...]
    pallas_call x1, Pallas kernels: 2.17 us -> 2.98 us  [on_device(): pl.pallas_call(functools.partial(first_kernel, z), out_shape=shapes, in_s...]
    unnamed x1 -> x2, local copies, waits for them, and re-layouts: 0.01 us -> 0.68 us
    pallas_call x1, Pallas kernels: 0.52 us -> 1.1 us  [on_device(): pl.pallas_call(functools.partial(third_kernel, z), out_shape=[part] * GRO...]
  transfers between devices with their start and end apart: 1 -> 4, of which waited for: 1 -> 2; matrix products, arithmetic and copies ran while one was open for 0% -> 0% of each run, Pallas kernels for 7% -> 10%
where the time goes in v4:
time: 31.3 us; the launch traced here: 31.1 us
  blocking collectives  16.6 us (53%)
  Pallas kernels  5.52 us (18%)
  starting transfers between devices  4.94 us (16%)
  waiting for transfers between devices  2.76 us (9%)
  local copies, waits for them, and re-layouts  0.68 us (2%)
  between operations  0.67 us (2%)
    all_to_all x1, blocking collectives, on_device(): received = lax.all_to_all(outgoing, 'tr', 0, 0, tiled=True)  16.6 us
    ppermute x1, starting transfers between devices, on_device(): lax.ppermute(features, 'subj', [((i + step) % z.subjects, i) for i in ran...  3 us
    pallas_call x1, Pallas kernels, on_device(): pl.pallas_call(functools.partial(first_kernel, z), out_shape=shapes, in_s...  2.98 us
    ppermute x3, waiting for transfers between devices, on_device(): lax.ppermute(parts[step], 'tr', [(i, i ^ step) for i in range(z.n)])  2.04 us
    ppermute x3, starting transfers between devices, on_device(): lax.ppermute(parts[step], 'tr', [(i, i ^ step) for i in range(z.n)])  1.93 us
    pallas_call x1, Pallas kernels, on_device(): pl.pallas_call(functools.partial(third_kernel, z), out_shape=[part] * GRO...  1.1 us
    pallas_call x1, Pallas kernels, on_device(): pl.pallas_call(functools.partial(fourth_kernel, z), out_shape=[jax.ShapeD...  0.77 us
    ppermute x1, waiting for transfers between devices, on_device(): lax.ppermute(features, 'subj', [((i + step) % z.subjects, i) for i in ran...  0.72 us
  transfers between devices with their start and end apart: 4, of which 2 were waited for; matrix products, arithmetic and copies ran while one was open for 0% of the time, Pallas kernels for 10%

profile of v4, /device:TPU:0, one launch (start us, length us, event | category | flops | bytes accessed | tf_op | source)
XLA Modules:
  0.0 31.1 jit_solution(11917620992221816932)
XLA Ops:
  0.6 3.0 %collective-permute-start = (bf16[64,1024]{1,0:T(8,128)(2,1)}, bf16[64,1024]{1,0:T(8,128)(2,1)S(1)}, u32[]{:S(2)}, u32[]{:S(2)}) collective-permute-start(bf16[64,1024]{1,0:T(8,128)(2,1)} %x_hbm.1), channel_id=1, source_target_pairs={{16,0},{0,16},{17,1},{1,17},{18,2},{2,18},{19,3},{3,19},{20,4},{4,... | collective-permute-start | bytes 393224 | tf_op jit(solution)/shard_map/ppermute | solution.py:369
  3.6 3.0 %prepare_and_own_columns.1 = (bf16[4,72,256]{2,1,0:T(8,128)(2,1)S(1)}, bf16[288,160]{1,0:T(8,128)(2,1)S(1)}, f32[288,128]{1,0:T(8,128)S(1)}, s32[8,256]{1,0:T(8,...) custom-call(s32[4,4]{1,0:T(4,128)} %offsets_hbm.1, ...), custom_call_target="tpu_custom_call" | custom-call | flops 37748736 | bytes 3145728 | tf_op jit(solution)/shard_map/prepare_and_own_columns/pallas_call | solution.py:400
  6.6 0.7 %collective-permute-done.refs_0_ = bf16[64,1024]{1,0:T(8,128)(2,1)S(1)} collective-permute-done((bf16[64,1024]{1,0:T(8,128)(2,1)}, bf16[64,1024]{1,0:T(8,128)(2,1)S(1)}, u32[]{:S(2)}, u32[]{:S(2)}) %collective-permute-start) | collective-permute-done | bytes 131104 | tf_op jit(solution)/shard_map/ppermute | solution.py:369
  7.3 0.7 %other_columns.1 = s16[16,72,128]{2,1,0:T(8,128)(2,1)S(1)} custom-call(bf16[4,72,256]{2,1,0:T(8,128)(2,1)S(1)} %get-tuple-element.17.table_ref, bf16[1024,256]{1,0:T(8,128)(2,1)S(1)} %get-tuple-element.18.w_ref, f32[72,256]{1,0:T(8,128)S(1)} %get-tuple-element.19.total_ref, bf16[288,160]{1,0:T(8,128)(2,1)S(1)} %get-tuple-element.20.order_ref, ...), custom_call_target="tpu_custom_call" | custom-call | flops 37748736 | bytes 2097152 | tf_op jit(solution)/shard_map/other_columns/pallas_call | solution.py:410
  8.0 16.6 %all_to_all.5.received_ref = s16[16,72,128]{2,1,0:T(8,128)(2,1)S(1)} all-to-all(s16[16,72,128]{2,1,0:T(8,128)(2,1)S(1)} %other_columns.1), channel_id=1, replica_groups=mesh['subj'=2,'tr'=16] {'tr'}, dimensions={0} | all-to-all | bytes 589824 | tf_op jit(solution)/shard_map/all_to_all | solution.py:419
  24.6 0.0 copy-start
  24.6 0.7 %copy-done = s32[4,16]{1,0:T(4,128)S(1)} copy-done((s32[4,16]{1,0:T(4,128)S(1)}, s32[4,16]{1,0:T(4,128)}, u32[]{:S(2)}) %copy-start) | copy-done | bytes 280
  25.3 1.1 %residuals.1 = (f32[24,128]{1,0:T(8,128)S(1)}, f32[24,128]{1,0:T(8,128)S(1)}, f32[24,128]{1,0:T(8,128)S(1)}, f32[24,128]{1,0:T(8,128)S(1)}) custom-call(s32[4,16]{1,0:T(4,128)S(1)} %copy-done, s32[8,256]{1,0:T(8,128)S(1)} %get-tuple-element.15.along_ref, bf16[256,128]{1,0:T(8,128)(2,1)S(1)} %get-tuple-element.16.place_ref, ...), custom_call_target="tpu_custom_call" | custom-call | flops 37748736 | bytes 1048576 | tf_op jit(solution)/shard_map/residuals/pallas_call | solution.py:422
  26.4 0.1 collective-permute-start.1
  26.4 0.7 %collective-permute-start.2 = (f32[24,128]{1,0:T(8,128)S(1)}, f32[24,128]{1,0:T(8,128)S(1)}, u32[]{:S(2)}, u32[]{:S(2)}) collective-permute-start(f32[24,128]{1,0:T(8,128)S(1)} %get-tuple-element.24), channel_id=1, source_target_pairs={{0,2},{1,3},{2,0},{3,1},{4,6},{5,7},{6,4},{7,5},{8,10},{9,11},{10,... | collective-permute-start | bytes 36872 | tf_op jit(solution)/shard_map/ppermute | solution.py:437
  27.1 1.2 %collective-permute-start.3 = (f32[24,128]{1,0:T(8,128)S(1)}, f32[24,128]{1,0:T(8,128)S(1)}, u32[]{:S(2)}, u32[]{:S(2)}) collective-permute-start(f32[24,128]{1,0:T(8,128)S(1)} %get-tuple-element.25), channel_id=1, source_target_pairs={{0,3},{1,2},{2,1},{3,0},{4,7},{5,6},{6,5},{7,4},{8,11},{9,10},{10,... | collective-permute-start | bytes 36872 | tf_op jit(solution)/shard_map/ppermute | solution.py:437
  28.3 0.0 collective-permute-done.1.refs_1_
  28.3 2.0 %collective-permute-done.2.refs_2_ = f32[24,128]{1,0:T(8,128)S(1)} collective-permute-done((f32[24,128]{1,0:T(8,128)S(1)}, f32[24,128]{1,0:T(8,128)S(1)}, u32[]{:S(2)}, u32[]{:S(2)}) %collective-permute-start.2) | collective-permute-done | bytes 12320 | tf_op jit(solution)/shard_map/ppermute | solution.py:437
  30.3 0.0 collective-permute-done.3.refs_3_
  30.3 0.8 %scores.1 = (f32[5,1,64]{2,1,0:T(1,128)}, f32[5,1,8]{2,1,0:T(1,128)}) custom-call(f32[24,128]{1,0:T(8,128)S(1)} %get-tuple-element.22.refs_0_, f32[24,128]{1,0:T(8,128)S(1)} %collective-permute-done.1.refs_1_, f32[24,128]{1,0:T(8,128)S(1)} %collective-permute-done.2.refs_2_, f32[24,128]{1,0:T(8,128)S(1)} %collective-permute-done.3.refs_3_), custom_call_target="tpu_custom_call" | custom-call | flops 1048576 | bytes 65536 | tf_op jit(solution)/shard_map/scores/pallas_call | solution.py:440
Async XLA Ops:
  0.6 6.7 %collective-permute-start = (bf16[64,1024]{1,0:T(8,128)(2,1)}, bf16[64,1024]{1,0:T(8,128)(2,1)S(1)}, u32[]{:S(2)}, u32[]{:S(2)}) collective-permute-start(bf16[64,1024]{1,0:T(8,128)(2,1)} %x_hbm.1), channel_id=1, source_target_pairs={{16,0},{0,16},{17,1},{1,17},{18,2},{2,18},{19,3},{3,19},{20,4},{4,... | collective-permute-start | bytes 393224 | tf_op jit(solution)/shard_map/ppermute | solution.py:369
  24.6 0.7 %copy-start = (s32[4,16]{1,0:T(4,128)S(1)}, s32[4,16]{1,0:T(4,128)}, u32[]{:S(2)}) copy-start(s32[4,16]{1,0:T(4,128)} %orders_ref.1) | copy-start | bytes 772
  26.4 1.9 %collective-permute-start.1 = (f32[24,128]{1,0:T(8,128)S(1)}, f32[24,128]{1,0:T(8,128)S(1)}, u32[]{:S(2)}, u32[]{:S(2)}) collective-permute-start(f32[24,128]{1,0:T(8,128)S(1)} %get-tuple-element.23), channel_id=1, source_target_pairs={{0,1},{1,0},{2,3},{3,2},{4,5},{5,4},{6,7},{7,6},{8,9},{9,8},{10,11... | collective-permute-start | bytes 36872 | tf_op jit(solution)/shard_map/ppermute | solution.py:437
  26.4 3.9 %collective-permute-start.2 = (f32[24,128]{1,0:T(8,128)S(1)}, f32[24,128]{1,0:T(8,128)S(1)}, u32[]{:S(2)}, u32[]{:S(2)}) collective-permute-start(f32[24,128]{1,0:T(8,128)S(1)} %get-tuple-element.24), channel_id=1, source_target_pairs={{0,2},{1,3},{2,0},{3,1},{4,6},{5,7},{6,4},{7,5},{8,10},{9,11},{10,... | collective-permute-start | bytes 36872 | tf_op jit(solution)/shard_map/ppermute | solution.py:437
  27.1 3.3 %collective-permute-start.3 = (f32[24,128]{1,0:T(8,128)S(1)}, f32[24,128]{1,0:T(8,128)S(1)}, u32[]{:S(2)}, u32[]{:S(2)}) collective-permute-start(f32[24,128]{1,0:T(8,128)S(1)} %get-tuple-element.25), channel_id=1, source_target_pairs={{0,3},{1,2},{2,1},{3,0},{4,7},{5,6},{6,5},{7,4},{8,11},{9,10},{10,... | collective-permute-start | bytes 36872 | tf_op jit(solution)/shard_map/ppermute | solution.py:437

commit v5 on v4

--- a/solution.py
+++ b/solution.py
@@ -19,7 +19,6 @@
 i32 = jnp.int32
 
 VMEM = pl.BlockSpec(memory_space=pltpu.VMEM)
-SMEM = pl.BlockSpec(memory_space=pltpu.SMEM)
 HBM = pl.BlockSpec(memory_space=pltpu.HBM)
 
 
@@ -77,8 +76,8 @@
     return jnp.clip(value, -32767.0, 32767.0), power
 
 
-def arranged(z, x, order):
-    value, power = coded(x)
+def signal_messages(z, signal, order):
+    value, power = coded(signal)
     upper = jnp.floor(value * (1.0 / 256.0))
     lower = value - 256.0 * upper
     powers = jnp.broadcast_to(power, (8, z.voxels))
@@ -94,24 +93,26 @@
 
 def filtered_product(z, x_ref, w_ref, table_ref, source):
     total = jnp.zeros((z.ext, z.voxels), f32)
+    early = iota((8, z.piece), 0) < z.own_tail
     for part in range(z.width // z.piece):
         columns = slice(part * z.piece, (part + 1) * z.piece)
         x = x_ref[:, columns]
         table = table_ref[lax.div(source * z.width + part * z.piece, z.band_width)]
         stacked = jnp.concatenate([x] * (table.shape[1] // z.rows), axis=0)
         filtered = dot(table, stacked)
-        high = filtered.astype(bf16)
-        low = filtered - high.astype(f32)
-        tail = z.rows + MAXLAG
-        edges = [filtered, low[:MAXLAG], low[z.rows : tail]]
+        low = filtered - filtered.astype(bf16).astype(f32)
+        edges = [filtered]
+        for start in range(0, z.rows, z.own):
+            edges.append(jnp.where(early, low[start : start + 8], 0.0))
+        edges.append(low[z.rows :])
         edges = jnp.concatenate(edges, axis=0).astype(bf16)
         product = dot(edges, w_ref[columns, :])
-        total = total + product[: z.ext]
-        head = product[z.ext : z.ext + MAXLAG]
-        rim = product[z.ext + MAXLAG :]
-        parts = [head, jnp.zeros((z.rows - MAXLAG, z.voxels), f32), rim]
-        if z.ext > tail:
-            parts.append(jnp.zeros((z.ext - tail, z.voxels), f32))
+        parts = []
+        for member in range(GROUP):
+            start, at = member * z.own, z.ext + member * 8
+            parts.append(product[start : start + 8] + product[at : at + 8])
+            parts.append(product[start + 8 : start + z.own])
+        parts.append(product[z.rows : z.ext] + product[z.ext + GROUP * 8 :])
         total = total + jnp.concatenate(parts, axis=0)
     return total
 
@@ -119,7 +120,11 @@
 def fill_table(z, offsets_ref, gains_ref, table_ref):
     lanes = table_ref.shape[2]
     column = iota((z.ext, lanes), 1)
-    lag = iota((z.ext, lanes), 0) - column % z.rows
+    row = iota((z.ext, 1), 0)
+    after = row - z.rows
+    time = row // z.own + GROUP * (row % z.own)
+    time_after = z.rows + after // z.own_tail + GROUP * (after % z.own_tail)
+    lag = jnp.where(after < 0, time, time_after) - column % z.rows
     term = column // z.rows
     for band in range(z.bands):
         value = jnp.zeros((z.ext, lanes), f32)
@@ -132,21 +137,17 @@
         table_ref[band] = chosen.astype(bf16)
 
 
-def fill_order(z, order_ref, rows, body_at, tail_at, scale_at):
+def fill_order(z, order_ref):
     row = iota((GROUP * z.message, 1), 0)
     member = row // z.message
     place = row % z.message
-    per = rows + 8
-    body = place - body_at
+    per = z.rows + 8
+    body = place - z.signal_at
     source = (body // z.own) * per + member + GROUP * (body % z.own)
-    source = jnp.where((body >= 0) & (body < z.tiles * z.own), source, -1)
-    if tail_at is not None:
-        tail = place - tail_at
-        found = (tail // z.own_tail) * per + z.rows + member
-        found = found + GROUP * (tail % z.own_tail)
-        source = jnp.where((tail >= 0) & (tail < z.tiles * z.own_tail), found, source)
-    scale = place - scale_at
-    source = jnp.where((scale >= 0) & (scale < z.tiles), scale * per + rows, source)
+    source = jnp.where((body >= 0) & (body < z.signal_at), source, -1)
+    scale = place - z.signal_scale_at
+    found = scale * per + z.rows
+    source = jnp.where((scale >= 0) & (scale < z.tiles), found, source)
     column = iota((GROUP * z.message, z.tiles * per), 1)
     order_ref[...] = (column == source).astype(f32).astype(bf16)
 
@@ -171,9 +172,9 @@
 
 
 def first_kernel(
-    z, offsets_hbm, gains_hbm, owners_hbm, x_hbm, w_hbm, signal_hbm,
-    table_ref, order_ref, base_ref, along_ref, place_ref, total_ref, rest_ref,
-    offsets_ref, gains_ref, owners_ref, x_ref, w_ref, signal_ref, signal_order_ref, sems,
+    z, offsets_hbm, gains_hbm, owners_hbm, x_hbm, w_hbm, signal_hbm, orders_hbm,
+    table_ref, base_ref, along_ref, place_ref, total_ref, rest_ref, orders_ref,
+    offsets_ref, gains_ref, owners_ref, x_ref, w_ref, signal_ref, order_ref, sems,
 ):
     me = lax.axis_index("subj")
 
@@ -189,6 +190,7 @@
         (weight_rows(0), w_ref),
         (owners_hbm, owners_ref),
         (signal_hbm, signal_ref),
+        (orders_hbm, orders_ref),
     ]
     for step in range(1, z.subjects):
         rows = pl.ds((step - 1) * z.width, z.width)
@@ -199,23 +201,22 @@
     ]
     for copy in copies:
         copy.start()
+    fill_order(z, order_ref)
     copies[0].wait()
     copies[1].wait()
     fill_table(z, offsets_ref, gains_ref, table_ref)
     copies[2].wait()
     copies[3].wait()
     total_ref[...] = filtered_product(z, x_ref, w_ref, table_ref, me)
-    fill_order(z, order_ref, z.ext, 0, z.tail_at, z.scale_at)
-    fill_order(z, signal_order_ref, z.rows, z.signal_at, None, z.signal_scale_at)
     copies[4].wait()
     fill_owners(z, owners_ref, along_ref, place_ref)
     copies[5].wait()
-    base_ref[...] = arranged(z, signal_ref[...].astype(f32), signal_order_ref[...])
+    base_ref[...] = signal_messages(z, signal_ref[...].astype(f32), order_ref[...])
     for copy in copies[6:]:
         copy.wait()
 
 
-def second_kernel(z, table_ref, w_ref, total_ref, order_ref, base_ref, *refs):
+def second_kernel(z, table_ref, w_ref, total_ref, base_ref, *refs):
     others, out_ref = refs[:-1], refs[-1]
     me = lax.axis_index("subj")
     total = total_ref[...]
@@ -223,16 +224,36 @@
         source = lax.rem(me + step + 1, z.subjects)
         rows = w_ref.at[step * z.width : (step + 1) * z.width, :]
         total = total + filtered_product(z, x_ref, rows, table_ref, source)
-    messages = arranged(z, total, order_ref[...]) + base_ref[...]
+    value, power = coded(total)
+    row = iota((8, LANES), 0)
     for member in range(GROUP):
-        message = messages[member * z.message : (member + 1) * z.message]
-        message = message.astype(i32).astype(jnp.int16)
+        start = member * z.message
+        body, ends = [], []
+        for at in range(z.tail_at, z.message, 8):
+            ends.append(base_ref[start + at : start + at + 8, :])
+        for tile in range(z.tiles):
+            lanes = slice(tile * LANES, (tile + 1) * LANES)
+            body.append(value[member * z.own : (member + 1) * z.own, lanes])
+            which, place = divmod(tile * z.own_tail, 8)
+            shift = (place - member * z.own_tail) % 8
+            tail = pltpu.roll(value[z.rows :, lanes], shift, 0)
+            here = (row >= place) & (row < place + z.own_tail)
+            ends[which] = jnp.where(here, tail, ends[which])
+            which, place = divmod(z.scale_at - z.tail_at + tile, 8)
+            ends[which] = jnp.where(row == place, power[:, lanes], ends[which])
+        body.append(base_ref[start + z.signal_at : start + z.tail_at, :])
+        message = jnp.concatenate(body + ends, axis=0).astype(i32).astype(jnp.int16)
         for index in range(member, z.n, GROUP):
             out_ref[index] = message
 
 
-def third_kernel(z, orders_ref, along_ref, place_ref, received_ref, *refs):
-    out_refs, (block_ref, tail_ref, signal_ref) = refs[:GROUP], refs[GROUP:]
+def third_kernel(z, orders_in_ref, along_ref, place_ref, received_ref, *refs):
+    out_refs, (block_ref, tail_ref, signal_ref, orders_ref, sem) = (
+        refs[:GROUP],
+        refs[GROUP:],
+    )
+    copy = pltpu.make_async_copy(orders_in_ref, orders_ref, sem)
+    copy.start()
     me = lax.axis_index("tr")
     row = iota((8, LANES), 0)
 
@@ -258,6 +279,7 @@
     if z.n > 16:
         lax.fori_loop(0, z.n, unpack, 0)
     tail_ref[z.n] = jnp.zeros((z.tiles * 8, LANES), f32)
+    copy.wait()
 
     def folded(x):
         return [
@@ -268,8 +290,7 @@
             for tile in range(z.tiles)
         ]
 
-    def squares(position, condition):
-        signal = signal_ref[position]
+    def squares(signal, position, condition):
         if condition == z.conditions:
             return signal * signal
         if condition == 0:
@@ -290,8 +311,9 @@
 
     def add_position(position, sums):
         added = []
+        signal = signal_ref[position]
         for condition in range(z.conditions + 1):
-            parts = folded(squares(position, condition))
+            parts = folded(squares(signal, position, condition))
             old = sums[condition * z.tiles : (condition + 1) * z.tiles]
             added += [o + p for o, p in zip(old, parts)]
         return tuple(added)
@@ -324,8 +346,10 @@
     lanes = iota((z.own, LANES), 1)
     for step, out_ref in enumerate(out_refs):
         energy = jnp.zeros((z.own, LANES), f32)
+        position = jnp.bitwise_xor(me, step)
+        signal = signal_ref[position]
         for condition in range(z.conditions):
-            value = squares(jnp.bitwise_xor(me, step), condition)
+            value = squares(signal, position, condition)
             value = sum(
                 value[tile * z.own : (tile + 1) * z.own] for tile in range(z.tiles)
             )
@@ -378,12 +402,12 @@
     messages = GROUP * z.message
     shapes = [
         jax.ShapeDtypeStruct((z.bands, z.ext, term_lanes), bf16),
-        jax.ShapeDtypeStruct((messages, z.tiles * (z.ext + 8)), bf16),
         jax.ShapeDtypeStruct((messages, LANES), f32),
         jax.ShapeDtypeStruct((8, z.voxels), i32),
         jax.ShapeDtypeStruct((z.voxels, LANES), bf16),
         jax.ShapeDtypeStruct((z.ext, z.voxels), f32),
         jax.ShapeDtypeStruct((z.columns - z.width, z.voxels), bf16),
+        jax.ShapeDtypeStruct(block_orders.shape, i32),
     ]
     scratch = [
         pltpu.SMEM(offsets.shape, i32),
@@ -393,14 +417,14 @@
         pltpu.VMEM((z.width, z.voxels), bf16),
         pltpu.VMEM((z.rows, z.voxels), bf16),
         pltpu.VMEM((messages, z.tiles * (z.rows + 8)), bf16),
-        pltpu.SemaphoreType.DMA((5 + z.subjects,)),
-    ]
-    operands = (offsets, tap_gains, owners, features, weights[0], signal[0])
+        pltpu.SemaphoreType.DMA((6 + z.subjects,)),
+    ]
+    operands = (offsets, tap_gains, owners, features, weights[0], signal[0], block_orders)
     operands = [pltpu.with_memory_space_constraint(x, pltpu.HBM) for x in operands]
-    table, order, base, along, place, total, rest = pl.pallas_call(
+    table, base, along, place, total, rest, orders = pl.pallas_call(
         functools.partial(first_kernel, z),
         out_shape=shapes,
-        in_specs=[HBM] * 6,
+        in_specs=[HBM] * 7,
         out_specs=[VMEM] * 7,
         scratch_shapes=scratch,
         compiler_params=params(),
@@ -410,24 +434,25 @@
     outgoing = pl.pallas_call(
         functools.partial(second_kernel, z),
         out_shape=jax.ShapeDtypeStruct((z.n, z.message, LANES), jnp.int16),
-        in_specs=[VMEM] * (5 + len(others)),
+        in_specs=[VMEM] * (4 + len(others)),
         out_specs=VMEM,
         compiler_params=params(),
         cost_estimate=cost(work, 2 << 20),
         name="other_columns",
-    )(table, rest, total, order, base, *others)
+    )(table, rest, total, base, *others)
     received = lax.all_to_all(outgoing, "tr", 0, 0, tiled=True)
-    orders = pltpu.with_memory_space_constraint(block_orders, pltpu.SMEM)
     part = jax.ShapeDtypeStruct((z.own + 8, LANES), f32)
     parts = pl.pallas_call(
         functools.partial(third_kernel, z),
         out_shape=[part] * GROUP,
-        in_specs=[SMEM, VMEM, VMEM, VMEM],
+        in_specs=[VMEM] * 4,
         out_specs=[VMEM] * GROUP,
         scratch_shapes=[
             pltpu.VMEM((z.n, z.tiles * z.own, LANES), f32),
             pltpu.VMEM((z.n + 1, z.tiles * 8, LANES), f32),
             pltpu.VMEM((z.n, z.tiles * z.own, LANES), f32),
+            pltpu.SMEM(block_orders.shape, i32),
+            pltpu.SemaphoreType.DMA,
         ],
         compiler_params=params(),
         cost_estimate=cost(work, 1 << 20),

time: 31.3 us -> 30.4 us (0.971)
  Pallas kernels: 5.52 us -> 4.41 us
  waiting for transfers between devices: 2.76 us -> 3.59 us
  local copies, waits for them, and re-layouts: 0.68 us -> 0 us
    pallas_call x1, Pallas kernels: 2.98 us -> 2.14 us  [on_device(): pl.pallas_call(functools.partial(first_kernel, z), out_shape=shapes, in_s...]
    ppermute x1, waiting for transfers between devices: 0.72 us -> 1.55 us  [on_device(): lax.ppermute(features, 'subj', [((i + step) % z.subjects, i) for i in ran...]
    unnamed x2 -> x0, local copies, waits for them, and re-layouts: 0.68 us -> none
  transfers between devices with their start and end apart: 4 -> 4, of which waited for: 2 -> 2; matrix products, arithmetic and copies ran while one was open for 0% -> 0% of each run, Pallas kernels for 10% -> 7%
where the time goes in v5:
time: 30.4 us; the launch traced here: 30.2 us
  blocking collectives  16.6 us (55%)
  starting transfers between devices  4.94 us (16%)
  Pallas kernels  4.41 us (15%)
  waiting for transfers between devices  3.59 us (12%)
  between operations  0.67 us (2%)
    all_to_all x1, blocking collectives, on_device(): received = lax.all_to_all(outgoing, 'tr', 0, 0, tiled=True)  16.6 us
    ppermute x1, starting transfers between devices, on_device(): lax.ppermute(features, 'subj', [((i + step) % z.subjects, i) for i in ran...  3 us
    pallas_call x1, Pallas kernels, on_device(): pl.pallas_call(functools.partial(first_kernel, z), out_shape=shapes, in_s...  2.14 us
    ppermute x3, waiting for transfers between devices, on_device(): lax.ppermute(parts[step], 'tr', [(i, i ^ step) for i in range(z.n)])  2.04 us
    ppermute x3, starting transfers between devices, on_device(): lax.ppermute(parts[step], 'tr', [(i, i ^ step) for i in range(z.n)])  1.93 us
    ppermute x1, waiting for transfers between devices, on_device(): lax.ppermute(features, 'subj', [((i + step) % z.subjects, i) for i in ran...  1.55 us
    pallas_call x1, Pallas kernels, on_device(): pl.pallas_call(functools.partial(third_kernel, z), out_shape=[part] * GRO...  1.03 us
    pallas_call x1, Pallas kernels, on_device(): pl.pallas_call(functools.partial(fourth_kernel, z), out_shape=[jax.ShapeD...  0.77 us
  transfers between devices with their start and end apart: 4, of which 2 were waited for; matrix products, arithmetic and copies ran while one was open for 0% of the time, Pallas kernels for 7%

profile of v5, /device:TPU:0, one launch (start us, length us, event | category | flops | bytes accessed | tf_op | source)
XLA Modules:
  0.0 30.2 jit_solution(480333564853686050)
XLA Ops:
  0.6 3.0 %collective-permute-start = (bf16[64,1024]{1,0:T(8,128)(2,1)}, bf16[64,1024]{1,0:T(8,128)(2,1)S(1)}, u32[]{:S(2)}, u32[]{:S(2)}) collective-permute-start(bf16[64,1024]{1,0:T(8,128)(2,1)} %x_hbm.1), channel_id=1, source_target_pairs={{16,0},{0,16},{17,1},{1,17},{18,2},{2,18},{19,3},{3,19},{20,4},{4,... | collective-permute-start | bytes 393224 | tf_op jit(solution)/shard_map/ppermute | solution.py:393
  3.6 2.1 %prepare_and_own_columns.1 = (bf16[4,72,256]{2,1,0:T(8,128)(2,1)S(1)}, f32[288,128]{1,0:T(8,128)S(1)}, s32[8,256]{1,0:T(8,128)S(1)}, bf16[256,128]{1,0:T(8,128)(...) custom-call(s32[4,4]{1,0:T(4,128)} %offsets_hbm.1, f32[4,4]{1,0:T(4,128)} %gains_hbm.1, ...), custom_call_target="tpu_custom_call" | custom-call | flops 37748736 | bytes 3145728 | tf_op jit(solution)/shard_map/prepare_and_own_columns/pallas_call | solution.py:424
  5.8 1.6 %collective-permute-done.refs_0_ = bf16[64,1024]{1,0:T(8,128)(2,1)S(1)} collective-permute-done((bf16[64,1024]{1,0:T(8,128)(2,1)}, bf16[64,1024]{1,0:T(8,128)(2,1)S(1)}, u32[]{:S(2)}, u32[]{:S(2)}) %collective-permute-start) | collective-permute-done | bytes 131104 | tf_op jit(solution)/shard_map/ppermute | solution.py:393
  7.3 0.5 %other_columns.1 = s16[16,72,128]{2,1,0:T(8,128)(2,1)S(1)} custom-call(bf16[4,72,256]{2,1,0:T(8,128)(2,1)S(1)} %get-tuple-element.18.table_ref, bf16[1024,256]{1,0:T(8,128)(2,1)S(1)} %get-tuple-element.19.w_ref, f32[72,256]{1,0:T(8,128)S(1)} %get-tuple-element.20.total_ref, f32[288,128]{1,0:T(8,128)S(1)} %get-tuple-element.21.base_ref, ...), custom_call_target="tpu_custom_call" | custom-call | flops 37748736 | bytes 2097152 | tf_op jit(solution)/shard_map/other_columns/pallas_call | solution.py:434
  7.8 16.6 %all_to_all.5.received_ref = s16[16,72,128]{2,1,0:T(8,128)(2,1)S(1)} all-to-all(s16[16,72,128]{2,1,0:T(8,128)(2,1)S(1)} %other_columns.1), channel_id=1, replica_groups=mesh['subj'=2,'tr'=16] {'tr'}, dimensions={0} | all-to-all | bytes 589824 | tf_op jit(solution)/shard_map/all_to_all | solution.py:443
  24.4 1.0 %residuals.1 = (f32[24,128]{1,0:T(8,128)S(1)}, f32[24,128]{1,0:T(8,128)S(1)}, f32[24,128]{1,0:T(8,128)S(1)}, f32[24,128]{1,0:T(8,128)S(1)}) custom-call(s32[4,16]{1,0:T(4,128)S(1)} %get-tuple-element.15.orders_in_ref, s32[8,256]{1,0:T(8,128)S(1)} %get-tuple-element.16.along_ref, bf16[256,128]{1,0:T(8,128)(2,1)S(1)} %get-tuple-element.17.place_ref, ...), custom_call_target="tpu_custom_call" | custom-call | flops 37748736 | bytes 1048576 | tf_op jit(solution)/shard_map/residuals/pallas_call | solution.py:445
  25.4 0.1 collective-permute-start.1
  25.5 0.7 %collective-permute-start.2 = (f32[24,128]{1,0:T(8,128)S(1)}, f32[24,128]{1,0:T(8,128)S(1)}, u32[]{:S(2)}, u32[]{:S(2)}) collective-permute-start(f32[24,128]{1,0:T(8,128)S(1)} %get-tuple-element.24), channel_id=1, source_target_pairs={{0,2},{1,3},{2,0},{3,1},{4,6},{5,7},{6,4},{7,5},{8,10},{9,11},{10,... | collective-permute-start | bytes 36872 | tf_op jit(solution)/shard_map/ppermute | solution.py:462
  26.1 1.2 %collective-permute-start.3 = (f32[24,128]{1,0:T(8,128)S(1)}, f32[24,128]{1,0:T(8,128)S(1)}, u32[]{:S(2)}, u32[]{:S(2)}) collective-permute-start(f32[24,128]{1,0:T(8,128)S(1)} %get-tuple-element.25), channel_id=1, source_target_pairs={{0,3},{1,2},{2,1},{3,0},{4,7},{5,6},{6,5},{7,4},{8,11},{9,10},{10,... | collective-permute-start | bytes 36872 | tf_op jit(solution)/shard_map/ppermute | solution.py:462
  27.4 0.0 collective-permute-done.1.refs_1_
  27.4 2.0 %collective-permute-done.2.refs_2_ = f32[24,128]{1,0:T(8,128)S(1)} collective-permute-done((f32[24,128]{1,0:T(8,128)S(1)}, f32[24,128]{1,0:T(8,128)S(1)}, u32[]{:S(2)}, u32[]{:S(2)}) %collective-permute-start.2) | collective-permute-done | bytes 12320 | tf_op jit(solution)/shard_map/ppermute | solution.py:462
  29.4 0.0 collective-permute-done.3.refs_3_
  29.4 0.8 %scores.1 = (f32[5,1,64]{2,1,0:T(1,128)}, f32[5,1,8]{2,1,0:T(1,128)}) custom-call(f32[24,128]{1,0:T(8,128)S(1)} %get-tuple-element.22.refs_0_, f32[24,128]{1,0:T(8,128)S(1)} %collective-permute-done.1.refs_1_, f32[24,128]{1,0:T(8,128)S(1)} %collective-permute-done.2.refs_2_, f32[24,128]{1,0:T(8,128)S(1)} %collective-permute-done.3.refs_3_), custom_call_target="tpu_custom_call" | custom-call | flops 1048576 | bytes 65536 | tf_op jit(solution)/shard_map/scores/pallas_call | solution.py:465
Async XLA Ops:
  0.6 6.7 %collective-permute-start = (bf16[64,1024]{1,0:T(8,128)(2,1)}, bf16[64,1024]{1,0:T(8,128)(2,1)S(1)}, u32[]{:S(2)}, u32[]{:S(2)}) collective-permute-start(bf16[64,1024]{1,0:T(8,128)(2,1)} %x_hbm.1), channel_id=1, source_target_pairs={{16,0},{0,16},{17,1},{1,17},{18,2},{2,18},{19,3},{3,19},{20,4},{4,... | collective-permute-start | bytes 393224 | tf_op jit(solution)/shard_map/ppermute | solution.py:393
  25.4 1.9 %collective-permute-start.1 = (f32[24,128]{1,0:T(8,128)S(1)}, f32[24,128]{1,0:T(8,128)S(1)}, u32[]{:S(2)}, u32[]{:S(2)}) collective-permute-start(f32[24,128]{1,0:T(8,128)S(1)} %get-tuple-element.23), channel_id=1, source_target_pairs={{0,1},{1,0},{2,3},{3,2},{4,5},{5,4},{6,7},{7,6},{8,9},{9,8},{10,11... | collective-permute-start | bytes 36872 | tf_op jit(solution)/shard_map/ppermute | solution.py:462
  25.5 3.9 %collective-permute-start.2 = (f32[24,128]{1,0:T(8,128)S(1)}, f32[24,128]{1,0:T(8,128)S(1)}, u32[]{:S(2)}, u32[]{:S(2)}) collective-permute-start(f32[24,128]{1,0:T(8,128)S(1)} %get-tuple-element.24), channel_id=1, source_target_pairs={{0,2},{1,3},{2,0},{3,1},{4,6},{5,7},{6,4},{7,5},{8,10},{9,11},{10,... | collective-permute-start | bytes 36872 | tf_op jit(solution)/shard_map/ppermute | solution.py:462
  26.1 3.3 %collective-permute-start.3 = (f32[24,128]{1,0:T(8,128)S(1)}, f32[24,128]{1,0:T(8,128)S(1)}, u32[]{:S(2)}, u32[]{:S(2)}) collective-permute-start(f32[24,128]{1,0:T(8,128)S(1)} %get-tuple-element.25), channel_id=1, source_target_pairs={{0,3},{1,2},{2,1},{3,0},{4,7},{5,6},{6,5},{7,4},{8,11},{9,10},{10,... | collective-permute-start | bytes 36872 | tf_op jit(solution)/shard_map/ppermute | solution.py:462

commit v6 on v5

--- a/solution.py
+++ b/solution.py
@@ -152,28 +152,21 @@
     order_ref[...] = (column == source).astype(f32).astype(bf16)
 
 
-def fill_owners(z, owners_ref, along_ref, place_ref):
+def fill_owners(z, owners_ref, mean_ref):
     owners = owners_ref[...]
     other = iota((z.voxels, z.blocks), 1)
     block = iota((z.voxels, 1), 0) // VB
     owner = jnp.sum(jnp.where(other == block, owners, 0), axis=1, keepdims=True)
     before = (owners == owner) & (other < block)
     rank = jnp.sum(before.astype(i32), axis=1, keepdims=True)
-    lane = rank * VB + iota((z.voxels, 1), 0) % VB
-    place = iota((z.voxels, LANES), 1) == lane
-    place_ref[...] = place.astype(f32).astype(bf16)
-    square = (z.blocks, z.blocks)
-    diagonal = iota(square, 0) == iota(square, 1)
-    down = jnp.sum(jnp.where(diagonal, owners, 0), axis=1, keepdims=True)
-    shape = (z.blocks, z.voxels)
-    held = iota(shape, 0) == iota(shape, 1) // VB
-    along = jnp.sum(jnp.where(held, down, 0), axis=0, keepdims=True)
-    along_ref[...] = jnp.broadcast_to(along, (8, z.voxels))
+    rank = jnp.where(owner == lax.axis_index("tr"), rank, -1)
+    mean = jnp.where(iota((z.voxels, LANES), 1) == rank, 1.0 / VB, 0.0)
+    mean_ref[...] = mean.astype(bf16)
 
 
 def first_kernel(
     z, offsets_hbm, gains_hbm, owners_hbm, x_hbm, w_hbm, signal_hbm, orders_hbm,
-    table_ref, base_ref, along_ref, place_ref, total_ref, rest_ref, orders_ref,
+    table_ref, base_ref, mean_ref, total_ref, rest_ref, orders_ref,
     offsets_ref, gains_ref, owners_ref, x_ref, w_ref, signal_ref, order_ref, sems,
 ):
     me = lax.axis_index("subj")
@@ -209,7 +202,7 @@
     copies[3].wait()
     total_ref[...] = filtered_product(z, x_ref, w_ref, table_ref, me)
     copies[4].wait()
-    fill_owners(z, owners_ref, along_ref, place_ref)
+    fill_owners(z, owners_ref, mean_ref)
     copies[5].wait()
     base_ref[...] = signal_messages(z, signal_ref[...].astype(f32), order_ref[...])
     for copy in copies[6:]:
@@ -247,85 +240,98 @@
             out_ref[index] = message
 
 
-def third_kernel(z, orders_in_ref, along_ref, place_ref, received_ref, *refs):
-    out_refs, (block_ref, tail_ref, signal_ref, orders_ref, sem) = (
-        refs[:GROUP],
-        refs[GROUP:],
-    )
-    copy = pltpu.make_async_copy(orders_in_ref, orders_ref, sem)
-    copy.start()
+def third_kernel(z, orders_in_ref, received_ref, *refs):
+    out_refs, (block_ref, tail_ref, *more) = refs[:GROUP], refs[GROUP:]
+    orders = orders_in_ref[...]
+    if more:
+        orders_ref, sem = more
+        copy = pltpu.make_async_copy(orders_in_ref, orders_ref, sem)
+        copy.start()
     me = lax.axis_index("tr")
     row = iota((8, LANES), 0)
 
-    def unpack(index, _):
-        x = received_ref[index].astype(i32).astype(f32)
-        scales = jnp.exp2(x[z.scale_at : z.scale_at + 2 * z.tiles] - 15.0)
-        for tile in range(z.tiles):
-            scale = scales[tile : tile + 1]
-            own = slice(tile * z.own, (tile + 1) * z.own)
-            block_ref[index, own, :] = x[own] * scale
-            at = z.tail_at + tile * z.own_tail
-            start = at // 8 * 8
-            tail = pltpu.roll(x[start : start + 8], (8 - at % 8) % 8, 0)
-            tail = jnp.where(row < z.own_tail, tail * scale, 0.0)
-            tail_ref[index, tile * 8 : (tile + 1) * 8, :] = tail
-            scale = scales[z.tiles + tile : z.tiles + tile + 1]
-            values = x[z.signal_at + tile * z.own : z.signal_at + (tile + 1) * z.own]
-            signal_ref[index, own, :] = values * scale
-        return 0
-
-    for index in range(z.n) if z.n <= 16 else ():
-        unpack(index, 0)
-    if z.n > 16:
-        lax.fori_loop(0, z.n, unpack, 0)
-    tail_ref[z.n] = jnp.zeros((z.tiles * 8, LANES), f32)
-    copy.wait()
-
-    def folded(x):
-        return [
-            sum(
-                x[tile * z.own + start : tile * z.own + start + 8]
-                for start in range(0, z.own, 8)
-            )
+    def numbers(index, start, stop):
+        return received_ref[index, start:stop, :].astype(i32).astype(f32)
+
+    def scales(index, start):
+        at = start // 8 * 8
+        stop = -(-(start + z.tiles) // 8) * 8
+        power = numbers(index, at, stop)[start - at : start - at + z.tiles]
+        return jnp.exp2(power - 15.0)
+
+    def scaled(x, scale):
+        parts = [
+            x[tile * z.own : (tile + 1) * z.own] * scale[tile : tile + 1]
             for tile in range(z.tiles)
         ]
-
-    def squares(signal, position, condition):
-        if condition == z.conditions:
-            return signal * signal
-        if condition == 0:
-            here, ahead = position, position - 1
-        else:
-            here = orders_ref[condition - 1, position]
-            ahead = orders_ref[condition - 1, jnp.maximum(position - 1, 0)]
-        ahead = jnp.where(position == 0, z.n, ahead)
+        return jnp.concatenate(parts, axis=0)
+
+    def unpack(index, carry):
+        scale = scales(index, z.scale_at)
+        block_ref[index] = scaled(numbers(index, 0, z.signal_at), scale)
+        end = -(-z.scale_at // 8) * 8
+        tails = numbers(index, z.tail_at, end)
+        for tile in range(z.tiles):
+            which, place = divmod(tile * z.own_tail, 8)
+            tail = pltpu.roll(tails[which * 8 : which * 8 + 8], (8 - place) % 8, 0)
+            tail = jnp.where(row < z.own_tail, tail * scale[tile : tile + 1], 0.0)
+            tail_ref[index, tile * 8 : (tile + 1) * 8, :] = tail
+        return carry
+
+    def signal_of(position):
+        x = numbers(position, z.signal_at, z.tail_at)
+        return scaled(x, scales(position, z.signal_scale_at))
+
+    def squares(signal, here, ahead):
         residual = signal - block_ref[here]
-        tail = tail_ref[ahead]
         parts = []
         for tile in range(z.tiles):
             start = tile * z.own
-            head = residual[start : start + 8] - tail[tile * 8 : (tile + 1) * 8]
-            parts += [head, residual[start + 8 : start + z.own]]
+            tail = tail_ref[ahead, tile * 8 : (tile + 1) * 8, :]
+            parts.append(residual[start : start + 8] - tail)
+            parts.append(residual[start + 8 : start + z.own])
         residual = jnp.concatenate(parts, axis=0)
         return residual * residual
 
     def add_position(position, sums):
         added = []
-        signal = signal_ref[position]
+        signal = signal_of(position)
+        first = position == 0
+        before = jnp.maximum(position - 1, 0)
         for condition in range(z.conditions + 1):
-            parts = folded(squares(signal, position, condition))
-            old = sums[condition * z.tiles : (condition + 1) * z.tiles]
-            added += [o + p for o, p in zip(old, parts)]
+            if condition == z.conditions:
+                value = signal * signal
+            else:
+                if condition == 0:
+                    here, ahead = position, before
+                elif more:
+                    here = orders_ref[condition - 1, position]
+                    ahead = orders_ref[condition - 1, before]
+                else:
+                    here = orders[condition - 1, position]
+                    ahead = orders[condition - 1, max(position - 1, 0)]
+                value = squares(signal, here, jnp.where(first, z.n, ahead))
+            for tile in range(z.tiles):
+                total = sums[condition * z.tiles + tile]
+                for start in range(tile * z.own, (tile + 1) * z.own, 8):
+                    total = total + value[start : start + 8]
+                added.append(total)
         return tuple(added)
 
-    def add_positions(step, sums):
-        for index in range(GROUP):
-            sums = add_position(step * GROUP + index, sums)
-        return sums
-
+    def loop(body, carry):
+        if more:
+            return lax.fori_loop(0, z.n, body, carry)
+        for index in range(z.n):
+            carry = body(index, carry)
+        return carry
+
+    loop(unpack, 0)
+    tail_ref[z.n] = jnp.zeros((z.tiles * 8, LANES), f32)
+    if more:
+        copy.wait()
     zero = jnp.zeros((8, LANES), f32)
     sums = tuple(zero for _ in range((z.conditions + 1) * z.tiles))
-    sums = lax.fori_loop(0, z.n // GROUP, add_positions, sums)
+    sums = loop(add_position, sums)
     stats = []
     for tile in range(z.tiles):
         value = zero
@@ -333,34 +339,42 @@
             stat = jnp.sum(sums[condition * z.tiles + tile], axis=0, keepdims=True)
             value = jnp.where(row == condition, stat, value)
         stats.append(value)
-    stats = jnp.concatenate(stats, axis=1)
-    masked = [
-        jnp.where(along_ref[...] == jnp.bitwise_xor(me, step), stats, 0.0)
-        for step in range(GROUP)
-    ]
-    terms = jnp.concatenate(
-        [t.astype(f32) for t in thirds(jnp.concatenate(masked, axis=0))], axis=0
-    )
-    placed = dot(terms.astype(bf16), place_ref[...])
-    placed = placed[: GROUP * 8] + placed[GROUP * 8 : GROUP * 16] + placed[GROUP * 16 :]
+    stats = jnp.concatenate(stats, axis=0)
     lanes = iota((z.own, LANES), 1)
+    place = iota(orders.shape, 1)
     for step, out_ref in enumerate(out_refs):
         energy = jnp.zeros((z.own, LANES), f32)
         position = jnp.bitwise_xor(me, step)
-        signal = signal_ref[position]
+        signal = signal_of(position)
+        own = jnp.where(place == position, orders, 0)
+        own = jnp.sum(own, axis=1, keepdims=True)
+        before = jnp.where(place == position - 1, orders, 0)
+        before = jnp.sum(before, axis=1, keepdims=True)
         for condition in range(z.conditions):
-            value = squares(signal, position, condition)
+            if condition == 0:
+                here, ahead = position, position - 1
+            else:
+                here, ahead = own[condition - 1, 0], before[condition - 1, 0]
+            value = squares(signal, here, jnp.where(position == 0, z.n, ahead))
             value = sum(
                 value[tile * z.own : (tile + 1) * z.own] for tile in range(z.tiles)
             )
             value = jnp.sum(value, axis=1, keepdims=True) * (1.0 / z.voxels)
             energy = jnp.where(lanes == condition, value, energy)
         out_ref[: z.own, :] = energy
-        out_ref[z.own :, :] = placed[step * 8 : (step + 1) * 8]
-
-
-def fourth_kernel(z, *refs):
+        out_ref[z.own :, :] = stats
+
+
+def fourth_kernel(z, mean_ref, *refs):
     parts, (energy_ref, scores_ref) = refs[:GROUP], refs[GROUP:]
+    sums = sum(p[z.own :, :] for p in parts)
+    tiles = [sums[start : start + 8] for start in range(0, z.tiles * 8, 8)]
+    fit = [
+        jnp.log((x + EPSILON) / (x[z.conditions : z.conditions + 1] + EPSILON))
+        for x in tiles
+    ]
+    terms = [t.astype(f32) for t in thirds(jnp.concatenate(fit, axis=1))]
+    score = dot(jnp.concatenate(terms, axis=0).astype(bf16), mean_ref[...])
     member = lax.rem(lax.axis_index("tr"), GROUP)
     turned = jnp.transpose(jnp.concatenate([p[: z.own, :] for p in parts], axis=0))
     column = iota((z.rows, LANES), 0)
@@ -370,16 +384,6 @@
     terms = [t.astype(f32) for t in thirds(turned[:8, : z.rows])]
     energy = dot(jnp.concatenate(terms, axis=0).astype(bf16), order)
     energy = energy[:8] + energy[8:16] + energy[16:]
-    sums = sum(p[z.own :, :] for p in parts)
-    lanes = iota((8, LANES), 1)
-    sums = jnp.where(lanes < CAP * VB, sums, 0.0)
-    signal = sums[z.conditions : z.conditions + 1]
-    square = (LANES, LANES)
-    mean = iota(square, 0) // VB == iota(square, 1)
-    mean = jnp.where(mean & (iota(square, 1) < CAP), 1.0 / VB, 0.0).astype(bf16)
-    fit = jnp.log((sums + EPSILON) / (signal + EPSILON))
-    terms = jnp.concatenate([t.astype(f32) for t in thirds(fit)], axis=0).astype(bf16)
-    score = dot(terms, mean)
     score = score[:8] + score[8:16] + score[16:]
     for index in range(z.conditions):
         energy_ref[index] = energy[index : index + 1, : z.rows]
@@ -403,7 +407,6 @@
     shapes = [
         jax.ShapeDtypeStruct((z.bands, z.ext, term_lanes), bf16),
         jax.ShapeDtypeStruct((messages, LANES), f32),
-        jax.ShapeDtypeStruct((8, z.voxels), i32),
         jax.ShapeDtypeStruct((z.voxels, LANES), bf16),
         jax.ShapeDtypeStruct((z.ext, z.voxels), f32),
         jax.ShapeDtypeStruct((z.columns - z.width, z.voxels), bf16),
@@ -421,11 +424,11 @@
     ]
     operands = (offsets, tap_gains, owners, features, weights[0], signal[0], block_orders)
     operands = [pltpu.with_memory_space_constraint(x, pltpu.HBM) for x in operands]
-    table, base, along, place, total, rest, orders = pl.pallas_call(
+    table, base, mean, total, rest, orders = pl.pallas_call(
         functools.partial(first_kernel, z),
         out_shape=shapes,
         in_specs=[HBM] * 7,
-        out_specs=[VMEM] * 7,
+        out_specs=[VMEM] * 6,
         scratch_shapes=scratch,
         compiler_params=params(),
         cost_estimate=cost(work, 3 << 20),
@@ -441,23 +444,23 @@
         name="other_columns",
     )(table, rest, total, base, *others)
     received = lax.all_to_all(outgoing, "tr", 0, 0, tiled=True)
-    part = jax.ShapeDtypeStruct((z.own + 8, LANES), f32)
+    more = [pltpu.SMEM(block_orders.shape, i32), pltpu.SemaphoreType.DMA]
+    more = more if z.n > 16 else []
+    part = jax.ShapeDtypeStruct((z.own + z.tiles * 8, LANES), f32)
     parts = pl.pallas_call(
         functools.partial(third_kernel, z),
         out_shape=[part] * GROUP,
-        in_specs=[VMEM] * 4,
+        in_specs=[VMEM] * 2,
         out_specs=[VMEM] * GROUP,
         scratch_shapes=[
             pltpu.VMEM((z.n, z.tiles * z.own, LANES), f32),
             pltpu.VMEM((z.n + 1, z.tiles * 8, LANES), f32),
-            pltpu.VMEM((z.n, z.tiles * z.own, LANES), f32),
-            pltpu.SMEM(block_orders.shape, i32),
-            pltpu.SemaphoreType.DMA,
+            *more,
         ],
         compiler_params=params(),
         cost_estimate=cost(work, 1 << 20),
         name="residuals",
-    )(orders, along, place, received)
+    )(orders, received)
     parts = [parts[0]] + [
         lax.ppermute(parts[step], "tr", [(i, i ^ step) for i in range(z.n)])
         for step in range(1, GROUP)
@@ -468,12 +471,12 @@
             jax.ShapeDtypeStruct((z.conditions, 1, z.rows), f32),
             jax.ShapeDtypeStruct((z.conditions, 1, CAP), f32),
         ],
-        in_specs=[VMEM] * GROUP,
+        in_specs=[VMEM] * (1 + GROUP),
         out_specs=[VMEM, VMEM],
         compiler_params=params(),
         cost_estimate=cost(1 << 20, 1 << 16),
         name="scores",
-    )(*parts)
+    )(mean, *parts)
     return energy.transpose(1, 2, 0), scores.transpose(1, 2, 0)
 
 

time: 30.4 us -> 29.8 us (0.980)
  Pallas kernels: 4.41 us -> 3.76 us
    pallas_call x1, Pallas kernels: 1.03 us -> 0.38 us  [on_device(): pl.pallas_call(functools.partial(third_kernel, z), out_shape=[part] * GRO...]
where the time goes in v6:
time: 29.8 us; the launch traced here: 29.6 us
  blocking collectives  16.6 us (56%)
  starting transfers between devices  4.94 us (17%)
  Pallas kernels  3.76 us (13%)
  waiting for transfers between devices  3.68 us (12%)
  between operations  0.66 us (2%)
    all_to_all x1, blocking collectives, on_device(): received = lax.all_to_all(outgoing, 'tr', 0, 0, tiled=True)  16.6 us
    ppermute x1, starting transfers between devices, on_device(): lax.ppermute(features, 'subj', [((i + step) % z.subjects, i) for i in ran...  3 us
    pallas_call x1, Pallas kernels, on_device(): pl.pallas_call(functools.partial(first_kernel, z), out_shape=shapes, in_s...  2.15 us
    ppermute x3, waiting for transfers between devices, on_device(): lax.ppermute(parts[step], 'tr', [(i, i ^ step) for i in range(z.n)])  2.13 us
    ppermute x3, starting transfers between devices, on_device(): lax.ppermute(parts[step], 'tr', [(i, i ^ step) for i in range(z.n)])  1.93 us
    ppermute x1, waiting for transfers between devices, on_device(): lax.ppermute(features, 'subj', [((i + step) % z.subjects, i) for i in ran...  1.55 us
    pallas_call x1, Pallas kernels, on_device(): pl.pallas_call(functools.partial(fourth_kernel, z), out_shape=[jax.ShapeD...  0.78 us
  transfers between devices with their start and end apart: 4, of which 2 were waited for; matrix products, arithmetic and copies ran while one was open for 0% of the time, Pallas kernels for 7%

profile of v6, /device:TPU:0, one launch (start us, length us, event | category | flops | bytes accessed | tf_op | source)
XLA Modules:
  0.0 29.6 jit_solution(15925663674476650789)
XLA Ops:
  0.6 3.0 %collective-permute-start = (bf16[64,1024]{1,0:T(8,128)(2,1)}, bf16[64,1024]{1,0:T(8,128)(2,1)S(1)}, u32[]{:S(2)}, u32[]{:S(2)}) collective-permute-start(bf16[64,1024]{1,0:T(8,128)(2,1)} %x_hbm.1), channel_id=1, source_target_pairs={{16,0},{0,16},{17,1},{1,17},{18,2},{2,18},{19,3},{3,19},{20,4},{4,... | collective-permute-start | bytes 393224 | tf_op jit(solution)/shard_map/ppermute | solution.py:397
  3.6 2.1 %prepare_and_own_columns.1 = (bf16[4,72,256]{2,1,0:T(8,128)(2,1)S(1)}, f32[288,128]{1,0:T(8,128)S(1)}, bf16[256,128]{1,0:T(8,128)(2,1)S(1)}, f32[72,256]{1,0:T(8...) custom-call(s32[4,4]{1,0:T(4,128)} %offsets_hbm.1, f32[4,4]{1,0:T(4,128)} %gains_hbm.1, s32[1,64]{1,0:T(1,128)} %bitcast.7, ...), custom_call_target="tpu_custom_call" | custom-call | flops 37748736 | bytes 3145728 | tf_op jit(solution)/shard_map/prepare_and_own_columns/pallas_call | solution.py:427
  5.8 1.6 %collective-permute-done.refs_0_ = bf16[64,1024]{1,0:T(8,128)(2,1)S(1)} collective-permute-done((bf16[64,1024]{1,0:T(8,128)(2,1)}, bf16[64,1024]{1,0:T(8,128)(2,1)S(1)}, u32[]{:S(2)}, u32[]{:S(2)}) %collective-permute-start) | collective-permute-done | bytes 131104 | tf_op jit(solution)/shard_map/ppermute | solution.py:397
  7.3 0.5 %other_columns.1 = s16[16,72,128]{2,1,0:T(8,128)(2,1)S(1)} custom-call(bf16[4,72,256]{2,1,0:T(8,128)(2,1)S(1)} %get-tuple-element.16.table_ref, bf16[1024,256]{1,0:T(8,128)(2,1)S(1)} %get-tuple-element.17.w_ref, f32[72,256]{1,0:T(8,128)S(1)} %get-tuple-element.18.total_ref, f32[288,128]{1,0:T(8,128)S(1)} %get-tuple-element.19.base_ref, ...), custom_call_target="tpu_custom_call" | custom-call | flops 37748736 | bytes 2097152 | tf_op jit(solution)/shard_map/other_columns/pallas_call | solution.py:437
  7.8 16.6 %all_to_all.5.received_ref = s16[16,72,128]{2,1,0:T(8,128)(2,1)S(1)} all-to-all(s16[16,72,128]{2,1,0:T(8,128)(2,1)S(1)} %other_columns.1), channel_id=1, replica_groups=mesh['subj'=2,'tr'=16] {'tr'}, dimensions={0} | all-to-all | bytes 589824 | tf_op jit(solution)/shard_map/all_to_all | solution.py:446
  24.4 0.4 %residuals.1 = (f32[32,128]{1,0:T(8,128)S(1)}, f32[32,128]{1,0:T(8,128)S(1)}, f32[32,128]{1,0:T(8,128)S(1)}, f32[32,128]{1,0:T(8,128)S(1)}) custom-call(s32[4,16]{1,0:T(4,128)S(1)} %get-tuple-element.15.orders_in_ref, s16[16,72,128]{2,1,0:T(8,128)(2,1)S(1)} %all_to_all.5.received_ref), custom_call_target="tpu_custom_call" | custom-call | flops 37748736 | bytes 1048576 | tf_op jit(solution)/shard_map/residuals/pallas_call | solution.py:450
  24.8 0.1 collective-permute-start.1
  24.8 0.7 %collective-permute-start.2 = (f32[32,128]{1,0:T(8,128)S(1)}, f32[32,128]{1,0:T(8,128)S(1)}, u32[]{:S(2)}, u32[]{:S(2)}) collective-permute-start(f32[32,128]{1,0:T(8,128)S(1)} %get-tuple-element.22), channel_id=1, source_target_pairs={{0,2},{1,3},{2,0},{3,1},{4,6},{5,7},{6,4},{7,5},{8,10},{9,11},{10,... | collective-permute-start | bytes 49160 | tf_op jit(solution)/shard_map/ppermute | solution.py:465
  25.5 1.2 %collective-permute-start.3 = (f32[32,128]{1,0:T(8,128)S(1)}, f32[32,128]{1,0:T(8,128)S(1)}, u32[]{:S(2)}, u32[]{:S(2)}) collective-permute-start(f32[32,128]{1,0:T(8,128)S(1)} %get-tuple-element.23), channel_id=1, source_target_pairs={{0,3},{1,2},{2,1},{3,0},{4,7},{5,6},{6,5},{7,4},{8,11},{9,10},{10,... | collective-permute-start | bytes 49160 | tf_op jit(solution)/shard_map/ppermute | solution.py:465
  26.7 0.0 collective-permute-done.1.refs_1_
  26.7 2.1 %collective-permute-done.2.refs_2_ = f32[32,128]{1,0:T(8,128)S(1)} collective-permute-done((f32[32,128]{1,0:T(8,128)S(1)}, f32[32,128]{1,0:T(8,128)S(1)}, u32[]{:S(2)}, u32[]{:S(2)}) %collective-permute-start.2) | collective-permute-done | bytes 16416 | tf_op jit(solution)/shard_map/ppermute | solution.py:465
  28.8 0.0 collective-permute-done.3.refs_3_
  28.8 0.8 %scores.1 = (f32[5,1,64]{2,1,0:T(1,128)}, f32[5,1,8]{2,1,0:T(1,128)}) custom-call(bf16[256,128]{1,0:T(8,128)(2,1)S(1)} %get-tuple-element.14.mean_ref, f32[32,128]{1,0:T(8,128)S(1)} %get-tuple-element.20.refs_0_, f32[32,128]{1,0:T(8,128)S(1)} %collective-permute-done.1.refs_1_, f32[32,128]{1,0:T(8,128)S(1)} %collective-permute-done.2.refs_2_, ...), custom_call_target="tpu_custom_call" | custom-call | flops 1048576 | bytes 65536 | tf_op jit(solution)/shard_map/scores/pallas_call | solution.py:468
Async XLA Ops:
  0.6 6.7 %collective-permute-start = (bf16[64,1024]{1,0:T(8,128)(2,1)}, bf16[64,1024]{1,0:T(8,128)(2,1)S(1)}, u32[]{:S(2)}, u32[]{:S(2)}) collective-permute-start(bf16[64,1024]{1,0:T(8,128)(2,1)} %x_hbm.1), channel_id=1, source_target_pairs={{16,0},{0,16},{17,1},{1,17},{18,2},{2,18},{19,3},{3,19},{20,4},{4,... | collective-permute-start | bytes 393224 | tf_op jit(solution)/shard_map/ppermute | solution.py:397
  24.8 1.9 %collective-permute-start.1 = (f32[32,128]{1,0:T(8,128)S(1)}, f32[32,128]{1,0:T(8,128)S(1)}, u32[]{:S(2)}, u32[]{:S(2)}) collective-permute-start(f32[32,128]{1,0:T(8,128)S(1)} %get-tuple-element.21), channel_id=1, source_target_pairs={{0,1},{1,0},{2,3},{3,2},{4,5},{5,4},{6,7},{7,6},{8,9},{9,8},{10,11... | collective-permute-start | bytes 49160 | tf_op jit(solution)/shard_map/ppermute | solution.py:465
  24.8 4.0 %collective-permute-start.2 = (f32[32,128]{1,0:T(8,128)S(1)}, f32[32,128]{1,0:T(8,128)S(1)}, u32[]{:S(2)}, u32[]{:S(2)}) collective-permute-start(f32[32,128]{1,0:T(8,128)S(1)} %get-tuple-element.22), channel_id=1, source_target_pairs={{0,2},{1,3},{2,0},{3,1},{4,6},{5,7},{6,4},{7,5},{8,10},{9,11},{10,... | collective-permute-start | bytes 49160 | tf_op jit(solution)/shard_map/ppermute | solution.py:465
  25.5 3.3 %collective-permute-start.3 = (f32[32,128]{1,0:T(8,128)S(1)}, f32[32,128]{1,0:T(8,128)S(1)}, u32[]{:S(2)}, u32[]{:S(2)}) collective-permute-start(f32[32,128]{1,0:T(8,128)S(1)} %get-tuple-element.23), channel_id=1, source_target_pairs={{0,3},{1,2},{2,1},{3,0},{4,7},{5,6},{6,5},{7,4},{8,11},{9,10},{10,... | collective-permute-start | bytes 49160 | tf_op jit(solution)/shard_map/ppermute | solution.py:465

commit v7 on v6

v7 whole, which is shorter than its diff:
```python
import functools

import jax
import jax.numpy as jnp
from jax import lax
from jax.experimental import pallas as pl
from jax.experimental.pallas import tpu as pltpu
from jax.sharding import PartitionSpec as P

MAXLAG = 8
VB = 4
CAP = 8
LANES = 128
GROUP = 2
EPSILON = 1e-6

f32 = jnp.float32
bf16 = jnp.bfloat16
i32 = jnp.int32

VMEM = pl.BlockSpec(memory_space=pltpu.VMEM)
HBM = pl.BlockSpec(memory_space=pltpu.HBM)


def iota(shape, axis):
    return lax.broadcasted_iota(i32, shape, axis)


def dot(a, b):
    return jnp.dot(a, b, preferred_element_type=f32)


def thirds(x):
    first = x.astype(bf16)
    rest = x - first.astype(f32)
    second = rest.astype(bf16)
    return first, second, (rest - second.astype(f32)).astype(bf16)


def params(**more):
    return pltpu.CompilerParams(vmem_limit_bytes=48 * 1024 * 1024, **more)


def cost(flops, nbytes):
    return pl.CostEstimate(flops=flops, bytes_accessed=nbytes, transcendentals=0)


class Sizes:
    def __init__(self, features, block_orders, offsets, weights, block_owner):
        self.subjects = lax.axis_size("subj")
        self.n = lax.axis_size("tr")
        self.rows, self.width = features.shape
        self.columns, self.voxels = weights.shape[1:]
        self.bands, self.taps = offsets.shape
        self.band_width = self.columns // self.bands
        self.piece = min(self.width, self.band_width)
        self.conditions = block_orders.shape[0] + 1
        self.blocks = block_owner.shape[1]
        self.ext = self.rows + MAXLAG
        self.own = self.rows // GROUP
        self.own_tail = MAXLAG // GROUP
        self.tiles = self.voxels // LANES
        self.groups = self.n // GROUP
        self.half = self.own // 2
        self.tail_at = self.tiles * self.own
        self.scale_at = self.tail_at + self.tiles * self.own_tail
        self.signal_scale = self.tiles
        self.signal_at = self.scale_at + -(-(self.tiles + 1) // 8) * 8
        self.message = self.signal_at + self.half
        self.source = self.own + 16
        assert GROUP * CAP * VB * 2 == LANES and self.n % GROUP == 0
        assert self.half % 8 == 0 and self.conditions < 8 and self.own_tail < 8
        assert self.tiles * self.own_tail % 8 == 0


def coded(x):
    largest = jnp.max(jnp.abs(x), axis=0, keepdims=True)
    power = jnp.floor(jnp.log2(jnp.maximum(largest, 2.0**-100))) + 1.0
    value = jnp.round(x * jnp.exp2(15.0 - power))
    return jnp.clip(value, -32767.0, 32767.0), power


def fill_signal(z, rows_ref, all_columns, base_ref):
    pieces = []
    for member in range(GROUP):
        for part in range(2):
            start = member + GROUP * part * z.half
            piece = [
                rows_ref[pl.ds(tile * z.rows + start, z.half, stride=GROUP), :]
                for tile in range(z.tiles)
            ]
            pieces.append(jnp.concatenate(piece, axis=1))
    value, power = coded(jnp.concatenate(pieces, axis=0))
    upper = jnp.floor(value * (1.0 / 256.0))
    lower = value - 256.0 * upper
    powers = jnp.broadcast_to(power, (8, z.voxels))
    terms = jnp.concatenate([upper, lower, powers], axis=0).astype(bf16)
    picked = dot(terms, all_columns)
    value = 256.0 * picked[: z.rows] + picked[z.rows : 2 * z.rows]
    left = iota((z.half, LANES), 1) < LANES // 2
    row = iota((z.signal_at - z.scale_at, LANES), 0)
    for index in range(z.n):
        lanes = slice(index // GROUP * LANES, (index // GROUP + 1) * LANES)
        start = (index % GROUP) * z.own
        first = value[start : start + z.half, lanes]
        second = value[start + z.half : start + z.own, lanes]
        power = picked[2 * z.rows : 2 * z.rows + 1, lanes]
        power = jnp.where(row == z.signal_scale, power, 0.0)
        body = jnp.where(left, first, second)
        base_ref[index] = jnp.concatenate([power, body], axis=0)


def filtered_product(z, x_ref, w_ref, table_ref, source):
    total = jnp.zeros((z.ext, z.voxels), f32)
    early = iota((8, z.piece), 0) < z.own_tail
    for part in range(z.width // z.piece):
        columns = slice(part * z.piece, (part + 1) * z.piece)
        x = x_ref[:, columns]
        table = table_ref[lax.div(source * z.width + part * z.piece, z.band_width)]
        stacked = jnp.concatenate([x] * (table.shape[1] // z.rows), axis=0)
        filtered = dot(table, stacked)
        low = filtered - filtered.astype(bf16).astype(f32)
        edges = [filtered]
        for start in range(0, z.rows, z.own):
            edges.append(jnp.where(early, low[start : start + 8], 0.0))
        edges.append(low[z.rows :])
        edges = jnp.concatenate(edges, axis=0).astype(bf16)
        product = dot(edges, w_ref[columns, :])
        parts = []
        for member in range(GROUP):
            start, at = member * z.own, z.ext + member * 8
            parts.append(product[start : start + 8] + product[at : at + 8])
            parts.append(product[start + 8 : start + z.own])
        parts.append(product[z.rows : z.ext] + product[z.ext + GROUP * 8 :])
        total = total + jnp.concatenate(parts, axis=0)
    return total


def fill_table(z, offsets_ref, gains_ref, table_ref):
    lanes = table_ref.shape[2]
    column = iota((z.ext, lanes), 1)
    row = iota((z.ext, 1), 0)
    after = row - z.rows
    time = row // z.own + GROUP * (row % z.own)
    time_after = z.rows + after // z.own_tail + GROUP * (after % z.own_tail)
    lag = jnp.where(after < 0, time, time_after) - column % z.rows
    term = column // z.rows
    for band in range(z.bands):
        value = jnp.zeros((z.ext, lanes), f32)
        for tap in range(z.taps):
            hit = lag == offsets_ref[band, tap]
            value = value + jnp.where(hit, gains_ref[band, tap], 0.0)
        first, second, third = (t.astype(f32) for t in thirds(value))
        chosen = jnp.where(term == 0, first, jnp.where(term == 1, second, third))
        chosen = jnp.where(term > 2, 0.0, chosen)
        table_ref[band] = chosen.astype(bf16)


def owned_columns(z, owners_ref):
    owners = owners_ref[...]
    other = iota((z.voxels, z.blocks), 1)
    block = iota((z.voxels, 1), 0) // VB
    owner = jnp.sum(jnp.where(other == block, owners, 0), axis=1, keepdims=True)
    before = (owners == owner) & (other < block)
    rank = jnp.sum(before.astype(i32), axis=1, keepdims=True)
    place = (owner * CAP + rank) * VB + iota((z.voxels, 1), 0) % VB
    lane = iota((1, z.groups * LANES), 1)
    half = LANES // 2
    every = place == lane // LANES * half + lane % half
    group = lax.axis_index("tr") // GROUP
    mine = place == group * half + iota((1, LANES), 1) % half
    return every.astype(f32).astype(bf16), mine.astype(f32)


def first_kernel(
    z, offsets_hbm, gains_hbm, owners_hbm, x_hbm, w_hbm, signal_hbm, orders_hbm,
    table_ref, base_ref, mine_ref, total_ref, rest_ref, orders_ref, signal_ref,
    offsets_ref, gains_ref, owners_ref, x_ref, w_ref, rows_ref, sems,
):
    me = lax.axis_index("subj")

    def weight_rows(step):
        source = lax.rem(me + step, z.subjects)
        start = pl.multiple_of(source * z.width, z.width)
        return w_hbm.at[pl.ds(start, z.width), :]

    moves = [
        (offsets_hbm, offsets_ref),
        (gains_hbm, gains_ref),
        (x_hbm, x_ref),
        (weight_rows(0), w_ref),
        (owners_hbm, owners_ref),
        (signal_hbm, signal_ref),
        (orders_hbm, orders_ref),
    ]
    for step in range(1, z.subjects):
        rows = pl.ds((step - 1) * z.width, z.width)
        moves.append((weight_rows(step), rest_ref.at[rows, :]))
    copies = [
        pltpu.make_async_copy(origin, target, sems.at[index])
        for index, (origin, target) in enumerate(moves)
    ]
    for copy in copies:
        copy.start()
    copies[0].wait()
    copies[1].wait()
    fill_table(z, offsets_ref, gains_ref, table_ref)
    copies[2].wait()
    copies[3].wait()
    total_ref[...] = filtered_product(z, x_ref, w_ref, table_ref, me)
    copies[4].wait()
    every, mine = owned_columns(z, owners_ref)
    mine = jnp.concatenate([256.0 * mine, mine], axis=0)
    mine_ref[...] = mine.astype(bf16)
    copies[5].wait()
    for tile in range(z.tiles):
        lanes = slice(tile * LANES, (tile + 1) * LANES)
        rows = slice(tile * z.rows, (tile + 1) * z.rows)
        rows_ref[rows, :] = signal_ref[:, lanes].astype(f32)
    fill_signal(z, rows_ref, every, base_ref)
    for copy in copies[6:]:
        copy.wait()


def second_kernel(
    z, table_ref, w_ref, total_ref, base_ref, signal_ref, sibling_ref, *refs
):
    others, (out_ref, own_signal_ref) = refs[:-2], refs[-2:]
    me = lax.axis_index("subj")
    total = total_ref[...]
    for step, x_ref in enumerate(others):
        source = lax.rem(me + step + 1, z.subjects)
        rows = w_ref.at[step * z.width : (step + 1) * z.width, :]
        total = total + filtered_product(z, x_ref, rows, table_ref, source)
    value, power = coded(total)
    row = iota((8, LANES), 0)
    for member in range(GROUP):
        shared = []
        for tile in range(z.tiles):
            lanes = slice(tile * LANES, (tile + 1) * LANES)
            shared.append(value[member * z.own : (member + 1) * z.own, lanes])
        tails = [jnp.zeros((8, LANES), f32)] * (z.tiles * z.own_tail // 8)
        for tile in range(z.tiles):
            lanes = slice(tile * LANES, (tile + 1) * LANES)
            which, place = divmod(tile * z.own_tail, 8)
            shift = (place - member * z.own_tail) % 8
            tail = pltpu.roll(value[z.rows :, lanes], shift, 0)
            here = (row >= place) & (row < place + z.own_tail)
            tails[which] = jnp.where(here, tail, tails[which])
        powers = jnp.zeros((z.signal_at - z.scale_at, LANES), f32)
        place = iota(powers.shape, 0)
        for tile in range(z.tiles):
            lanes = slice(tile * LANES, (tile + 1) * LANES)
            powers = jnp.where(place == tile, power[:, lanes], powers)
        for index in range(member, z.n, GROUP):
            base = base_ref[index]
            last = [base[: powers.shape[0]] + powers, base[powers.shape[0] :]]
            message = jnp.concatenate(shared + tails + last, axis=0)
            out_ref[index] = message.astype(i32).astype(jnp.int16)
    member = lax.rem(lax.axis_index("tr"), GROUP)
    shape = (z.own, z.rows)
    pick = iota(shape, 1) == GROUP * iota(shape, 0) + member
    pick = pick.astype(f32).astype(bf16)
    own_signal_ref[0] = dot(pick, signal_ref[...])
    own_signal_ref[1] = dot(pick, sibling_ref[...])


def third_kernel(z, orders_in_ref, mine_ref, own_signal_ref, received_ref, *refs):
    out_refs, (terms_ref, placed_ref, block_ref, tail_ref, *more) = (
        refs[:GROUP],
        refs[GROUP:],
    )
    orders = orders_in_ref[...]
    if more:
        orders_ref, sem = more
        copy = pltpu.make_async_copy(orders_in_ref, orders_ref, sem)
        copy.start()
    me = lax.axis_index("tr")
    row = iota((8, LANES), 0)
    left = iota((z.half, LANES), 1) < LANES // 2

    def integers(index, start, stop):
        return received_ref[index, start:stop, :].astype(i32)

    def numbers(index, start, stop):
        return integers(index, start, stop).astype(f32)

    def tails_of(x):
        tails = []
        for tile in range(z.tiles):
            which, place = divmod(tile * z.own_tail, 8)
            tail = x[which * 8 : which * 8 + 8]
            tails.append(pltpu.roll(tail, (8 - place) % 8, 0))
        return tails

    def unpack(index, carry):
        start = index * z.source
        start = start if isinstance(start, int) else pl.multiple_of(start, 16)
        body = integers(index, 0, z.tail_at)
        tails = tails_of(numbers(index, z.tail_at, z.scale_at))
        powers = numbers(index, z.scale_at, z.signal_at)
        for tile in range(z.tiles):
            x = body[tile * z.own : (tile + 1) * z.own]
            upper = lax.shift_right_arithmetic(x, jnp.full_like(x, 8))
            lower = x - upper * 256
            tail = tails[tile]
            high = jnp.floor(tail * (1.0 / 256.0))
            low = tail - 256.0 * high
            power = powers[tile : tile + 1]
            none = jnp.zeros((8, LANES), f32)
            power = jnp.broadcast_to(power, none.shape)
            first = jnp.concatenate([upper.astype(f32), high, none], axis=0)
            second = jnp.concatenate([lower.astype(f32), low, power], axis=0)
            lanes = slice(tile * LANES, (tile + 1) * LANES)
            terms_ref[pl.ds(start, z.source), lanes] = first.astype(bf16)
            lanes = slice(z.voxels + lanes.start, z.voxels + lanes.stop)
            terms_ref[pl.ds(start, z.source), lanes] = second.astype(bf16)
        return carry

    def place_block(index, carry):
        start = index * z.source
        start = start if isinstance(start, int) else pl.multiple_of(start, 16)
        x = placed_ref[pl.ds(start, z.source), :]
        scale = jnp.exp2(x[z.own + 8 : z.own + 9] - 15.0)
        block_ref[index] = jnp.where(left, x[: z.half], x[z.half : z.own]) * scale
        first = left[:8] & (row < z.own_tail)
        tail_ref[index] = jnp.where(first, x[z.own : z.own + 8] * scale, 0.0)
        return carry

    def add_position(position, sums):
        added = []
        at = z.scale_at + z.signal_scale
        power = numbers(position, at // 8 * 8, z.signal_at)[at % 8 : at % 8 + 1]
        signal = numbers(position, z.signal_at, z.message) * jnp.exp2(power - 15.0)
        before = jnp.maximum(position - 1, 0)
        for condition in range(z.conditions + 1):
            if condition == z.conditions:
                residual = signal
            else:
                if condition == 0:
                    here, ahead = position, before
                elif more:
                    here = orders_ref[condition - 1, position]
                    ahead = orders_ref[condition - 1, before]
                else:
                    here = orders[condition - 1, position]
                    ahead = orders[condition - 1, max(position - 1, 0)]
                tail = tail_ref[jnp.where(position == 0, z.n, ahead)]
                residual = signal - block_ref[here]
                parts = [residual[:8] - tail, residual[8:]]
                residual = jnp.concatenate(parts, axis=0)
            value = residual * residual
            total = sums[condition]
            for start in range(0, z.half, 8):
                total = total + value[start : start + 8]
            added.append(total)
        return tuple(added)

    def loop(body, carry):
        if more:
            return lax.fori_loop(0, z.n, body, carry)
        for index in range(z.n):
            carry = body(index, carry)
        return carry

    def scales_of(index):
        powers = numbers(index, z.scale_at, z.signal_at)
        return jnp.exp2(powers[: z.tiles] - 15.0)

    def energy_of(step, here, ahead, kept):
        scale, scale_ahead = scales_of(here), scales_of(ahead) * kept
        body = numbers(here, 0, z.tail_at)
        tails = tails_of(numbers(ahead, z.tail_at, z.scale_at))
        total = jnp.zeros((z.own, LANES), f32)
        for tile in range(z.tiles):
            lanes = slice(tile * LANES, (tile + 1) * LANES)
            block = body[tile * z.own : (tile + 1) * z.own] * scale[tile : tile + 1]
            residual = own_signal_ref[step, :, lanes] - block
            tail = tails[tile] * scale_ahead[tile : tile + 1]
            tail = jnp.where(row < z.own_tail, tail, 0.0)
            residual = jnp.concatenate([residual[:8] - tail, residual[8:]], axis=0)
            total = total + residual * residual
        return jnp.sum(total, axis=1, keepdims=True)

    loop(unpack, 0)
    chunk = 16 * z.source
    for start in range(0, z.n * z.source, chunk):
        stop = min(start + chunk, z.n * z.source)
        placed_ref[start:stop, :] = dot(terms_ref[start:stop, :], mine_ref[...])
    lanes = iota((z.own, LANES), 1)
    place = iota(orders.shape, 1)
    energies = []
    for step in range(GROUP):
        energy = jnp.zeros((z.own, LANES), f32)
        position = jnp.bitwise_xor(me, step)
        kept = jnp.where(position == 0, 0.0, 1.0)
        before = jnp.maximum(position - 1, 0)
        own = jnp.where(place == position, orders, 0)
        own = jnp.sum(own, axis=1, keepdims=True)
        preceding = jnp.where(place == before, orders, 0)
        preceding = jnp.sum(preceding, axis=1, keepdims=True)
        for condition in range(z.conditions):
            if condition == 0:
                here, ahead = position, before
            else:
                here, ahead = own[condition - 1, 0], preceding[condition - 1, 0]
            value = energy_of(step, here, ahead, kept) * (1.0 / z.voxels)
            energy = jnp.where(lanes == condition, value, energy)
        energies.append(energy)
    loop(place_block, 0)
    tail_ref[z.n] = jnp.zeros((8, LANES), f32)
    if more:
        copy.wait()
    zero = jnp.zeros((8, LANES), f32)
    sums = loop(add_position, (zero,) * (z.conditions + 1))
    stats = zero
    for condition, value in enumerate(sums):
        stat = jnp.sum(value, axis=0, keepdims=True)
        stats = jnp.where(row == condition, stat, stats)
    for energy, out_ref in zip(energies, out_refs):
        out_ref[: z.own, :] = energy
        out_ref[z.own :, :] = stats


def fourth_kernel(z, *refs):
    parts, (energy_ref, scores_ref) = refs[:GROUP], refs[GROUP:]
    member = lax.rem(lax.axis_index("tr"), GROUP)
    sums = sum(p[z.own :, :] for p in parts)
    sums = sums + pltpu.roll(sums, LANES // 2, 1)
    signal = sums[z.conditions : z.conditions + 1]
    fit = jnp.log((sums + EPSILON) / (signal + EPSILON))
    terms = [t.astype(f32) for t in thirds(fit)]
    square = (LANES, LANES)
    place = iota(square, 0) // VB - member * CAP
    mean = (place == iota(square, 1)) & (place >= 0) & (place < CAP)
    mean = mean & (iota(square, 0) < LANES // 2)
    mean = jnp.where(mean, 1.0 / VB, 0.0).astype(bf16)
    score = dot(jnp.concatenate(terms, axis=0).astype(bf16), mean)
    turned = jnp.transpose(jnp.concatenate([p[: z.own, :] for p in parts], axis=0))
    column = iota((z.rows, LANES), 0)
    owner = jnp.bitwise_xor(column // z.own, member)
    order = iota((z.rows, LANES), 1) == owner + GROUP * (column % z.own)
    order = order.astype(f32).astype(bf16)
    terms = [t.astype(f32) for t in thirds(turned[:8, : z.rows])]
    energy = dot(jnp.concatenate(terms, axis=0).astype(bf16), order)
    energy = energy[:8] + energy[8:16] + energy[16:]
    score = score[:8] + score[8:16] + score[16:]
    for index in range(z.conditions):
        energy_ref[index] = energy[index : index + 1, : z.rows]
        scores_ref[index] = score[index : index + 1, :CAP]


def on_device(features, block_orders, offsets, tap_gains, weights, signal, block_owner):
    z = Sizes(features, block_orders, offsets, weights, block_owner)
    owners = block_owner.reshape(1, z.blocks)
    siblings = [(i, i ^ 1) for i in range(z.n)]
    others = [
        lax.ppermute(
            features,
            "subj",
            [((i + step) % z.subjects, i) for i in range(z.subjects)],
        )
        for step in range(1, z.subjects)
    ]
    sibling_signal = lax.ppermute(signal[0], "tr", siblings)
    term_lanes = -(-3 * z.rows // LANES) * LANES
    work = 2 * z.ext * z.width * z.voxels
    shapes = [
        jax.ShapeDtypeStruct((z.bands, z.ext, term_lanes), bf16),
        jax.ShapeDtypeStruct((z.n, z.message - z.scale_at, LANES), f32),
        jax.ShapeDtypeStruct((2 * z.voxels, LANES), bf16),
        jax.ShapeDtypeStruct((z.ext, z.voxels), f32),
        jax.ShapeDtypeStruct((z.columns - z.width, z.voxels), bf16),
        jax.ShapeDtypeStruct(block_orders.shape, i32),
        jax.ShapeDtypeStruct((z.rows, z.voxels), bf16),
    ]
    scratch = [
        pltpu.SMEM(offsets.shape, i32),
        pltpu.SMEM(tap_gains.shape, f32),
        pltpu.VMEM(owners.shape, i32),
        pltpu.VMEM(features.shape, bf16),
        pltpu.VMEM((z.width, z.voxels), bf16),
        pltpu.VMEM((z.tiles * z.rows, LANES), f32),
        pltpu.SemaphoreType.DMA((6 + z.subjects,)),
    ]
    operands = (offsets, tap_gains, owners, features, weights[0], signal[0], block_orders)
    operands = [pltpu.with_memory_space_constraint(x, pltpu.HBM) for x in operands]
    table, base, mine, total, rest, orders, signal = pl.pallas_call(
        functools.partial(first_kernel, z),
        out_shape=shapes,
        in_specs=[HBM] * len(operands),
        out_specs=[VMEM] * len(shapes),
        scratch_shapes=scratch,
        compiler_params=params(),
        cost_estimate=cost(work, 3 << 20),
        name="prepare_and_own_columns",
    )(*operands)
    outgoing, own_signal = pl.pallas_call(
        functools.partial(second_kernel, z),
        out_shape=[
            jax.ShapeDtypeStruct((z.n, z.message, LANES), jnp.int16),
            jax.ShapeDtypeStruct((GROUP, z.own, z.voxels), f32),
        ],
        in_specs=[VMEM] * (6 + len(others)),
        out_specs=[VMEM, VMEM],
        compiler_params=params(),
        cost_estimate=cost(work, 2 << 20),
        name="other_columns",
    )(table, rest, total, base, signal, sibling_signal, *others)
    received = lax.all_to_all(outgoing, "tr", 0, 0, tiled=True)
    more = [pltpu.SMEM(block_orders.shape, i32), pltpu.SemaphoreType.DMA]
    more = more if z.n > 16 else []
    part = jax.ShapeDtypeStruct((z.own + 8, LANES), f32)
    parts = pl.pallas_call(
        functools.partial(third_kernel, z),
        out_shape=[part] * GROUP,
        in_specs=[VMEM] * 4,
        out_specs=[VMEM] * GROUP,
        scratch_shapes=[
            pltpu.VMEM((z.n * z.source, 2 * z.voxels), bf16),
            pltpu.VMEM((z.n * z.source, LANES), f32),
            pltpu.VMEM((z.n, z.half, LANES), f32),
            pltpu.VMEM((z.n + 1, 8, LANES), f32),
            *more,
        ],
        compiler_params=params(),
        cost_estimate=cost(work, 1 << 20),
        name="residuals",
    )(orders, mine, own_signal, received)
    parts = [parts[0], lax.ppermute(parts[1], "tr", siblings)]
    energy, scores = pl.pallas_call(
        functools.partial(fourth_kernel, z),
        out_shape=[
            jax.ShapeDtypeStruct((z.conditions, 1, z.rows), f32),
            jax.ShapeDtypeStruct((z.conditions, 1, CAP), f32),
        ],
        in_specs=[VMEM] * GROUP,
        out_specs=[VMEM, VMEM],
        compiler_params=params(),
        cost_estimate=cost(1 << 20, 1 << 16),
        name="scores",
    )(*parts)
    return energy.transpose(1, 2, 0), scores.transpose(1, 2, 0)


def solution(mesh):
    placed = (
        P("tr", "subj"),
        P(),
        P(),
        P(),
        P("subj", None, None),
        P("subj", "tr", None),
        P("subj", None, None),
    )
    return jax.shard_map(
        on_device,
        mesh=mesh,
        in_specs=placed,
        out_specs=(P("subj", "tr", None), P("subj", "tr", None)),
        check_vma=False,
    )
```

time: 29.8 us -> 28.9 us (0.970)
  starting transfers between devices: 4.94 us -> 3.19 us
  blocking collectives: 16.6 us -> 18.2 us
  waiting for transfers between devices: 3.68 us -> 2.63 us
  Pallas kernels: 3.76 us -> 4.06 us
    ppermute x3 -> x2, starting transfers between devices: 1.93 us -> 0.18 us  [the longest x1 0.18 us: on_device(): parts = [parts[0], lax.ppermute(parts[1], 'tr', siblings)]]
    all_to_all x1, blocking collectives: 16.6 us -> 18.2 us  [on_device(): received = lax.all_to_all(outgoing, 'tr', 0, 0, tiled=True)]
    ppermute x3 -> x2, waiting for transfers between devices: 2.13 us -> 1.08 us  [the longest x1 1.07 us: on_device(): parts = [parts[0], lax.ppermute(parts[1], 'tr', siblings)]]
  transfers between devices with their start and end apart: 4 -> 3, of which waited for: 2 -> 2; matrix products, arithmetic and copies ran while one was open for 0% -> 0% of each run, Pallas kernels for 7% -> 7%
where the time goes in v7:
time: 28.9 us; the launch traced here: 28.7 us
  blocking collectives  18.2 us (63%)
  Pallas kernels  4.06 us (14%)
  starting transfers between devices  3.19 us (11%)
  waiting for transfers between devices  2.63 us (9%)
  between operations  0.67 us (2%)
    all_to_all x1, blocking collectives, on_device(): received = lax.all_to_all(outgoing, 'tr', 0, 0, tiled=True)  18.2 us
    ppermute x1, starting transfers between devices, on_device(): lax.ppermute(features, 'subj', [((i + step) % z.subjects, i) for i in ran...  3 us
    pallas_call x1, Pallas kernels, on_device(): pl.pallas_call(functools.partial(first_kernel, z), out_shape=shapes, in_s...  2.13 us
    ppermute x1, waiting for transfers between devices, on_device(): lax.ppermute(features, 'subj', [((i + step) % z.subjects, i) for i in ran...  1.55 us
    ppermute x1, waiting for transfers between devices, on_device(): parts = [parts[0], lax.ppermute(parts[1], 'tr', siblings)]  1.07 us
    pallas_call x1, Pallas kernels, on_device(): pl.pallas_call(functools.partial(fourth_kernel, z), out_shape=[jax.ShapeD...  0.79 us
    pallas_call x1, Pallas kernels, on_device(): pl.pallas_call(functools.partial(third_kernel, z), out_shape=[part] * GRO...  0.66 us
  transfers between devices with their start and end apart: 3, of which 2 were waited for; matrix products, arithmetic and copies ran while one was open for 0% of the time, Pallas kernels for 7%

profile of v7, /device:TPU:0, one launch (start us, length us, event | category | flops | bytes accessed | tf_op | source)
XLA Modules:
  0.0 28.7 jit_solution(11549607023579696502)
XLA Ops:
  0.6 3.0 %collective-permute-start.1 = (bf16[64,1024]{1,0:T(8,128)(2,1)}, bf16[64,1024]{1,0:T(8,128)(2,1)S(1)}, u32[]{:S(2)}, u32[]{:S(2)}) collective-permute-start(bf16[64,1024]{1,0:T(8,128)(2,1)} %x_hbm.1), channel_id=1, source_target_pairs={{16,0},{0,16},{17,1},{1,17},{18,2},{2,18},{19,3},{3,19},{20,4},{4,... | collective-permute-start | bytes 393224 | tf_op jit(solution)/shard_map/ppermute | solution.py:458
  3.6 0.0 collective-permute-start
  3.6 2.1 %prepare_and_own_columns.1 = (bf16[4,72,256]{2,1,0:T(8,128)(2,1)S(1)}, f32[16,24,128]{2,1,0:T(8,128)S(1)}, bf16[512,128]{1,0:T(8,128)(2,1)S(1)}, f32[72,256]{1,0...) custom-call(s32[4,4]{1,0:T(4,128)} %offsets_hbm.1, ...), custom_call_target="tpu_custom_call" | custom-call | flops 37748736 | bytes 3145728 | tf_op jit(solution)/shard_map/prepare_and_own_columns/pallas_call | solution.py:488
  5.8 0.0 collective-permute-done.sibling_ref
  5.8 1.6 %collective-permute-done.1.refs_0_ = bf16[64,1024]{1,0:T(8,128)(2,1)S(1)} collective-permute-done((bf16[64,1024]{1,0:T(8,128)(2,1)}, bf16[64,1024]{1,0:T(8,128)(2,1)S(1)}, u32[]{:S(2)}, u32[]{:S(2)}) %collective-permute-start.1) | collective-permute-done | bytes 131104 | tf_op jit(solution)/shard_map/ppermute | solution.py:458
  7.3 0.5 %other_columns.1 = (s16[16,96,128]{2,1,0:T(8,128)(2,1)S(1)}, f32[2,32,256]{2,1,0:T(8,128)S(1)}) custom-call(bf16[4,72,256]{2,1,0:T(8,128)(2,1)S(1)} %get-tuple-element.17.table_ref, bf16[1024,256]{1,0:T(8,128)(2,1)S(1)} %get-tuple-element.18.w_ref, f32[72,256]{1,0:T(8,128)S(1)} %get-tuple-element.19.total_ref, ...), custom_call_target="tpu_custom_call" | custom-call | flops 37748736 | bytes 2097152 | tf_op jit(solution)/shard_map/other_columns/pallas_call | solution.py:498
  7.8 18.2 %all_to_all.5.received_ref = s16[16,96,128]{2,1,0:T(8,128)(2,1)S(1)} all-to-all(s16[16,96,128]{2,1,0:T(8,128)(2,1)S(1)} %get-tuple-element.23), channel_id=1, replica_groups=mesh['subj'=2,'tr'=16] {'tr'}, dimensions={0} | all-to-all | bytes 786432 | tf_op jit(solution)/shard_map/all_to_all | solution.py:510
  26.0 0.7 %residuals.1 = (f32[40,128]{1,0:T(8,128)S(1)}, f32[40,128]{1,0:T(8,128)S(1)}) custom-call(s32[4,16]{1,0:T(4,128)S(1)} %get-tuple-element.15.orders_in_ref, bf16[512,128]{1,0:T(8,128)(2,1)S(1)} %get-tuple-element.16.mine_ref, f32[2,32,256]{2,1,0:T(8,128)S(1)} %get-tuple-element.22.own_signal_ref, s16[16,96,128]{2,1,0:T(8,128)(2,1)S(1)} %all_to_all.5.received_ref), custom_call_target="tpu_custom_call" | custom-call | flops 37748736 | bytes 1048576 | tf_op jit(solution)/shard_map/residuals/pallas_call | solution.py:514
  26.7 0.2 collective-permute-start.2
  26.9 1.1 %collective-permute-done.2.refs_1_ = f32[40,128]{1,0:T(8,128)S(1)} collective-permute-done((f32[40,128]{1,0:T(8,128)S(1)}, f32[40,128]{1,0:T(8,128)S(1)}, u32[]{:S(2)}, u32[]{:S(2)}) %collective-permute-start.2) | collective-permute-done | bytes 20512 | tf_op jit(solution)/shard_map/ppermute | solution.py:530
  27.9 0.8 %scores.1 = (f32[5,1,64]{2,1,0:T(1,128)}, f32[5,1,8]{2,1,0:T(1,128)}) custom-call(f32[40,128]{1,0:T(8,128)S(1)} %get-tuple-element.24.refs_0_, f32[40,128]{1,0:T(8,128)S(1)} %collective-permute-done.2.refs_1_), custom_call_target="tpu_custom_call" | custom-call | flops 1048576 | bytes 65536 | tf_op jit(solution)/shard_map/scores/pallas_call | solution.py:531
Async XLA Ops:
  0.6 6.7 %collective-permute-start.1 = (bf16[64,1024]{1,0:T(8,128)(2,1)}, bf16[64,1024]{1,0:T(8,128)(2,1)S(1)}, u32[]{:S(2)}, u32[]{:S(2)}) collective-permute-start(bf16[64,1024]{1,0:T(8,128)(2,1)} %x_hbm.1), channel_id=1, source_target_pairs={{16,0},{0,16},{17,1},{1,17},{18,2},{2,18},{19,3},{3,19},{20,4},{4,... | collective-permute-start | bytes 393224 | tf_op jit(solution)/shard_map/ppermute | solution.py:458
  3.6 2.1 %collective-permute-start = (bf16[64,256]{1,0:T(8,128)(2,1)}, bf16[64,256]{1,0:T(8,128)(2,1)S(1)}, u32[]{:S(2)}, u32[]{:S(2)}) collective-permute-start(bf16[64,256]{1,0:T(8,128)(2,1)} %bitcast.6), channel_id=1, source_target_pairs={{0,1},{1,0},{2,3},{3,2},{4,5},{5,4},{6,7},{7,6},{8,9},{9,8},{10,11... | collective-permute-start | bytes 98312 | tf_op jit(solution)/shard_map/ppermute | solution.py:465
  26.7 1.3 %collective-permute-start.2 = (f32[40,128]{1,0:T(8,128)S(1)}, f32[40,128]{1,0:T(8,128)S(1)}, u32[]{:S(2)}, u32[]{:S(2)}) collective-permute-start(f32[40,128]{1,0:T(8,128)S(1)} %get-tuple-element.25), channel_id=1, source_target_pairs={{0,1},{1,0},{2,3},{3,2},{4,5},{5,4},{6,7},{7,6},{8,9},{9,8},{10,11... | collective-permute-start | bytes 61448 | tf_op jit(solution)/shard_map/ppermute | solution.py:530

commit v8 on v7

--- a/solution.py
+++ b/solution.py
@@ -63,21 +63,47 @@
         self.groups = self.n // GROUP
         self.half = self.own // 2
         self.tail_at = self.tiles * self.own
-        self.scale_at = self.tail_at + self.tiles * self.own_tail
-        self.signal_scale = self.tiles
-        self.signal_at = self.scale_at + -(-(self.tiles + 1) // 8) * 8
+        self.signal_at = self.tail_at + self.tiles * self.own_tail
         self.message = self.signal_at + self.half
-        self.source = self.own + 16
+        self.pair = 2 * (self.own + 8)
         assert GROUP * CAP * VB * 2 == LANES and self.n % GROUP == 0
-        assert self.half % 8 == 0 and self.conditions < 8 and self.own_tail < 8
+        assert self.half % 8 == 0 and self.conditions < 8 and 8 % self.own_tail == 0
         assert self.tiles * self.own_tail % 8 == 0
 
 
-def coded(x):
-    largest = jnp.max(jnp.abs(x), axis=0, keepdims=True)
-    power = jnp.floor(jnp.log2(jnp.maximum(largest, 2.0**-100))) + 1.0
-    value = jnp.round(x * jnp.exp2(15.0 - power))
-    return jnp.clip(value, -32767.0, 32767.0), power
+BITS, LEAST = 7, -126
+STEPS, SMALLEST = 512.0, -50.0
+
+
+def coded_signal(x):
+    size = jnp.abs(x)
+    power = jnp.floor(jnp.log2(jnp.maximum(size, 2.0**LEAST)))
+    half = jnp.floor(power * 0.5)
+    significand = size * jnp.exp2(-half) * jnp.exp2(half - power)
+    code = jnp.round((power - LEAST + significand - 1.0) * 2.0**BITS)
+    code = jnp.clip(code, 0.0, 32767.0)
+    return jnp.where(x < 0.0, -code, code)
+
+
+def decoded_signal(code):
+    size = jnp.abs(code)
+    power = lax.shift_right_logical(size, jnp.full_like(size, BITS))
+    significand = (size & (2**BITS - 1)) + 2**BITS
+    scale = jnp.exp2((power + (LEAST - BITS)).astype(f32))
+    value = significand.astype(f32) * scale
+    return jnp.where(code < 0, -value, value)
+
+
+def coded_prediction(x):
+    size = jnp.maximum(jnp.abs(x), 2.0**SMALLEST)
+    code = jnp.round((jnp.log2(size) - SMALLEST) * STEPS)
+    code = jnp.minimum(code, 32767.0)
+    return jnp.where(x < 0.0, -code, code)
+
+
+def decoded_prediction(code):
+    value = jnp.exp2(jnp.abs(code) * (1.0 / STEPS) + SMALLEST)
+    return jnp.where(code < 0.0, -value, value)
 
 
 def fill_signal(z, rows_ref, all_columns, base_ref):
@@ -90,24 +116,18 @@
                 for tile in range(z.tiles)
             ]
             pieces.append(jnp.concatenate(piece, axis=1))
-    value, power = coded(jnp.concatenate(pieces, axis=0))
+    value = coded_signal(jnp.concatenate(pieces, axis=0))
     upper = jnp.floor(value * (1.0 / 256.0))
     lower = value - 256.0 * upper
-    powers = jnp.broadcast_to(power, (8, z.voxels))
-    terms = jnp.concatenate([upper, lower, powers], axis=0).astype(bf16)
-    picked = dot(terms, all_columns)
-    value = 256.0 * picked[: z.rows] + picked[z.rows : 2 * z.rows]
+    picked = dot(jnp.concatenate([upper, lower], axis=0).astype(bf16), all_columns)
+    value = 256.0 * picked[: z.rows] + picked[z.rows :]
     left = iota((z.half, LANES), 1) < LANES // 2
-    row = iota((z.signal_at - z.scale_at, LANES), 0)
     for index in range(z.n):
         lanes = slice(index // GROUP * LANES, (index // GROUP + 1) * LANES)
         start = (index % GROUP) * z.own
         first = value[start : start + z.half, lanes]
         second = value[start + z.half : start + z.own, lanes]
-        power = picked[2 * z.rows : 2 * z.rows + 1, lanes]
-        power = jnp.where(row == z.signal_scale, power, 0.0)
-        body = jnp.where(left, first, second)
-        base_ref[index] = jnp.concatenate([power, body], axis=0)
+        base_ref[index] = jnp.where(left, first, second)
 
 
 def filtered_product(z, x_ref, w_ref, table_ref, source):
@@ -232,7 +252,7 @@
         source = lax.rem(me + step + 1, z.subjects)
         rows = w_ref.at[step * z.width : (step + 1) * z.width, :]
         total = total + filtered_product(z, x_ref, rows, table_ref, source)
-    value, power = coded(total)
+    value = coded_prediction(total)
     row = iota((8, LANES), 0)
     for member in range(GROUP):
         shared = []
@@ -247,15 +267,8 @@
             tail = pltpu.roll(value[z.rows :, lanes], shift, 0)
             here = (row >= place) & (row < place + z.own_tail)
             tails[which] = jnp.where(here, tail, tails[which])
-        powers = jnp.zeros((z.signal_at - z.scale_at, LANES), f32)
-        place = iota(powers.shape, 0)
-        for tile in range(z.tiles):
-            lanes = slice(tile * LANES, (tile + 1) * LANES)
-            powers = jnp.where(place == tile, power[:, lanes], powers)
         for index in range(member, z.n, GROUP):
-            base = base_ref[index]
-            last = [base[: powers.shape[0]] + powers, base[powers.shape[0] :]]
-            message = jnp.concatenate(shared + tails + last, axis=0)
+            message = jnp.concatenate(shared + tails + [base_ref[index]], axis=0)
             out_ref[index] = message.astype(i32).astype(jnp.int16)
     member = lax.rem(lax.axis_index("tr"), GROUP)
     shape = (z.own, z.rows)
@@ -282,56 +295,50 @@
     def integers(index, start, stop):
         return received_ref[index, start:stop, :].astype(i32)
 
-    def numbers(index, start, stop):
-        return integers(index, start, stop).astype(f32)
-
-    def tails_of(x):
+    def tails_of(index):
+        x = integers(index, z.tail_at, z.signal_at)
         tails = []
         for tile in range(z.tiles):
             which, place = divmod(tile * z.own_tail, 8)
-            tail = x[which * 8 : which * 8 + 8]
-            tails.append(pltpu.roll(tail, (8 - place) % 8, 0))
+            tail = pltpu.roll(x[which * 8 : which * 8 + 8], (8 - place) % 8, 0)
+            tails.append(jnp.where(row < z.own_tail, tail, 0))
         return tails
 
-    def unpack(index, carry):
-        start = index * z.source
+    def unpack(pair, carry):
+        start = pair * z.pair
         start = start if isinstance(start, int) else pl.multiple_of(start, 16)
-        body = integers(index, 0, z.tail_at)
-        tails = tails_of(numbers(index, z.tail_at, z.scale_at))
-        powers = numbers(index, z.scale_at, z.signal_at)
+        bodies = [integers(2 * pair + i, 0, z.tail_at) for i in range(2)]
+        tails = [tails_of(2 * pair + i) for i in range(2)]
         for tile in range(z.tiles):
-            x = body[tile * z.own : (tile + 1) * z.own]
+            rows = slice(tile * z.own, (tile + 1) * z.own)
+            x = [body[rows] for body in bodies] + [tail[tile] for tail in tails]
+            x = jnp.concatenate(x, axis=0)
             upper = lax.shift_right_arithmetic(x, jnp.full_like(x, 8))
-            lower = x - upper * 256
-            tail = tails[tile]
-            high = jnp.floor(tail * (1.0 / 256.0))
-            low = tail - 256.0 * high
-            power = powers[tile : tile + 1]
-            none = jnp.zeros((8, LANES), f32)
-            power = jnp.broadcast_to(power, none.shape)
-            first = jnp.concatenate([upper.astype(f32), high, none], axis=0)
-            second = jnp.concatenate([lower.astype(f32), low, power], axis=0)
+            lower = x & 255
             lanes = slice(tile * LANES, (tile + 1) * LANES)
-            terms_ref[pl.ds(start, z.source), lanes] = first.astype(bf16)
+            terms_ref[pl.ds(start, z.pair), lanes] = upper.astype(f32).astype(bf16)
             lanes = slice(z.voxels + lanes.start, z.voxels + lanes.stop)
-            terms_ref[pl.ds(start, z.source), lanes] = second.astype(bf16)
+            terms_ref[pl.ds(start, z.pair), lanes] = lower.astype(f32).astype(bf16)
         return carry
 
-    def place_block(index, carry):
-        start = index * z.source
+    def place_pair(pair, carry):
+        start = pair * z.pair
         start = start if isinstance(start, int) else pl.multiple_of(start, 16)
-        x = placed_ref[pl.ds(start, z.source), :]
-        scale = jnp.exp2(x[z.own + 8 : z.own + 9] - 15.0)
-        block_ref[index] = jnp.where(left, x[: z.half], x[z.half : z.own]) * scale
-        first = left[:8] & (row < z.own_tail)
-        tail_ref[index] = jnp.where(first, x[z.own : z.own + 8] * scale, 0.0)
+        x = placed_ref[pl.ds(start, z.pair), :]
+        for i in range(2):
+            first = x[i * z.own : i * z.own + z.half]
+            second = x[i * z.own + z.half : (i + 1) * z.own]
+            block = decoded_prediction(jnp.where(left, first, second))
+            block_ref[2 * pair + i] = block
+            at = 2 * z.own + 8 * i
+            tail = decoded_prediction(x[at : at + 8])
+            here = left[:8] & (row < z.own_tail)
+            tail_ref[2 * pair + i] = jnp.where(here, tail, 0.0)
         return carry
 
     def add_position(position, sums):
         added = []
-        at = z.scale_at + z.signal_scale
-        power = numbers(position, at // 8 * 8, z.signal_at)[at % 8 : at % 8 + 1]
-        signal = numbers(position, z.signal_at, z.message) * jnp.exp2(power - 15.0)
+        signal = decoded_signal(integers(position, z.signal_at, z.message))
         before = jnp.maximum(position - 1, 0)
         for condition in range(z.conditions + 1):
             if condition == z.conditions:
@@ -356,36 +363,31 @@
             added.append(total)
         return tuple(added)
 
-    def loop(body, carry):
+    def loop(count, body, carry):
         if more:
-            return lax.fori_loop(0, z.n, body, carry)
-        for index in range(z.n):
+            return lax.fori_loop(0, count, body, carry)
+        for index in range(count):
             carry = body(index, carry)
         return carry
 
-    def scales_of(index):
-        powers = numbers(index, z.scale_at, z.signal_at)
-        return jnp.exp2(powers[: z.tiles] - 15.0)
-
     def energy_of(step, here, ahead, kept):
-        scale, scale_ahead = scales_of(here), scales_of(ahead) * kept
-        body = numbers(here, 0, z.tail_at)
-        tails = tails_of(numbers(ahead, z.tail_at, z.scale_at))
+        body = decoded_prediction(integers(here, 0, z.tail_at).astype(f32))
+        tails = tails_of(ahead)
         total = jnp.zeros((z.own, LANES), f32)
         for tile in range(z.tiles):
             lanes = slice(tile * LANES, (tile + 1) * LANES)
-            block = body[tile * z.own : (tile + 1) * z.own] * scale[tile : tile + 1]
+            block = body[tile * z.own : (tile + 1) * z.own]
             residual = own_signal_ref[step, :, lanes] - block
-            tail = tails[tile] * scale_ahead[tile : tile + 1]
+            tail = decoded_prediction(tails[tile].astype(f32)) * kept
             tail = jnp.where(row < z.own_tail, tail, 0.0)
             residual = jnp.concatenate([residual[:8] - tail, residual[8:]], axis=0)
             total = total + residual * residual
         return jnp.sum(total, axis=1, keepdims=True)
 
-    loop(unpack, 0)
-    chunk = 16 * z.source
-    for start in range(0, z.n * z.source, chunk):
-        stop = min(start + chunk, z.n * z.source)
+    loop(z.n // 2, unpack, 0)
+    chunk = 8 * z.pair
+    for start in range(0, z.n // 2 * z.pair, chunk):
+        stop = min(start + chunk, z.n // 2 * z.pair)
         placed_ref[start:stop, :] = dot(terms_ref[start:stop, :], mine_ref[...])
     lanes = iota((z.own, LANES), 1)
     place = iota(orders.shape, 1)
@@ -407,12 +409,12 @@
             value = energy_of(step, here, ahead, kept) * (1.0 / z.voxels)
             energy = jnp.where(lanes == condition, value, energy)
         energies.append(energy)
-    loop(place_block, 0)
+    loop(z.n // 2, place_pair, 0)
     tail_ref[z.n] = jnp.zeros((8, LANES), f32)
     if more:
         copy.wait()
     zero = jnp.zeros((8, LANES), f32)
-    sums = loop(add_position, (zero,) * (z.conditions + 1))
+    sums = loop(z.n, add_position, (zero,) * (z.conditions + 1))
     stats = zero
     for condition, value in enumerate(sums):
         stat = jnp.sum(value, axis=0, keepdims=True)
@@ -467,7 +469,7 @@
     work = 2 * z.ext * z.width * z.voxels
     shapes = [
         jax.ShapeDtypeStruct((z.bands, z.ext, term_lanes), bf16),
-        jax.ShapeDtypeStruct((z.n, z.message - z.scale_at, LANES), f32),
+        jax.ShapeDtypeStruct((z.n, z.half, LANES), f32),
         jax.ShapeDtypeStruct((2 * z.voxels, LANES), bf16),
         jax.ShapeDtypeStruct((z.ext, z.voxels), f32),
         jax.ShapeDtypeStruct((z.columns - z.width, z.voxels), bf16),
@@ -517,8 +519,8 @@
         in_specs=[VMEM] * 4,
         out_specs=[VMEM] * GROUP,
         scratch_shapes=[
-            pltpu.VMEM((z.n * z.source, 2 * z.voxels), bf16),
-            pltpu.VMEM((z.n * z.source, LANES), f32),
+            pltpu.VMEM((z.n // 2 * z.pair, 2 * z.voxels), bf16),
+            pltpu.VMEM((z.n // 2 * z.pair, LANES), f32),
             pltpu.VMEM((z.n, z.half, LANES), f32),
             pltpu.VMEM((z.n + 1, 8, LANES), f32),
             *more,

time: 28.9 us -> 28.4 us (0.983)
  blocking collectives: 18.2 us -> 17.7 us
    all_to_all x1, blocking collectives: 18.2 us -> 17.7 us  [on_device(): received = lax.all_to_all(outgoing, 'tr', 0, 0, tiled=True)]
  transfers between devices with their start and end apart: 3 -> 3, of which waited for: 2 -> 2; matrix products, arithmetic and copies ran while one was open for 0% -> 0% of each run, Pallas kernels for 7% -> 8%
where the time goes in v8:
time: 28.4 us; the launch traced here: 28.2 us
  blocking collectives  17.7 us (62%)
  Pallas kernels  4.08 us (14%)
  starting transfers between devices  3.19 us (11%)
  waiting for transfers between devices  2.61 us (9%)
  between operations  0.66 us (2%)
    all_to_all x1, blocking collectives, on_device(): received = lax.all_to_all(outgoing, 'tr', 0, 0, tiled=True)  17.7 us
    ppermute x1, starting transfers between devices, on_device(): lax.ppermute(features, 'subj', [((i + step) % z.subjects, i) for i in ran...  3 us
    pallas_call x1, Pallas kernels, on_device(): pl.pallas_call(functools.partial(first_kernel, z), out_shape=shapes, in_s...  2.15 us
    ppermute x1, waiting for transfers between devices, on_device(): lax.ppermute(features, 'subj', [((i + step) % z.subjects, i) for i in ran...  1.53 us
    ppermute x1, waiting for transfers between devices, on_device(): parts = [parts[0], lax.ppermute(parts[1], 'tr', siblings)]  1.08 us
    pallas_call x1, Pallas kernels, on_device(): pl.pallas_call(functools.partial(fourth_kernel, z), out_shape=[jax.ShapeD...  0.79 us
    pallas_call x1, Pallas kernels, on_device(): pl.pallas_call(functools.partial(third_kernel, z), out_shape=[part] * GRO...  0.7 us
  transfers between devices with their start and end apart: 3, of which 2 were waited for; matrix products, arithmetic and copies ran while one was open for 0% of the time, Pallas kernels for 8%

profile of v8, /device:TPU:0, one launch (start us, length us, event | category | flops | bytes accessed | tf_op | source)
XLA Modules:
  0.0 28.2 jit_solution(2454113603478806154)
XLA Ops:
  0.6 3.0 %collective-permute-start.1 = (bf16[64,1024]{1,0:T(8,128)(2,1)}, bf16[64,1024]{1,0:T(8,128)(2,1)S(1)}, u32[]{:S(2)}, u32[]{:S(2)}) collective-permute-start(bf16[64,1024]{1,0:T(8,128)(2,1)} %x_hbm.1), channel_id=1, source_target_pairs={{16,0},{0,16},{17,1},{1,17},{18,2},{2,18},{19,3},{3,19},{20,4},{4,... | collective-permute-start | bytes 393224 | tf_op jit(solution)/shard_map/ppermute | solution.py:460
  3.6 0.0 collective-permute-start
  3.6 2.2 %prepare_and_own_columns.1 = (bf16[4,72,256]{2,1,0:T(8,128)(2,1)S(1)}, f32[16,16,128]{2,1,0:T(8,128)S(1)}, bf16[512,128]{1,0:T(8,128)(2,1)S(1)}, f32[72,256]{1,0...) custom-call(s32[4,4]{1,0:T(4,128)} %offsets_hbm.1, ...), custom_call_target="tpu_custom_call" | custom-call | flops 37748736 | bytes 3145728 | tf_op jit(solution)/shard_map/prepare_and_own_columns/pallas_call | solution.py:490
  5.8 0.0 collective-permute-done.sibling_ref
  5.8 1.5 %collective-permute-done.1.refs_0_ = bf16[64,1024]{1,0:T(8,128)(2,1)S(1)} collective-permute-done((bf16[64,1024]{1,0:T(8,128)(2,1)}, bf16[64,1024]{1,0:T(8,128)(2,1)S(1)}, u32[]{:S(2)}, u32[]{:S(2)}) %collective-permute-start.1) | collective-permute-done | bytes 131104 | tf_op jit(solution)/shard_map/ppermute | solution.py:460
  7.3 0.4 %other_columns.1 = (s16[16,88,128]{2,1,0:T(8,128)(2,1)S(1)}, f32[2,32,256]{2,1,0:T(8,128)S(1)}) custom-call(bf16[4,72,256]{2,1,0:T(8,128)(2,1)S(1)} %get-tuple-element.17.table_ref, bf16[1024,256]{1,0:T(8,128)(2,1)S(1)} %get-tuple-element.18.w_ref, f32[72,256]{1,0:T(8,128)S(1)} %get-tuple-element.19.total_ref, ...), custom_call_target="tpu_custom_call" | custom-call | flops 37748736 | bytes 2097152 | tf_op jit(solution)/shard_map/other_columns/pallas_call | solution.py:500
  7.8 17.7 %all_to_all.5.received_ref = s16[16,88,128]{2,1,0:T(8,128)(2,1)S(1)} all-to-all(s16[16,88,128]{2,1,0:T(8,128)(2,1)S(1)} %get-tuple-element.23), channel_id=1, replica_groups=mesh['subj'=2,'tr'=16] {'tr'}, dimensions={0} | all-to-all | bytes 720896 | tf_op jit(solution)/shard_map/all_to_all | solution.py:512
  25.5 0.7 %residuals.1 = (f32[40,128]{1,0:T(8,128)S(1)}, f32[40,128]{1,0:T(8,128)S(1)}) custom-call(s32[4,16]{1,0:T(4,128)S(1)} %get-tuple-element.15.orders_in_ref, bf16[512,128]{1,0:T(8,128)(2,1)S(1)} %get-tuple-element.16.mine_ref, f32[2,32,256]{2,1,0:T(8,128)S(1)} %get-tuple-element.22.own_signal_ref, s16[16,88,128]{2,1,0:T(8,128)(2,1)S(1)} %all_to_all.5.received_ref), custom_call_target="tpu_custom_call" | custom-call | flops 37748736 | bytes 1048576 | tf_op jit(solution)/shard_map/residuals/pallas_call | solution.py:516
  26.2 0.2 collective-permute-start.2
  26.3 1.1 %collective-permute-done.2.refs_1_ = f32[40,128]{1,0:T(8,128)S(1)} collective-permute-done((f32[40,128]{1,0:T(8,128)S(1)}, f32[40,128]{1,0:T(8,128)S(1)}, u32[]{:S(2)}, u32[]{:S(2)}) %collective-permute-start.2) | collective-permute-done | bytes 20512 | tf_op jit(solution)/shard_map/ppermute | solution.py:532
  27.4 0.8 %scores.1 = (f32[5,1,64]{2,1,0:T(1,128)}, f32[5,1,8]{2,1,0:T(1,128)}) custom-call(f32[40,128]{1,0:T(8,128)S(1)} %get-tuple-element.24.refs_0_, f32[40,128]{1,0:T(8,128)S(1)} %collective-permute-done.2.refs_1_), custom_call_target="tpu_custom_call" | custom-call | flops 1048576 | bytes 65536 | tf_op jit(solution)/shard_map/scores/pallas_call | solution.py:533
Async XLA Ops:
  0.6 6.7 %collective-permute-start.1 = (bf16[64,1024]{1,0:T(8,128)(2,1)}, bf16[64,1024]{1,0:T(8,128)(2,1)S(1)}, u32[]{:S(2)}, u32[]{:S(2)}) collective-permute-start(bf16[64,1024]{1,0:T(8,128)(2,1)} %x_hbm.1), channel_id=1, source_target_pairs={{16,0},{0,16},{17,1},{1,17},{18,2},{2,18},{19,3},{3,19},{20,4},{4,... | collective-permute-start | bytes 393224 | tf_op jit(solution)/shard_map/ppermute | solution.py:460
  3.6 2.2 %collective-permute-start = (bf16[64,256]{1,0:T(8,128)(2,1)}, bf16[64,256]{1,0:T(8,128)(2,1)S(1)}, u32[]{:S(2)}, u32[]{:S(2)}) collective-permute-start(bf16[64,256]{1,0:T(8,128)(2,1)} %bitcast.6), channel_id=1, source_target_pairs={{0,1},{1,0},{2,3},{3,2},{4,5},{5,4},{6,7},{7,6},{8,9},{9,8},{10,11... | collective-permute-start | bytes 98312 | tf_op jit(solution)/shard_map/ppermute | solution.py:467
  26.2 1.3 %collective-permute-start.2 = (f32[40,128]{1,0:T(8,128)S(1)}, f32[40,128]{1,0:T(8,128)S(1)}, u32[]{:S(2)}, u32[]{:S(2)}) collective-permute-start(f32[40,128]{1,0:T(8,128)S(1)} %get-tuple-element.25), channel_id=1, source_target_pairs={{0,1},{1,0},{2,3},{3,2},{4,5},{5,4},{6,7},{7,6},{8,9},{9,8},{10,11... | collective-permute-start | bytes 61448 | tf_op jit(solution)/shard_map/ppermute | solution.py:532

commit v9 on v8

--- a/solution.py
+++ b/solution.py
@@ -72,7 +72,7 @@
 
 
 BITS, LEAST = 7, -126
-STEPS, SMALLEST = 512.0, -50.0
+STEPS, SMALLEST = 668.0, -36.0
 
 
 def coded_signal(x):
@@ -189,7 +189,8 @@
     every = place == lane // LANES * half + lane % half
     group = lax.axis_index("tr") // GROUP
     mine = place == group * half + iota((1, LANES), 1) % half
-    return every.astype(f32).astype(bf16), mine.astype(f32)
+    voxel = jnp.sum(jnp.where(mine, iota(mine.shape, 0) + 1, 0), axis=0, keepdims=True)
+    return every.astype(f32).astype(bf16), voxel - 1
 
 
 def first_kernel(
@@ -230,8 +231,7 @@
     total_ref[...] = filtered_product(z, x_ref, w_ref, table_ref, me)
     copies[4].wait()
     every, mine = owned_columns(z, owners_ref)
-    mine = jnp.concatenate([256.0 * mine, mine], axis=0)
-    mine_ref[...] = mine.astype(bf16)
+    mine_ref[...] = jnp.broadcast_to(mine, (8, LANES))
     copies[5].wait()
     for tile in range(z.tiles):
         lanes = slice(tile * LANES, (tile + 1) * LANES)
@@ -279,7 +279,7 @@
 
 
 def third_kernel(z, orders_in_ref, mine_ref, own_signal_ref, received_ref, *refs):
-    out_refs, (terms_ref, placed_ref, block_ref, tail_ref, *more) = (
+    out_refs, (block_ref, tail_ref, *more) = (
         refs[:GROUP],
         refs[GROUP:],
     )
@@ -304,36 +304,30 @@
             tails.append(jnp.where(row < z.own_tail, tail, 0))
         return tails
 
-    def unpack(pair, carry):
-        start = pair * z.pair
-        start = start if isinstance(start, int) else pl.multiple_of(start, 16)
-        bodies = [integers(2 * pair + i, 0, z.tail_at) for i in range(2)]
-        tails = [tails_of(2 * pair + i) for i in range(2)]
-        for tile in range(z.tiles):
-            rows = slice(tile * z.own, (tile + 1) * z.own)
-            x = [body[rows] for body in bodies] + [tail[tile] for tail in tails]
-            x = jnp.concatenate(x, axis=0)
-            upper = lax.shift_right_arithmetic(x, jnp.full_like(x, 8))
-            lower = x & 255
-            lanes = slice(tile * LANES, (tile + 1) * LANES)
-            terms_ref[pl.ds(start, z.pair), lanes] = upper.astype(f32).astype(bf16)
-            lanes = slice(z.voxels + lanes.start, z.voxels + lanes.stop)
-            terms_ref[pl.ds(start, z.pair), lanes] = lower.astype(f32).astype(bf16)
-        return carry
-
-    def place_pair(pair, carry):
-        start = pair * z.pair
-        start = start if isinstance(start, int) else pl.multiple_of(start, 16)
-        x = placed_ref[pl.ds(start, z.pair), :]
-        for i in range(2):
-            first = x[i * z.own : i * z.own + z.half]
-            second = x[i * z.own + z.half : (i + 1) * z.own]
-            block = decoded_prediction(jnp.where(left, first, second))
-            block_ref[2 * pair + i] = block
-            at = 2 * z.own + 8 * i
-            tail = decoded_prediction(x[at : at + 8])
-            here = left[:8] & (row < z.own_tail)
-            tail_ref[2 * pair + i] = jnp.where(here, tail, 0.0)
+    voxel = mine_ref[...]
+    tile_of = voxel // LANES
+    lane_of = jnp.maximum(voxel, 0) % LANES
+
+    def picked(parts):
+        value = jnp.zeros((8, LANES), i32)
+        for tile, part in enumerate(parts):
+            found = jnp.take_along_axis(part, lane_of, axis=1)
+            value = jnp.where(tile_of == tile, found, value)
+        return value
+
+    def place(index, carry):
+        x = integers(index, 0, z.tail_at)
+        for start in range(0, z.half, 8):
+            halves = []
+            for first in (start, start + z.half):
+                at = [tile * z.own + first for tile in range(z.tiles)]
+                halves.append(picked([x[i : i + 8] for i in at]))
+            value = jnp.where(left[:8], *halves).astype(f32)
+            value = jnp.where(voxel >= 0, decoded_prediction(value), 0.0)
+            block_ref[index, start : start + 8, :] = value
+        tail = decoded_prediction(picked(tails_of(index)).astype(f32))
+        here = left[:8] & (row < z.own_tail) & (voxel >= 0)
+        tail_ref[index] = jnp.where(here, tail, 0.0)
         return carry
 
     def add_position(position, sums):
@@ -384,22 +378,17 @@
             total = total + residual * residual
         return jnp.sum(total, axis=1, keepdims=True)
 
-    loop(z.n // 2, unpack, 0)
-    chunk = 8 * z.pair
-    for start in range(0, z.n // 2 * z.pair, chunk):
-        stop = min(start + chunk, z.n // 2 * z.pair)
-        placed_ref[start:stop, :] = dot(terms_ref[start:stop, :], mine_ref[...])
     lanes = iota((z.own, LANES), 1)
-    place = iota(orders.shape, 1)
+    column = iota(orders.shape, 1)
     energies = []
     for step in range(GROUP):
         energy = jnp.zeros((z.own, LANES), f32)
         position = jnp.bitwise_xor(me, step)
         kept = jnp.where(position == 0, 0.0, 1.0)
         before = jnp.maximum(position - 1, 0)
-        own = jnp.where(place == position, orders, 0)
+        own = jnp.where(column == position, orders, 0)
         own = jnp.sum(own, axis=1, keepdims=True)
-        preceding = jnp.where(place == before, orders, 0)
+        preceding = jnp.where(column == before, orders, 0)
         preceding = jnp.sum(preceding, axis=1, keepdims=True)
         for condition in range(z.conditions):
             if condition == 0:
@@ -409,7 +398,7 @@
             value = energy_of(step, here, ahead, kept) * (1.0 / z.voxels)
             energy = jnp.where(lanes == condition, value, energy)
         energies.append(energy)
-    loop(z.n // 2, place_pair, 0)
+    loop(z.n, place, 0)
     tail_ref[z.n] = jnp.zeros((8, LANES), f32)
     if more:
         copy.wait()
@@ -470,7 +459,7 @@
     shapes = [
         jax.ShapeDtypeStruct((z.bands, z.ext, term_lanes), bf16),
         jax.ShapeDtypeStruct((z.n, z.half, LANES), f32),
-        jax.ShapeDtypeStruct((2 * z.voxels, LANES), bf16),
+        jax.ShapeDtypeStruct((8, LANES), i32),
         jax.ShapeDtypeStruct((z.ext, z.voxels), f32),
         jax.ShapeDtypeStruct((z.columns - z.width, z.voxels), bf16),
         jax.ShapeDtypeStruct(block_orders.shape, i32),
@@ -519,8 +508,6 @@
         in_specs=[VMEM] * 4,
         out_specs=[VMEM] * GROUP,
         scratch_shapes=[
-            pltpu.VMEM((z.n // 2 * z.pair, 2 * z.voxels), bf16),
-            pltpu.VMEM((z.n // 2 * z.pair, LANES), f32),
             pltpu.VMEM((z.n, z.half, LANES), f32),
             pltpu.VMEM((z.n + 1, 8, LANES), f32),
             *more,

time: 28.4 us -> 28.3 us (level)
  no operation moved by 1% of the time
where the time goes in v9:
time: 28.3 us; the launch traced here: 28.2 us
  blocking collectives  17.7 us (63%)
  Pallas kernels  4.02 us (14%)
  starting transfers between devices  3.19 us (11%)
  waiting for transfers between devices  2.63 us (9%)
  between operations  0.66 us (2%)
    all_to_all x1, blocking collectives, on_device(): received = lax.all_to_all(outgoing, 'tr', 0, 0, tiled=True)  17.7 us
    ppermute x1, starting transfers between devices, on_device(): lax.ppermute(features, 'subj', [((i + step) % z.subjects, i) for i in ran...  3 us
    pallas_call x1, Pallas kernels, on_device(): pl.pallas_call(functools.partial(first_kernel, z), out_shape=shapes, in_s...  2.13 us
    ppermute x1, waiting for transfers between devices, on_device(): lax.ppermute(features, 'subj', [((i + step) % z.subjects, i) for i in ran...  1.55 us
    ppermute x1, waiting for transfers between devices, on_device(): parts = [parts[0], lax.ppermute(parts[1], 'tr', siblings)]  1.08 us
    pallas_call x1, Pallas kernels, on_device(): pl.pallas_call(functools.partial(fourth_kernel, z), out_shape=[jax.ShapeD...  0.79 us
    pallas_call x1, Pallas kernels, on_device(): pl.pallas_call(functools.partial(third_kernel, z), out_shape=[part] * GRO...  0.65 us
  transfers between devices with their start and end apart: 3, of which 2 were waited for; matrix products, arithmetic and copies ran while one was open for 0% of the time, Pallas kernels for 8%

profile of v9, /device:TPU:0, one launch (start us, length us, event | category | flops | bytes accessed | tf_op | source)
XLA Modules:
  0.0 28.2 jit_solution(12601332403567165649)
XLA Ops:
  0.6 3.0 %collective-permute-start.1 = (bf16[64,1024]{1,0:T(8,128)(2,1)}, bf16[64,1024]{1,0:T(8,128)(2,1)S(1)}, u32[]{:S(2)}, u32[]{:S(2)}) collective-permute-start(bf16[64,1024]{1,0:T(8,128)(2,1)} %x_hbm.1), channel_id=1, source_target_pairs={{16,0},{0,16},{17,1},{1,17},{18,2},{2,18},{19,3},{3,19},{20,4},{4,... | collective-permute-start | bytes 393224 | tf_op jit(solution)/shard_map/ppermute | solution.py:449
  3.6 0.0 collective-permute-start
  3.6 2.1 %prepare_and_own_columns.1 = (bf16[4,72,256]{2,1,0:T(8,128)(2,1)S(1)}, f32[16,16,128]{2,1,0:T(8,128)S(1)}, s32[8,128]{1,0:T(8,128)S(1)}, f32[72,256]{1,0:T(8,128...) custom-call(s32[4,4]{1,0:T(4,128)} %offsets_hbm.1, f32[4,4]{1,0:T(4,128)} %gains_hbm.1, ...), custom_call_target="tpu_custom_call" | custom-call | flops 37748736 | bytes 3145728 | tf_op jit(solution)/shard_map/prepare_and_own_columns/pallas_call | solution.py:479
  5.8 0.0 collective-permute-done.sibling_ref
  5.8 1.6 %collective-permute-done.1.refs_0_ = bf16[64,1024]{1,0:T(8,128)(2,1)S(1)} collective-permute-done((bf16[64,1024]{1,0:T(8,128)(2,1)}, bf16[64,1024]{1,0:T(8,128)(2,1)S(1)}, u32[]{:S(2)}, u32[]{:S(2)}) %collective-permute-start.1) | collective-permute-done | bytes 131104 | tf_op jit(solution)/shard_map/ppermute | solution.py:449
  7.3 0.4 %other_columns.1 = (s16[16,88,128]{2,1,0:T(8,128)(2,1)S(1)}, f32[2,32,256]{2,1,0:T(8,128)S(1)}) custom-call(bf16[4,72,256]{2,1,0:T(8,128)(2,1)S(1)} %get-tuple-element.17.table_ref, bf16[1024,256]{1,0:T(8,128)(2,1)S(1)} %get-tuple-element.18.w_ref, f32[72,256]{1,0:T(8,128)S(1)} %get-tuple-element.19.total_ref, ...), custom_call_target="tpu_custom_call" | custom-call | flops 37748736 | bytes 2097152 | tf_op jit(solution)/shard_map/other_columns/pallas_call | solution.py:489
  7.8 17.7 %all_to_all.5.received_ref = s16[16,88,128]{2,1,0:T(8,128)(2,1)S(1)} all-to-all(s16[16,88,128]{2,1,0:T(8,128)(2,1)S(1)} %get-tuple-element.23), channel_id=1, replica_groups=mesh['subj'=2,'tr'=16] {'tr'}, dimensions={0} | all-to-all | bytes 720896 | tf_op jit(solution)/shard_map/all_to_all | solution.py:501
  25.5 0.7 %residuals.1 = (f32[40,128]{1,0:T(8,128)S(1)}, f32[40,128]{1,0:T(8,128)S(1)}) custom-call(s32[4,16]{1,0:T(4,128)S(1)} %get-tuple-element.15.orders_in_ref, s32[8,128]{1,0:T(8,128)S(1)} %get-tuple-element.16.mine_ref, f32[2,32,256]{2,1,0:T(8,128)S(1)} %get-tuple-element.22.own_signal_ref, s16[16,88,128]{2,1,0:T(8,128)(2,1)S(1)} %all_to_all.5.received_ref), custom_call_target="tpu_custom_call" | custom-call | flops 37748736 | bytes 1048576 | tf_op jit(solution)/shard_map/residuals/pallas_call | solution.py:505
  26.1 0.2 collective-permute-start.2
  26.3 1.1 %collective-permute-done.2.refs_1_ = f32[40,128]{1,0:T(8,128)S(1)} collective-permute-done((f32[40,128]{1,0:T(8,128)S(1)}, f32[40,128]{1,0:T(8,128)S(1)}, u32[]{:S(2)}, u32[]{:S(2)}) %collective-permute-start.2) | collective-permute-done | bytes 20512 | tf_op jit(solution)/shard_map/ppermute | solution.py:519
  27.4 0.8 %scores.1 = (f32[5,1,64]{2,1,0:T(1,128)}, f32[5,1,8]{2,1,0:T(1,128)}) custom-call(f32[40,128]{1,0:T(8,128)S(1)} %get-tuple-element.24.refs_0_, f32[40,128]{1,0:T(8,128)S(1)} %collective-permute-done.2.refs_1_), custom_call_target="tpu_custom_call" | custom-call | flops 1048576 | bytes 65536 | tf_op jit(solution)/shard_map/scores/pallas_call | solution.py:520
Async XLA Ops:
  0.6 6.7 %collective-permute-start.1 = (bf16[64,1024]{1,0:T(8,128)(2,1)}, bf16[64,1024]{1,0:T(8,128)(2,1)S(1)}, u32[]{:S(2)}, u32[]{:S(2)}) collective-permute-start(bf16[64,1024]{1,0:T(8,128)(2,1)} %x_hbm.1), channel_id=1, source_target_pairs={{16,0},{0,16},{17,1},{1,17},{18,2},{2,18},{19,3},{3,19},{20,4},{4,... | collective-permute-start | bytes 393224 | tf_op jit(solution)/shard_map/ppermute | solution.py:449
  3.6 2.1 %collective-permute-start = (bf16[64,256]{1,0:T(8,128)(2,1)}, bf16[64,256]{1,0:T(8,128)(2,1)S(1)}, u32[]{:S(2)}, u32[]{:S(2)}) collective-permute-start(bf16[64,256]{1,0:T(8,128)(2,1)} %bitcast.6), channel_id=1, source_target_pairs={{0,1},{1,0},{2,3},{3,2},{4,5},{5,4},{6,7},{7,6},{8,9},{9,8},{10,11... | collective-permute-start | bytes 98312 | tf_op jit(solution)/shard_map/ppermute | solution.py:456
  26.1 1.3 %collective-permute-start.2 = (f32[40,128]{1,0:T(8,128)S(1)}, f32[40,128]{1,0:T(8,128)S(1)}, u32[]{:S(2)}, u32[]{:S(2)}) collective-permute-start(f32[40,128]{1,0:T(8,128)S(1)} %get-tuple-element.25), channel_id=1, source_target_pairs={{0,1},{1,0},{2,3},{3,2},{4,5},{5,4},{6,7},{7,6},{8,9},{9,8},{10,11... | collective-permute-start | bytes 61448 | tf_op jit(solution)/shard_map/ppermute | solution.py:519

commit v10 on v9

--- a/solution.py
+++ b/solution.py
@@ -49,6 +49,7 @@
     def __init__(self, features, block_orders, offsets, weights, block_owner):
         self.subjects = lax.axis_size("subj")
         self.n = lax.axis_size("tr")
+        self.middle = self.n // 8 * 4 + 1
         self.rows, self.width = features.shape
         self.columns, self.voxels = weights.shape[1:]
         self.bands, self.taps = offsets.shape
@@ -67,12 +68,18 @@
         self.message = self.signal_at + self.half
         self.pair = 2 * (self.own + 8)
         assert GROUP * CAP * VB * 2 == LANES and self.n % GROUP == 0
+        assert self.n & (self.n - 1) == 0 and self.n >= 4
         assert self.half % 8 == 0 and self.conditions < 8 and 8 % self.own_tail == 0
         assert self.tiles * self.own_tail % 8 == 0
 
 
 BITS, LEAST = 7, -126
 STEPS, SMALLEST = 668.0, -36.0
+
+
+def place_of(z, position):
+    position = position ^ z.middle
+    return (position >> 1 & 1) * (z.n // 2) + (position >> 2) * 2 + (position & 1)
 
 
 def coded_signal(x):
@@ -269,7 +276,8 @@
             tails[which] = jnp.where(here, tail, tails[which])
         for index in range(member, z.n, GROUP):
             message = jnp.concatenate(shared + tails + [base_ref[index]], axis=0)
-            out_ref[index] = message.astype(i32).astype(jnp.int16)
+            message = message.astype(i32).astype(jnp.int16)
+            out_ref[place_of(z, index)] = message
     member = lax.rem(lax.axis_index("tr"), GROUP)
     shape = (z.own, z.rows)
     pick = iota(shape, 1) == GROUP * iota(shape, 0) + member
@@ -293,7 +301,7 @@
     left = iota((z.half, LANES), 1) < LANES // 2
 
     def integers(index, start, stop):
-        return received_ref[index, start:stop, :].astype(i32)
+        return received_ref[place_of(z, index), start:stop, :].astype(i32)
 
     def tails_of(index):
         x = integers(index, z.tail_at, z.signal_at)
@@ -498,7 +506,10 @@
         cost_estimate=cost(work, 2 << 20),
         name="other_columns",
     )(table, rest, total, base, signal, sibling_signal, *others)
-    received = lax.all_to_all(outgoing, "tr", 0, 0, tiled=True)
+    order = sorted(range(z.n), key=functools.partial(place_of, z))
+    received = lax.all_to_all(
+        outgoing, "tr", 0, 0, axis_index_groups=[order], tiled=True
+    )
     more = [pltpu.SMEM(block_orders.shape, i32), pltpu.SemaphoreType.DMA]
     more = more if z.n > 16 else []
     part = jax.ShapeDtypeStruct((z.own + 8, LANES), f32)

time: 28.3 us -> 26.5 us (0.936)
  blocking collectives: 17.7 us -> 15.3 us
  starting transfers between devices: 3.19 us -> 3.93 us
    all_to_all x1, blocking collectives: 17.7 us -> 15.3 us  [on_device(): lax.all_to_all(outgoing, 'tr', 0, 0, axis_index_groups=[order], tiled=True)]
    ppermute x1, starting transfers between devices: 0.18 us -> 0.92 us  [on_device(): parts = [parts[0], lax.ppermute(parts[1], 'tr', siblings)]]
where the time goes in v10:
time: 26.5 us; the launch traced here: 26.3 us
  blocking collectives  15.3 us (58%)
  Pallas kernels  4.04 us (15%)
  starting transfers between devices  3.93 us (15%)
  waiting for transfers between devices  2.4 us (9%)
  between operations  0.66 us (2%)
    all_to_all x1, blocking collectives, on_device(): lax.all_to_all(outgoing, 'tr', 0, 0, axis_index_groups=[order], tiled=True)  15.3 us
    ppermute x1, starting transfers between devices, on_device(): lax.ppermute(features, 'subj', [((i + step) % z.subjects, i) for i in ran...  3 us
    pallas_call x1, Pallas kernels, on_device(): pl.pallas_call(functools.partial(first_kernel, z), out_shape=shapes, in_s...  2.13 us
    ppermute x1, waiting for transfers between devices, on_device(): lax.ppermute(features, 'subj', [((i + step) % z.subjects, i) for i in ran...  1.55 us
    ppermute x1, starting transfers between devices, on_device(): parts = [parts[0], lax.ppermute(parts[1], 'tr', siblings)]  0.92 us
    ppermute x1, waiting for transfers between devices, on_device(): parts = [parts[0], lax.ppermute(parts[1], 'tr', siblings)]  0.84 us
    pallas_call x1, Pallas kernels, on_device(): pl.pallas_call(functools.partial(fourth_kernel, z), out_shape=[jax.ShapeD...  0.79 us
    pallas_call x1, Pallas kernels, on_device(): pl.pallas_call(functools.partial(third_kernel, z), out_shape=[part] * GRO...  0.67 us
  transfers between devices with their start and end apart: 3, of which 2 were waited for; matrix products, arithmetic and copies ran while one was open for 0% of the time, Pallas kernels for 8%

profile of v10, /device:TPU:0, one launch (start us, length us, event | category | flops | bytes accessed | tf_op | source)
XLA Modules:
  0.0 26.3 jit_solution(12297711560792110690)
XLA Ops:
  0.6 3.0 %collective-permute-start.1 = (bf16[64,1024]{1,0:T(8,128)(2,1)}, bf16[64,1024]{1,0:T(8,128)(2,1)S(1)}, u32[]{:S(2)}, u32[]{:S(2)}) collective-permute-start(bf16[64,1024]{1,0:T(8,128)(2,1)} %x_hbm.1), channel_id=1, source_target_pairs={{16,0},{0,16},{17,1},{1,17},{18,2},{2,18},{19,3},{3,19},{20,4},{4,... | collective-permute-start | bytes 393224 | tf_op jit(solution)/shard_map/ppermute | solution.py:457
  3.6 0.0 collective-permute-start
  3.6 2.1 %prepare_and_own_columns.1 = (bf16[4,72,256]{2,1,0:T(8,128)(2,1)S(1)}, f32[16,16,128]{2,1,0:T(8,128)S(1)}, s32[8,128]{1,0:T(8,128)S(1)}, f32[72,256]{1,0:T(8,128...) custom-call(s32[4,4]{1,0:T(4,128)} %offsets_hbm.1, f32[4,4]{1,0:T(4,128)} %gains_hbm.1, ...), custom_call_target="tpu_custom_call" | custom-call | flops 37748736 | bytes 3145728 | tf_op jit(solution)/shard_map/prepare_and_own_columns/pallas_call | solution.py:487
  5.8 0.0 collective-permute-done.sibling_ref
  5.8 1.6 %collective-permute-done.1.refs_0_ = bf16[64,1024]{1,0:T(8,128)(2,1)S(1)} collective-permute-done((bf16[64,1024]{1,0:T(8,128)(2,1)}, bf16[64,1024]{1,0:T(8,128)(2,1)S(1)}, u32[]{:S(2)}, u32[]{:S(2)}) %collective-permute-start.1) | collective-permute-done | bytes 131104 | tf_op jit(solution)/shard_map/ppermute | solution.py:457
  7.3 0.4 %other_columns.1 = (s16[16,88,128]{2,1,0:T(8,128)(2,1)S(1)}, f32[2,32,256]{2,1,0:T(8,128)S(1)}) custom-call(bf16[4,72,256]{2,1,0:T(8,128)(2,1)S(1)} %get-tuple-element.17.table_ref, bf16[1024,256]{1,0:T(8,128)(2,1)S(1)} %get-tuple-element.18.w_ref, f32[72,256]{1,0:T(8,128)S(1)} %get-tuple-element.19.total_ref, ...), custom_call_target="tpu_custom_call" | custom-call | flops 37748736 | bytes 2097152 | tf_op jit(solution)/shard_map/other_columns/pallas_call | solution.py:497
  7.8 15.3 %all_to_all.5.received_ref = s16[16,88,128]{2,1,0:T(8,128)(2,1)S(1)} all-to-all(s16[16,88,128]{2,1,0:T(8,128)(2,1)S(1)} %get-tuple-element.23), channel_id=1, replica_groups={{9,8,13,12,1,0,5,4,11,10,15,14,3,2,7,6},{25,24,29,28,17,16,21,20,27,26,..., dimensions={0} | all-to-all | bytes 720896 | tf_op jit(solution)/shard_map/all_to_all | solution.py:510
  23.0 0.7 %residuals.1 = (f32[40,128]{1,0:T(8,128)S(1)}, f32[40,128]{1,0:T(8,128)S(1)}) custom-call(s32[4,16]{1,0:T(4,128)S(1)} %get-tuple-element.15.orders_in_ref, s32[8,128]{1,0:T(8,128)S(1)} %get-tuple-element.16.mine_ref, f32[2,32,256]{2,1,0:T(8,128)S(1)} %get-tuple-element.22.own_signal_ref, s16[16,88,128]{2,1,0:T(8,128)(2,1)S(1)} %all_to_all.5.received_ref), custom_call_target="tpu_custom_call" | custom-call | flops 37748736 | bytes 1048576 | tf_op jit(solution)/shard_map/residuals/pallas_call | solution.py:516
  23.7 0.9 %collective-permute-start.2 = (f32[40,128]{1,0:T(8,128)S(1)}, f32[40,128]{1,0:T(8,128)S(1)}, u32[]{:S(2)}, u32[]{:S(2)}) collective-permute-start(f32[40,128]{1,0:T(8,128)S(1)} %get-tuple-element.25), channel_id=1, source_target_pairs={{0,1},{1,0},{2,3},{3,2},{4,5},{5,4},{6,7},{7,6},{8,9},{9,8},{10,11... | collective-permute-start | bytes 61448 | tf_op jit(solution)/shard_map/ppermute | solution.py:530
  24.6 0.8 %collective-permute-done.2.refs_1_ = f32[40,128]{1,0:T(8,128)S(1)} collective-permute-done((f32[40,128]{1,0:T(8,128)S(1)}, f32[40,128]{1,0:T(8,128)S(1)}, u32[]{:S(2)}, u32[]{:S(2)}) %collective-permute-start.2) | collective-permute-done | bytes 20512 | tf_op jit(solution)/shard_map/ppermute | solution.py:530
  25.5 0.8 %scores.1 = (f32[5,1,64]{2,1,0:T(1,128)}, f32[5,1,8]{2,1,0:T(1,128)}) custom-call(f32[40,128]{1,0:T(8,128)S(1)} %get-tuple-element.24.refs_0_, f32[40,128]{1,0:T(8,128)S(1)} %collective-permute-done.2.refs_1_), custom_call_target="tpu_custom_call" | custom-call | flops 1048576 | bytes 65536 | tf_op jit(solution)/shard_map/scores/pallas_call | solution.py:531
Async XLA Ops:
  0.6 6.7 %collective-permute-start.1 = (bf16[64,1024]{1,0:T(8,128)(2,1)}, bf16[64,1024]{1,0:T(8,128)(2,1)S(1)}, u32[]{:S(2)}, u32[]{:S(2)}) collective-permute-start(bf16[64,1024]{1,0:T(8,128)(2,1)} %x_hbm.1), channel_id=1, source_target_pairs={{16,0},{0,16},{17,1},{1,17},{18,2},{2,18},{19,3},{3,19},{20,4},{4,... | collective-permute-start | bytes 393224 | tf_op jit(solution)/shard_map/ppermute | solution.py:457
  3.6 2.1 %collective-permute-start = (bf16[64,256]{1,0:T(8,128)(2,1)}, bf16[64,256]{1,0:T(8,128)(2,1)S(1)}, u32[]{:S(2)}, u32[]{:S(2)}) collective-permute-start(bf16[64,256]{1,0:T(8,128)(2,1)} %bitcast.6), channel_id=1, source_target_pairs={{0,1},{1,0},{2,3},{3,2},{4,5},{5,4},{6,7},{7,6},{8,9},{9,8},{10,11... | collective-permute-start | bytes 98312 | tf_op jit(solution)/shard_map/ppermute | solution.py:464
  23.7 1.8 %collective-permute-start.2 = (f32[40,128]{1,0:T(8,128)S(1)}, f32[40,128]{1,0:T(8,128)S(1)}, u32[]{:S(2)}, u32[]{:S(2)}) collective-permute-start(f32[40,128]{1,0:T(8,128)S(1)} %get-tuple-element.25), channel_id=1, source_target_pairs={{0,1},{1,0},{2,3},{3,2},{4,5},{5,4},{6,7},{7,6},{8,9},{9,8},{10,11... | collective-permute-start | bytes 61448 | tf_op jit(solution)/shard_map/ppermute | solution.py:530

commit v11 on v10

--- a/solution.py
+++ b/solution.py
@@ -49,7 +49,7 @@
     def __init__(self, features, block_orders, offsets, weights, block_owner):
         self.subjects = lax.axis_size("subj")
         self.n = lax.axis_size("tr")
-        self.middle = self.n // 8 * 4 + 1
+        self.middle = self.n // 8 * 4 + 3
         self.rows, self.width = features.shape
         self.columns, self.voxels = weights.shape[1:]
         self.bands, self.taps = offsets.shape

time: 26.5 us -> 25.3 us (0.955)
  blocking collectives: 15.3 us -> 14.6 us
  starting transfers between devices: 3.93 us -> 3.4 us
    all_to_all x1, blocking collectives: 15.3 us -> 14.6 us  [on_device(): lax.all_to_all(outgoing, 'tr', 0, 0, axis_index_groups=[order], tiled=True)]
    ppermute x1, starting transfers between devices: 0.92 us -> 0.4 us  [on_device(): parts = [parts[0], lax.ppermute(parts[1], 'tr', siblings)]]
  transfers between devices with their start and end apart: 3 -> 3, of which waited for: 2 -> 2; matrix products, arithmetic and copies ran while one was open for 0% -> 0% of each run, Pallas kernels for 8% -> 9%
where the time goes in v11:
time: 25.3 us; the launch traced here: 25.1 us
  blocking collectives  14.6 us (58%)
  Pallas kernels  4.04 us (16%)
  starting transfers between devices  3.4 us (13%)
  waiting for transfers between devices  2.41 us (10%)
  between operations  0.66 us (3%)
    all_to_all x1, blocking collectives, on_device(): lax.all_to_all(outgoing, 'tr', 0, 0, axis_index_groups=[order], tiled=True)  14.6 us
    ppermute x1, starting transfers between devices, on_device(): lax.ppermute(features, 'subj', [((i + step) % z.subjects, i) for i in ran...  3 us
    pallas_call x1, Pallas kernels, on_device(): pl.pallas_call(functools.partial(first_kernel, z), out_shape=shapes, in_s...  2.13 us
    ppermute x1, waiting for transfers between devices, on_device(): lax.ppermute(features, 'subj', [((i + step) % z.subjects, i) for i in ran...  1.55 us
    ppermute x1, waiting for transfers between devices, on_device(): parts = [parts[0], lax.ppermute(parts[1], 'tr', siblings)]  0.86 us
    pallas_call x1, Pallas kernels, on_device(): pl.pallas_call(functools.partial(fourth_kernel, z), out_shape=[jax.ShapeD...  0.79 us
    pallas_call x1, Pallas kernels, on_device(): pl.pallas_call(functools.partial(third_kernel, z), out_shape=[part] * GRO...  0.67 us
  transfers between devices with their start and end apart: 3, of which 2 were waited for; matrix products, arithmetic and copies ran while one was open for 0% of the time, Pallas kernels for 9%

profile of v11, /device:TPU:0, one launch (start us, length us, event | category | flops | bytes accessed | tf_op | source)
XLA Modules:
  0.0 25.1 jit_solution(11269643778757645365)
XLA Ops:
  0.6 3.0 %collective-permute-start.1 = (bf16[64,1024]{1,0:T(8,128)(2,1)}, bf16[64,1024]{1,0:T(8,128)(2,1)S(1)}, u32[]{:S(2)}, u32[]{:S(2)}) collective-permute-start(bf16[64,1024]{1,0:T(8,128)(2,1)} %x_hbm.1), channel_id=1, source_target_pairs={{16,0},{0,16},{17,1},{1,17},{18,2},{2,18},{19,3},{3,19},{20,4},{4,... | collective-permute-start | bytes 393224 | tf_op jit(solution)/shard_map/ppermute | solution.py:457
  3.6 0.0 collective-permute-start
  3.6 2.1 %prepare_and_own_columns.1 = (bf16[4,72,256]{2,1,0:T(8,128)(2,1)S(1)}, f32[16,16,128]{2,1,0:T(8,128)S(1)}, s32[8,128]{1,0:T(8,128)S(1)}, f32[72,256]{1,0:T(8,128...) custom-call(s32[4,4]{1,0:T(4,128)} %offsets_hbm.1, f32[4,4]{1,0:T(4,128)} %gains_hbm.1, ...), custom_call_target="tpu_custom_call" | custom-call | flops 37748736 | bytes 3145728 | tf_op jit(solution)/shard_map/prepare_and_own_columns/pallas_call | solution.py:487
  5.8 0.0 collective-permute-done.sibling_ref
  5.8 1.6 %collective-permute-done.1.refs_0_ = bf16[64,1024]{1,0:T(8,128)(2,1)S(1)} collective-permute-done((bf16[64,1024]{1,0:T(8,128)(2,1)}, bf16[64,1024]{1,0:T(8,128)(2,1)S(1)}, u32[]{:S(2)}, u32[]{:S(2)}) %collective-permute-start.1) | collective-permute-done | bytes 131104 | tf_op jit(solution)/shard_map/ppermute | solution.py:457
  7.3 0.4 %other_columns.1 = (s16[16,88,128]{2,1,0:T(8,128)(2,1)S(1)}, f32[2,32,256]{2,1,0:T(8,128)S(1)}) custom-call(bf16[4,72,256]{2,1,0:T(8,128)(2,1)S(1)} %get-tuple-element.17.table_ref, bf16[1024,256]{1,0:T(8,128)(2,1)S(1)} %get-tuple-element.18.w_ref, f32[72,256]{1,0:T(8,128)S(1)} %get-tuple-element.19.total_ref, ...), custom_call_target="tpu_custom_call" | custom-call | flops 37748736 | bytes 2097152 | tf_op jit(solution)/shard_map/other_columns/pallas_call | solution.py:497
  7.8 14.6 %all_to_all.5.received_ref = s16[16,88,128]{2,1,0:T(8,128)(2,1)S(1)} all-to-all(s16[16,88,128]{2,1,0:T(8,128)(2,1)S(1)} %get-tuple-element.23), channel_id=1, replica_groups={{11,10,15,14,3,2,7,6,9,8,13,12,1,0,5,4},{27,26,31,30,19,18,23,22,25,24,..., dimensions={0} | all-to-all | bytes 720896 | tf_op jit(solution)/shard_map/all_to_all | solution.py:510
  22.4 0.7 %residuals.1 = (f32[40,128]{1,0:T(8,128)S(1)}, f32[40,128]{1,0:T(8,128)S(1)}) custom-call(s32[4,16]{1,0:T(4,128)S(1)} %get-tuple-element.15.orders_in_ref, s32[8,128]{1,0:T(8,128)S(1)} %get-tuple-element.16.mine_ref, f32[2,32,256]{2,1,0:T(8,128)S(1)} %get-tuple-element.22.own_signal_ref, s16[16,88,128]{2,1,0:T(8,128)(2,1)S(1)} %all_to_all.5.received_ref), custom_call_target="tpu_custom_call" | custom-call | flops 37748736 | bytes 1048576 | tf_op jit(solution)/shard_map/residuals/pallas_call | solution.py:516
  23.1 0.4 %collective-permute-start.2 = (f32[40,128]{1,0:T(8,128)S(1)}, f32[40,128]{1,0:T(8,128)S(1)}, u32[]{:S(2)}, u32[]{:S(2)}) collective-permute-start(f32[40,128]{1,0:T(8,128)S(1)} %get-tuple-element.25), channel_id=1, source_target_pairs={{0,1},{1,0},{2,3},{3,2},{4,5},{5,4},{6,7},{7,6},{8,9},{9,8},{10,11... | collective-permute-start | bytes 61448 | tf_op jit(solution)/shard_map/ppermute | solution.py:530
  23.5 0.9 %collective-permute-done.2.refs_1_ = f32[40,128]{1,0:T(8,128)S(1)} collective-permute-done((f32[40,128]{1,0:T(8,128)S(1)}, f32[40,128]{1,0:T(8,128)S(1)}, u32[]{:S(2)}, u32[]{:S(2)}) %collective-permute-start.2) | collective-permute-done | bytes 20512 | tf_op jit(solution)/shard_map/ppermute | solution.py:530
  24.3 0.8 %scores.1 = (f32[5,1,64]{2,1,0:T(1,128)}, f32[5,1,8]{2,1,0:T(1,128)}) custom-call(f32[40,128]{1,0:T(8,128)S(1)} %get-tuple-element.24.refs_0_, f32[40,128]{1,0:T(8,128)S(1)} %collective-permute-done.2.refs_1_), custom_call_target="tpu_custom_call" | custom-call | flops 1048576 | bytes 65536 | tf_op jit(solution)/shard_map/scores/pallas_call | solution.py:531
Async XLA Ops:
  0.6 6.7 %collective-permute-start.1 = (bf16[64,1024]{1,0:T(8,128)(2,1)}, bf16[64,1024]{1,0:T(8,128)(2,1)S(1)}, u32[]{:S(2)}, u32[]{:S(2)}) collective-permute-start(bf16[64,1024]{1,0:T(8,128)(2,1)} %x_hbm.1), channel_id=1, source_target_pairs={{16,0},{0,16},{17,1},{1,17},{18,2},{2,18},{19,3},{3,19},{20,4},{4,... | collective-permute-start | bytes 393224 | tf_op jit(solution)/shard_map/ppermute | solution.py:457
  3.6 2.1 %collective-permute-start = (bf16[64,256]{1,0:T(8,128)(2,1)}, bf16[64,256]{1,0:T(8,128)(2,1)S(1)}, u32[]{:S(2)}, u32[]{:S(2)}) collective-permute-start(bf16[64,256]{1,0:T(8,128)(2,1)} %bitcast.6), channel_id=1, source_target_pairs={{0,1},{1,0},{2,3},{3,2},{4,5},{5,4},{6,7},{7,6},{8,9},{9,8},{10,11... | collective-permute-start | bytes 98312 | tf_op jit(solution)/shard_map/ppermute | solution.py:464
  23.1 1.3 %collective-permute-start.2 = (f32[40,128]{1,0:T(8,128)S(1)}, f32[40,128]{1,0:T(8,128)S(1)}, u32[]{:S(2)}, u32[]{:S(2)}) collective-permute-start(f32[40,128]{1,0:T(8,128)S(1)} %get-tuple-element.25), channel_id=1, source_target_pairs={{0,1},{1,0},{2,3},{3,2},{4,5},{5,4},{6,7},{7,6},{8,9},{9,8},{10,11... | collective-permute-start | bytes 61448 | tf_op jit(solution)/shard_map/ppermute | solution.py:530

commit v12 on v11

--- a/solution.py
+++ b/solution.py
@@ -68,7 +68,7 @@
         self.message = self.signal_at + self.half
         self.pair = 2 * (self.own + 8)
         assert GROUP * CAP * VB * 2 == LANES and self.n % GROUP == 0
-        assert self.n & (self.n - 1) == 0 and self.n >= 4
+        assert self.n & (self.n - 1) == 0 and self.n >= 8
         assert self.half % 8 == 0 and self.conditions < 8 and 8 % self.own_tail == 0
         assert self.tiles * self.own_tail % 8 == 0
 
@@ -79,7 +79,8 @@
 
 def place_of(z, position):
     position = position ^ z.middle
-    return (position >> 1 & 1) * (z.n // 2) + (position >> 2) * 2 + (position & 1)
+    low = (position >> 2 & 1) + (position & 2) + (position & 1) * 4
+    return (position >> 3) * 8 + low
 
 
 def coded_signal(x):

time: 25.3 us -> 24.8 us (0.980)
  blocking collectives: 14.6 us -> 14.1 us
  starting transfers between devices: 3.4 us -> 3.08 us
  waiting for transfers between devices: 2.41 us -> 2.73 us
    all_to_all x1, blocking collectives: 14.6 us -> 14.1 us  [on_device(): lax.all_to_all(outgoing, 'tr', 0, 0, axis_index_groups=[order], tiled=True)]
    ppermute x1, starting transfers between devices: 0.4 us -> 0.07 us  [on_device(): parts = [parts[0], lax.ppermute(parts[1], 'tr', siblings)]]
    ppermute x1, waiting for transfers between devices: 0.86 us -> 1.18 us  [on_device(): parts = [parts[0], lax.ppermute(parts[1], 'tr', siblings)]]
where the time goes in v12:
time: 24.8 us; the launch traced here: 24.6 us
  blocking collectives  14.1 us (57%)
  Pallas kernels  4.04 us (16%)
  starting transfers between devices  3.08 us (12%)
  waiting for transfers between devices  2.73 us (11%)
  between operations  0.67 us (3%)
    all_to_all x1, blocking collectives, on_device(): lax.all_to_all(outgoing, 'tr', 0, 0, axis_index_groups=[order], tiled=True)  14.1 us
    ppermute x1, starting transfers between devices, on_device(): lax.ppermute(features, 'subj', [((i + step) % z.subjects, i) for i in ran...  3 us
    pallas_call x1, Pallas kernels, on_device(): pl.pallas_call(functools.partial(first_kernel, z), out_shape=shapes, in_s...  2.13 us
    ppermute x1, waiting for transfers between devices, on_device(): lax.ppermute(features, 'subj', [((i + step) % z.subjects, i) for i in ran...  1.55 us
    ppermute x1, waiting for transfers between devices, on_device(): parts = [parts[0], lax.ppermute(parts[1], 'tr', siblings)]  1.18 us
    pallas_call x1, Pallas kernels, on_device(): pl.pallas_call(functools.partial(fourth_kernel, z), out_shape=[jax.ShapeD...  0.79 us
    pallas_call x1, Pallas kernels, on_device(): pl.pallas_call(functools.partial(third_kernel, z), out_shape=[part] * GRO...  0.67 us
  transfers between devices with their start and end apart: 3, of which 2 were waited for; matrix products, arithmetic and copies ran while one was open for 0% of the time, Pallas kernels for 9%

profile of v12, /device:TPU:0, one launch (start us, length us, event | category | flops | bytes accessed | tf_op | source)
XLA Modules:
  0.0 24.6 jit_solution(6944229450690958251)
XLA Ops:
  0.6 3.0 %collective-permute-start.1 = (bf16[64,1024]{1,0:T(8,128)(2,1)}, bf16[64,1024]{1,0:T(8,128)(2,1)S(1)}, u32[]{:S(2)}, u32[]{:S(2)}) collective-permute-start(bf16[64,1024]{1,0:T(8,128)(2,1)} %x_hbm.1), channel_id=1, source_target_pairs={{16,0},{0,16},{17,1},{1,17},{18,2},{2,18},{19,3},{3,19},{20,4},{4,... | collective-permute-start | bytes 393224 | tf_op jit(solution)/shard_map/ppermute | solution.py:458
  3.6 0.0 collective-permute-start
  3.6 2.1 %prepare_and_own_columns.1 = (bf16[4,72,256]{2,1,0:T(8,128)(2,1)S(1)}, f32[16,16,128]{2,1,0:T(8,128)S(1)}, s32[8,128]{1,0:T(8,128)S(1)}, f32[72,256]{1,0:T(8,128...) custom-call(s32[4,4]{1,0:T(4,128)} %offsets_hbm.1, f32[4,4]{1,0:T(4,128)} %gains_hbm.1, ...), custom_call_target="tpu_custom_call" | custom-call | flops 37748736 | bytes 3145728 | tf_op jit(solution)/shard_map/prepare_and_own_columns/pallas_call | solution.py:488
  5.8 0.0 collective-permute-done.sibling_ref
  5.8 1.6 %collective-permute-done.1.refs_0_ = bf16[64,1024]{1,0:T(8,128)(2,1)S(1)} collective-permute-done((bf16[64,1024]{1,0:T(8,128)(2,1)}, bf16[64,1024]{1,0:T(8,128)(2,1)S(1)}, u32[]{:S(2)}, u32[]{:S(2)}) %collective-permute-start.1) | collective-permute-done | bytes 131104 | tf_op jit(solution)/shard_map/ppermute | solution.py:458
  7.3 0.4 %other_columns.1 = (s16[16,88,128]{2,1,0:T(8,128)(2,1)S(1)}, f32[2,32,256]{2,1,0:T(8,128)S(1)}) custom-call(bf16[4,72,256]{2,1,0:T(8,128)(2,1)S(1)} %get-tuple-element.17.table_ref, bf16[1024,256]{1,0:T(8,128)(2,1)S(1)} %get-tuple-element.18.w_ref, f32[72,256]{1,0:T(8,128)S(1)} %get-tuple-element.19.total_ref, ...), custom_call_target="tpu_custom_call" | custom-call | flops 37748736 | bytes 2097152 | tf_op jit(solution)/shard_map/other_columns/pallas_call | solution.py:498
  7.8 14.1 %all_to_all.5.received_ref = s16[16,88,128]{2,1,0:T(8,128)(2,1)S(1)} all-to-all(s16[16,88,128]{2,1,0:T(8,128)(2,1)S(1)} %get-tuple-element.23), channel_id=1, replica_groups={{11,15,9,13,10,14,8,12,3,7,1,5,2,6,0,4},{27,31,25,29,26,30,24,28,19,23,..., dimensions={0} | all-to-all | bytes 720896 | tf_op jit(solution)/shard_map/all_to_all | solution.py:511
  21.8 0.7 %residuals.1 = (f32[40,128]{1,0:T(8,128)S(1)}, f32[40,128]{1,0:T(8,128)S(1)}) custom-call(s32[4,16]{1,0:T(4,128)S(1)} %get-tuple-element.15.orders_in_ref, s32[8,128]{1,0:T(8,128)S(1)} %get-tuple-element.16.mine_ref, f32[2,32,256]{2,1,0:T(8,128)S(1)} %get-tuple-element.22.own_signal_ref, s16[16,88,128]{2,1,0:T(8,128)(2,1)S(1)} %all_to_all.5.received_ref), custom_call_target="tpu_custom_call" | custom-call | flops 37748736 | bytes 1048576 | tf_op jit(solution)/shard_map/residuals/pallas_call | solution.py:517
  22.5 0.1 collective-permute-start.2
  22.6 1.2 %collective-permute-done.2.refs_1_ = f32[40,128]{1,0:T(8,128)S(1)} collective-permute-done((f32[40,128]{1,0:T(8,128)S(1)}, f32[40,128]{1,0:T(8,128)S(1)}, u32[]{:S(2)}, u32[]{:S(2)}) %collective-permute-start.2) | collective-permute-done | bytes 20512 | tf_op jit(solution)/shard_map/ppermute | solution.py:531
  23.8 0.8 %scores.1 = (f32[5,1,64]{2,1,0:T(1,128)}, f32[5,1,8]{2,1,0:T(1,128)}) custom-call(f32[40,128]{1,0:T(8,128)S(1)} %get-tuple-element.24.refs_0_, f32[40,128]{1,0:T(8,128)S(1)} %collective-permute-done.2.refs_1_), custom_call_target="tpu_custom_call" | custom-call | flops 1048576 | bytes 65536 | tf_op jit(solution)/shard_map/scores/pallas_call | solution.py:532
Async XLA Ops:
  0.6 6.7 %collective-permute-start.1 = (bf16[64,1024]{1,0:T(8,128)(2,1)}, bf16[64,1024]{1,0:T(8,128)(2,1)S(1)}, u32[]{:S(2)}, u32[]{:S(2)}) collective-permute-start(bf16[64,1024]{1,0:T(8,128)(2,1)} %x_hbm.1), channel_id=1, source_target_pairs={{16,0},{0,16},{17,1},{1,17},{18,2},{2,18},{19,3},{3,19},{20,4},{4,... | collective-permute-start | bytes 393224 | tf_op jit(solution)/shard_map/ppermute | solution.py:458
  3.6 2.1 %collective-permute-start = (bf16[64,256]{1,0:T(8,128)(2,1)}, bf16[64,256]{1,0:T(8,128)(2,1)S(1)}, u32[]{:S(2)}, u32[]{:S(2)}) collective-permute-start(bf16[64,256]{1,0:T(8,128)(2,1)} %bitcast.6), channel_id=1, source_target_pairs={{0,1},{1,0},{2,3},{3,2},{4,5},{5,4},{6,7},{7,6},{8,9},{9,8},{10,11... | collective-permute-start | bytes 98312 | tf_op jit(solution)/shard_map/ppermute | solution.py:465
  22.5 1.3 %collective-permute-start.2 = (f32[40,128]{1,0:T(8,128)S(1)}, f32[40,128]{1,0:T(8,128)S(1)}, u32[]{:S(2)}, u32[]{:S(2)}) collective-permute-start(f32[40,128]{1,0:T(8,128)S(1)} %get-tuple-element.25), channel_id=1, source_target_pairs={{0,1},{1,0},{2,3},{3,2},{4,5},{5,4},{6,7},{7,6},{8,9},{9,8},{10,11... | collective-permute-start | bytes 61448 | tf_op jit(solution)/shard_map/ppermute | solution.py:531

commit v13 on v12

--- a/solution.py
+++ b/solution.py
@@ -250,10 +250,8 @@
         copy.wait()
 
 
-def second_kernel(
-    z, table_ref, w_ref, total_ref, base_ref, signal_ref, sibling_ref, *refs
-):
-    others, (out_ref, own_signal_ref) = refs[:-2], refs[-2:]
+def second_kernel(z, table_ref, w_ref, total_ref, base_ref, _, *refs):
+    others, out_ref = refs[:-1], refs[-1]
     me = lax.axis_index("subj")
     total = total_ref[...]
     for step, x_ref in enumerate(others):
@@ -279,6 +277,9 @@
             message = jnp.concatenate(shared + tails + [base_ref[index]], axis=0)
             message = message.astype(i32).astype(jnp.int16)
             out_ref[place_of(z, index)] = message
+
+
+def signal_kernel(z, signal_ref, sibling_ref, own_signal_ref):
     member = lax.rem(lax.axis_index("tr"), GROUP)
     shape = (z.own, z.rows)
     pick = iota(shape, 1) == GROUP * iota(shape, 0) + member
@@ -495,18 +496,24 @@
         cost_estimate=cost(work, 3 << 20),
         name="prepare_and_own_columns",
     )(*operands)
-    outgoing, own_signal = pl.pallas_call(
+    own_signal = pl.pallas_call(
+        functools.partial(signal_kernel, z),
+        out_shape=jax.ShapeDtypeStruct((GROUP, z.own, z.voxels), f32),
+        in_specs=[VMEM, VMEM],
+        out_specs=VMEM,
+        compiler_params=params(),
+        cost_estimate=cost(work // 8, 1 << 18),
+        name="signal_rows",
+    )(signal, sibling_signal)
+    outgoing = pl.pallas_call(
         functools.partial(second_kernel, z),
-        out_shape=[
-            jax.ShapeDtypeStruct((z.n, z.message, LANES), jnp.int16),
-            jax.ShapeDtypeStruct((GROUP, z.own, z.voxels), f32),
-        ],
-        in_specs=[VMEM] * (6 + len(others)),
-        out_specs=[VMEM, VMEM],
+        out_shape=jax.ShapeDtypeStruct((z.n, z.message, LANES), jnp.int16),
+        in_specs=[VMEM] * (5 + len(others)),
+        out_specs=VMEM,
         compiler_params=params(),
         cost_estimate=cost(work, 2 << 20),
         name="other_columns",
-    )(table, rest, total, base, signal, sibling_signal, *others)
+    )(table, rest, total, base, own_signal, *others)
     order = sorted(range(z.n), key=functools.partial(place_of, z))
     received = lax.all_to_all(
         outgoing, "tr", 0, 0, axis_index_groups=[order], tiled=True

time: 24.8 us -> 24.8 us (level)
    pallas_call x1 -> x2, Pallas kernels: 0.44 us -> 0.57 us  [the longest x1 0.44 us: on_device(): pl.pallas_call(functools.partial(second_kernel, z), out_shape=jax.ShapeDt...]
where the time goes in v13:
time: 24.8 us; the launch traced here: 24.6 us
  blocking collectives  14.1 us (57%)
  Pallas kernels  4.18 us (17%)
  starting transfers between devices  3.08 us (12%)
  waiting for transfers between devices  2.6 us (10%)
  between operations  0.67 us (3%)
    all_to_all x1, blocking collectives, on_device(): lax.all_to_all(outgoing, 'tr', 0, 0, axis_index_groups=[order], tiled=True)  14.1 us
    ppermute x1, starting transfers between devices, on_device(): lax.ppermute(features, 'subj', [((i + step) % z.subjects, i) for i in ran...  3 us
    pallas_call x1, Pallas kernels, on_device(): pl.pallas_call(functools.partial(first_kernel, z), out_shape=shapes, in_s...  2.14 us
    ppermute x1, waiting for transfers between devices, on_device(): lax.ppermute(features, 'subj', [((i + step) % z.subjects, i) for i in ran...  1.42 us
    ppermute x1, waiting for transfers between devices, on_device(): parts = [parts[0], lax.ppermute(parts[1], 'tr', siblings)]  1.18 us
    pallas_call x1, Pallas kernels, on_device(): pl.pallas_call(functools.partial(fourth_kernel, z), out_shape=[jax.ShapeD...  0.79 us
    pallas_call x1, Pallas kernels, on_device(): pl.pallas_call(functools.partial(third_kernel, z), out_shape=[part] * GRO...  0.67 us
  transfers between devices with their start and end apart: 3, of which 2 were waited for; matrix products, arithmetic and copies ran while one was open for 0% of the time, Pallas kernels for 9%

profile of v13, /device:TPU:0, one launch (start us, length us, event | category | flops | bytes accessed | tf_op | source)
XLA Modules:
  0.0 24.6 jit_solution(5050255420432474346)
XLA Ops:
  0.6 3.0 %collective-permute-start.1 = (bf16[64,1024]{1,0:T(8,128)(2,1)}, bf16[64,1024]{1,0:T(8,128)(2,1)S(1)}, u32[]{:S(2)}, u32[]{:S(2)}) collective-permute-start(bf16[64,1024]{1,0:T(8,128)(2,1)} %x_hbm.1), channel_id=1, source_target_pairs={{16,0},{0,16},{17,1},{1,17},{18,2},{2,18},{19,3},{3,19},{20,4},{4,... | collective-permute-start | bytes 393224 | tf_op jit(solution)/shard_map/ppermute | solution.py:459
  3.6 0.0 collective-permute-start
  3.6 2.1 %prepare_and_own_columns.1 = (bf16[4,72,256]{2,1,0:T(8,128)(2,1)S(1)}, f32[16,16,128]{2,1,0:T(8,128)S(1)}, s32[8,128]{1,0:T(8,128)S(1)}, f32[72,256]{1,0:T(8,128...) custom-call(s32[4,4]{1,0:T(4,128)} %offsets_hbm.1, f32[4,4]{1,0:T(4,128)} %gains_hbm.1, ...), custom_call_target="tpu_custom_call" | custom-call | flops 37748736 | bytes 3145728 | tf_op jit(solution)/shard_map/prepare_and_own_columns/pallas_call | solution.py:489
  5.8 0.0 collective-permute-done.sibling_ref
  5.8 0.1 signal_rows.1._.own_signal_ref
  5.9 1.4 %collective-permute-done.1.refs_0_ = bf16[64,1024]{1,0:T(8,128)(2,1)S(1)} collective-permute-done((bf16[64,1024]{1,0:T(8,128)(2,1)}, bf16[64,1024]{1,0:T(8,128)(2,1)S(1)}, u32[]{:S(2)}, u32[]{:S(2)}) %collective-permute-start.1) | collective-permute-done | bytes 131104 | tf_op jit(solution)/shard_map/ppermute | solution.py:459
  7.3 0.4 %other_columns.1 = s16[16,88,128]{2,1,0:T(8,128)(2,1)S(1)} custom-call(bf16[4,72,256]{2,1,0:T(8,128)(2,1)S(1)} %get-tuple-element.16.table_ref, bf16[1024,256]{1,0:T(8,128)(2,1)S(1)} %get-tuple-element.17.w_ref, f32[72,256]{1,0:T(8,128)S(1)} %get-tuple-element.18.total_ref, f32[16,16,128]{2,1,0:T(8,128)S(1)} %get-tuple-element.19.base_ref, ...), custom_call_target="tpu_custom_call" | custom-call | flops 37748736 | bytes 2097152 | tf_op jit(solution)/shard_map/other_columns/pallas_call | solution.py:508
  7.8 14.1 %all_to_all.5.received_ref = s16[16,88,128]{2,1,0:T(8,128)(2,1)S(1)} all-to-all(s16[16,88,128]{2,1,0:T(8,128)(2,1)S(1)} %other_columns.1), channel_id=1, replica_groups={{11,15,9,13,10,14,8,12,3,7,1,5,2,6,0,4},{27,31,25,29,26,30,24,28,19,23,..., dimensions={0} | all-to-all | bytes 720896 | tf_op jit(solution)/shard_map/all_to_all | solution.py:518
  21.8 0.7 %residuals.1 = (f32[40,128]{1,0:T(8,128)S(1)}, f32[40,128]{1,0:T(8,128)S(1)}) custom-call(s32[4,16]{1,0:T(4,128)S(1)} %get-tuple-element.13.orders_in_ref, s32[8,128]{1,0:T(8,128)S(1)} %get-tuple-element.14.mine_ref, f32[2,32,256]{2,1,0:T(8,128)S(1)} %signal_rows.1._.own_signal_ref, s16[16,88,128]{2,1,0:T(8,128)(2,1)S(1)} %all_to_all.5.received_ref), custom_call_target="tpu_custom_call" | custom-call | flops 37748736 | bytes 1048576 | tf_op jit(solution)/shard_map/residuals/pallas_call | solution.py:524
  22.5 0.1 collective-permute-start.2
  22.6 1.2 %collective-permute-done.2.refs_1_ = f32[40,128]{1,0:T(8,128)S(1)} collective-permute-done((f32[40,128]{1,0:T(8,128)S(1)}, f32[40,128]{1,0:T(8,128)S(1)}, u32[]{:S(2)}, u32[]{:S(2)}) %collective-permute-start.2) | collective-permute-done | bytes 20512 | tf_op jit(solution)/shard_map/ppermute | solution.py:538
  23.8 0.8 %scores.1 = (f32[5,1,64]{2,1,0:T(1,128)}, f32[5,1,8]{2,1,0:T(1,128)}) custom-call(f32[40,128]{1,0:T(8,128)S(1)} %get-tuple-element.20.refs_0_, f32[40,128]{1,0:T(8,128)S(1)} %collective-permute-done.2.refs_1_), custom_call_target="tpu_custom_call" | custom-call | flops 1048576 | bytes 65536 | tf_op jit(solution)/shard_map/scores/pallas_call | solution.py:539
Async XLA Ops:
  0.6 6.7 %collective-permute-start.1 = (bf16[64,1024]{1,0:T(8,128)(2,1)}, bf16[64,1024]{1,0:T(8,128)(2,1)S(1)}, u32[]{:S(2)}, u32[]{:S(2)}) collective-permute-start(bf16[64,1024]{1,0:T(8,128)(2,1)} %x_hbm.1), channel_id=1, source_target_pairs={{16,0},{0,16},{17,1},{1,17},{18,2},{2,18},{19,3},{3,19},{20,4},{4,... | collective-permute-start | bytes 393224 | tf_op jit(solution)/shard_map/ppermute | solution.py:459
  3.6 2.2 %collective-permute-start = (bf16[64,256]{1,0:T(8,128)(2,1)}, bf16[64,256]{1,0:T(8,128)(2,1)S(1)}, u32[]{:S(2)}, u32[]{:S(2)}) collective-permute-start(bf16[64,256]{1,0:T(8,128)(2,1)} %bitcast.6), channel_id=1, source_target_pairs={{0,1},{1,0},{2,3},{3,2},{4,5},{5,4},{6,7},{7,6},{8,9},{9,8},{10,11... | collective-permute-start | bytes 98312 | tf_op jit(solution)/shard_map/ppermute | solution.py:466
  22.5 1.3 %collective-permute-start.2 = (f32[40,128]{1,0:T(8,128)S(1)}, f32[40,128]{1,0:T(8,128)S(1)}, u32[]{:S(2)}, u32[]{:S(2)}) collective-permute-start(f32[40,128]{1,0:T(8,128)S(1)} %get-tuple-element.21), channel_id=1, source_target_pairs={{0,1},{1,0},{2,3},{3,2},{4,5},{5,4},{6,7},{7,6},{8,9},{9,8},{10,11... | collective-permute-start | bytes 61448 | tf_op jit(solution)/shard_map/ppermute | solution.py:538

commit v14 on v12

--- a/solution.py
+++ b/solution.py
@@ -429,13 +429,9 @@
     sums = sums + pltpu.roll(sums, LANES // 2, 1)
     signal = sums[z.conditions : z.conditions + 1]
     fit = jnp.log((sums + EPSILON) / (signal + EPSILON))
-    terms = [t.astype(f32) for t in thirds(fit)]
-    square = (LANES, LANES)
-    place = iota(square, 0) // VB - member * CAP
-    mean = (place == iota(square, 1)) & (place >= 0) & (place < CAP)
-    mean = mean & (iota(square, 0) < LANES // 2)
-    mean = jnp.where(mean, 1.0 / VB, 0.0).astype(bf16)
-    score = dot(jnp.concatenate(terms, axis=0).astype(bf16), mean)
+    slot = iota((8, LANES), 1) % CAP + member * CAP
+    score = sum(jnp.take_along_axis(fit, slot * VB + i, axis=1) for i in range(VB))
+    score = score * (1.0 / VB)
     turned = jnp.transpose(jnp.concatenate([p[: z.own, :] for p in parts], axis=0))
     column = iota((z.rows, LANES), 0)
     owner = jnp.bitwise_xor(column // z.own, member)
@@ -444,7 +440,6 @@
     terms = [t.astype(f32) for t in thirds(turned[:8, : z.rows])]
     energy = dot(jnp.concatenate(terms, axis=0).astype(bf16), order)
     energy = energy[:8] + energy[8:16] + energy[16:]
-    score = score[:8] + score[8:16] + score[16:]
     for index in range(z.conditions):
         energy_ref[index] = energy[index : index + 1, : z.rows]
         scores_ref[index] = score[index : index + 1, :CAP]

time: 24.8 us -> 24.8 us (level)
  no operation moved by 1% of the time
where the time goes in v14:
time: 24.8 us; the launch traced here: 24.6 us
  blocking collectives  14.1 us (57%)
  Pallas kernels  4.02 us (16%)
  starting transfers between devices  3.08 us (12%)
  waiting for transfers between devices  2.73 us (11%)
  between operations  0.67 us (3%)
    all_to_all x1, blocking collectives, on_device(): lax.all_to_all(outgoing, 'tr', 0, 0, axis_index_groups=[order], tiled=True)  14.1 us
    ppermute x1, starting transfers between devices, on_device(): lax.ppermute(features, 'subj', [((i + step) % z.subjects, i) for i in ran...  3 us
    pallas_call x1, Pallas kernels, on_device(): pl.pallas_call(functools.partial(first_kernel, z), out_shape=shapes, in_s...  2.13 us
    ppermute x1, waiting for transfers between devices, on_device(): lax.ppermute(features, 'subj', [((i + step) % z.subjects, i) for i in ran...  1.55 us
    ppermute x1, waiting for transfers between devices, on_device(): parts = [parts[0], lax.ppermute(parts[1], 'tr', siblings)]  1.18 us
    pallas_call x1, Pallas kernels, on_device(): pl.pallas_call(functools.partial(fourth_kernel, z), out_shape=[jax.ShapeD...  0.77 us
    pallas_call x1, Pallas kernels, on_device(): pl.pallas_call(functools.partial(third_kernel, z), out_shape=[part] * GRO...  0.67 us
  transfers between devices with their start and end apart: 3, of which 2 were waited for; matrix products, arithmetic and copies ran while one was open for 0% of the time, Pallas kernels for 9%

profile of v14, /device:TPU:0, one launch (start us, length us, event | category | flops | bytes accessed | tf_op | source)
XLA Modules:
  0.0 24.6 jit_solution(842088313012420018)
XLA Ops:
  0.6 3.0 %collective-permute-start.1 = (bf16[64,1024]{1,0:T(8,128)(2,1)}, bf16[64,1024]{1,0:T(8,128)(2,1)S(1)}, u32[]{:S(2)}, u32[]{:S(2)}) collective-permute-start(bf16[64,1024]{1,0:T(8,128)(2,1)} %x_hbm.1), channel_id=1, source_target_pairs={{16,0},{0,16},{17,1},{1,17},{18,2},{2,18},{19,3},{3,19},{20,4},{4,... | collective-permute-start | bytes 393224 | tf_op jit(solution)/shard_map/ppermute | solution.py:453
  3.6 0.0 collective-permute-start
  3.6 2.1 %prepare_and_own_columns.1 = (bf16[4,72,256]{2,1,0:T(8,128)(2,1)S(1)}, f32[16,16,128]{2,1,0:T(8,128)S(1)}, s32[8,128]{1,0:T(8,128)S(1)}, f32[72,256]{1,0:T(8,128...) custom-call(s32[4,4]{1,0:T(4,128)} %offsets_hbm.1, f32[4,4]{1,0:T(4,128)} %gains_hbm.1, ...), custom_call_target="tpu_custom_call" | custom-call | flops 37748736 | bytes 3145728 | tf_op jit(solution)/shard_map/prepare_and_own_columns/pallas_call | solution.py:483
  5.8 0.0 collective-permute-done.sibling_ref
  5.8 1.6 %collective-permute-done.1.refs_0_ = bf16[64,1024]{1,0:T(8,128)(2,1)S(1)} collective-permute-done((bf16[64,1024]{1,0:T(8,128)(2,1)}, bf16[64,1024]{1,0:T(8,128)(2,1)S(1)}, u32[]{:S(2)}, u32[]{:S(2)}) %collective-permute-start.1) | collective-permute-done | bytes 131104 | tf_op jit(solution)/shard_map/ppermute | solution.py:453
  7.3 0.4 %other_columns.1 = (s16[16,88,128]{2,1,0:T(8,128)(2,1)S(1)}, f32[2,32,256]{2,1,0:T(8,128)S(1)}) custom-call(bf16[4,72,256]{2,1,0:T(8,128)(2,1)S(1)} %get-tuple-element.17.table_ref, bf16[1024,256]{1,0:T(8,128)(2,1)S(1)} %get-tuple-element.18.w_ref, f32[72,256]{1,0:T(8,128)S(1)} %get-tuple-element.19.total_ref, ...), custom_call_target="tpu_custom_call" | custom-call | flops 37748736 | bytes 2097152 | tf_op jit(solution)/shard_map/other_columns/pallas_call | solution.py:493
  7.8 14.1 %all_to_all.5.received_ref = s16[16,88,128]{2,1,0:T(8,128)(2,1)S(1)} all-to-all(s16[16,88,128]{2,1,0:T(8,128)(2,1)S(1)} %get-tuple-element.23), channel_id=1, replica_groups={{11,15,9,13,10,14,8,12,3,7,1,5,2,6,0,4},{27,31,25,29,26,30,24,28,19,23,..., dimensions={0} | all-to-all | bytes 720896 | tf_op jit(solution)/shard_map/all_to_all | solution.py:506
  21.8 0.7 %residuals.1 = (f32[40,128]{1,0:T(8,128)S(1)}, f32[40,128]{1,0:T(8,128)S(1)}) custom-call(s32[4,16]{1,0:T(4,128)S(1)} %get-tuple-element.15.orders_in_ref, s32[8,128]{1,0:T(8,128)S(1)} %get-tuple-element.16.mine_ref, f32[2,32,256]{2,1,0:T(8,128)S(1)} %get-tuple-element.22.own_signal_ref, s16[16,88,128]{2,1,0:T(8,128)(2,1)S(1)} %all_to_all.5.received_ref), custom_call_target="tpu_custom_call" | custom-call | flops 37748736 | bytes 1048576 | tf_op jit(solution)/shard_map/residuals/pallas_call | solution.py:512
  22.5 0.1 collective-permute-start.2
  22.6 1.2 %collective-permute-done.2.refs_1_ = f32[40,128]{1,0:T(8,128)S(1)} collective-permute-done((f32[40,128]{1,0:T(8,128)S(1)}, f32[40,128]{1,0:T(8,128)S(1)}, u32[]{:S(2)}, u32[]{:S(2)}) %collective-permute-start.2) | collective-permute-done | bytes 20512 | tf_op jit(solution)/shard_map/ppermute | solution.py:526
  23.8 0.8 %scores.1 = (f32[5,1,64]{2,1,0:T(1,128)}, f32[5,1,8]{2,1,0:T(1,128)}) custom-call(f32[40,128]{1,0:T(8,128)S(1)} %get-tuple-element.24.refs_0_, f32[40,128]{1,0:T(8,128)S(1)} %collective-permute-done.2.refs_1_), custom_call_target="tpu_custom_call" | custom-call | flops 1048576 | bytes 65536 | tf_op jit(solution)/shard_map/scores/pallas_call | solution.py:527
Async XLA Ops:
  0.6 6.7 %collective-permute-start.1 = (bf16[64,1024]{1,0:T(8,128)(2,1)}, bf16[64,1024]{1,0:T(8,128)(2,1)S(1)}, u32[]{:S(2)}, u32[]{:S(2)}) collective-permute-start(bf16[64,1024]{1,0:T(8,128)(2,1)} %x_hbm.1), channel_id=1, source_target_pairs={{16,0},{0,16},{17,1},{1,17},{18,2},{2,18},{19,3},{3,19},{20,4},{4,... | collective-permute-start | bytes 393224 | tf_op jit(solution)/shard_map/ppermute | solution.py:453
  3.6 2.1 %collective-permute-start = (bf16[64,256]{1,0:T(8,128)(2,1)}, bf16[64,256]{1,0:T(8,128)(2,1)S(1)}, u32[]{:S(2)}, u32[]{:S(2)}) collective-permute-start(bf16[64,256]{1,0:T(8,128)(2,1)} %bitcast.6), channel_id=1, source_target_pairs={{0,1},{1,0},{2,3},{3,2},{4,5},{5,4},{6,7},{7,6},{8,9},{9,8},{10,11... | collective-permute-start | bytes 98312 | tf_op jit(solution)/shard_map/ppermute | solution.py:460
  22.5 1.3 %collective-permute-start.2 = (f32[40,128]{1,0:T(8,128)S(1)}, f32[40,128]{1,0:T(8,128)S(1)}, u32[]{:S(2)}, u32[]{:S(2)}) collective-permute-start(f32[40,128]{1,0:T(8,128)S(1)} %get-tuple-element.25), channel_id=1, source_target_pairs={{0,1},{1,0},{2,3},{3,2},{4,5},{5,4},{6,7},{7,6},{8,9},{9,8},{10,11... | collective-permute-start | bytes 61448 | tf_op jit(solution)/shard_map/ppermute | solution.py:526
